TPU v7x, 32 devices: a whole 2x2x4 slice. The times are simulated.
32 devices in a mesh: layer: 4 (over y, core), trace: 8 (over z, x).
Axes of the slice: x: 2, y: 2, z: 4, core: 2. Of those that a mesh axis runs over, the one named last changes fastest.
Arguments:
- source_up: bfloat16 [4, 8192, 256], P('layer', 'trace'), may hold values from -6 to 6
- source_down: bfloat16 [4, 8192, 256], P('layer', 'trace'), may hold values from -6 to 6
- diag_up: bfloat16 [4, 2, 8192, 1024], P('layer', None, 'trace'), may hold values from -0.125 to 0.125
- diag_down: bfloat16 [4, 2, 8192, 1024], P('layer', None, 'trace'), may hold values from -0.125 to 0.125
- projection: bfloat16 [4, 2, 32, 8192], P('layer', None, None, 'trace'), may hold values from -0.1875 to 0.1875
- expansion: bfloat16 [4, 2, 32, 8192], P('layer', None, None, 'trace'), may hold values from -1 to 1
- coupling: bfloat16 [4, 2, 2, 256, 256], P('layer', None, None, 'trace'), may hold values from -0.25 to 0.25
Outputs:
- trace_up: bfloat16 [4, 8192, 256], P('layer', 'trace')
- trace_down: bfloat16 [4, 8192, 256], P('layer', 'trace')
All inputs are finite; a program needn't handle non-finite values.
Results may differ from a plain program's by a relative error of at most 0.013.
Values may be sent and summed in bfloat16 or wider, within the bound.
No kernel may reach another device: no remote copies, remote signals or barrier semaphores. Data moves between devices by JAX's collectives and lax.ppermute only.
A program may use at most 64 MiB of HBM per device.

v0:
```python
import jax
import jax.numpy as jnp
from jax import lax
from jax.sharding import PartitionSpec as P

ITERS = 3


def for_sending(shard):

    def short(part):
        return part.astype(jnp.bfloat16) if part.dtype == jnp.float32 else part

    return jax.tree.map(short, shard)


def shifted(value, axis, steps):
    count = lax.axis_size(axis)
    initial, last = (max(0, -steps), min(count, count - steps))
    return lax.ppermute(value, axis, [(source, source + steps) for source in range(initial, last)])


def rotate(field):
    half = field.shape[-1] // 2
    return jnp.concatenate([-field[..., half:], field[..., :half]], axis=-1)


def shards(source_up, source_down, diag_up, diag_down, projection, expansion, coupling):
    upward = source_up[0]
    downward = source_down[0]
    blocks = (diag_up[0], diag_down[0])
    for step in range(ITERS):
        fields = (upward, downward)
        coeffs = tuple(
            (
                jnp.dot(
                    projection[0, which], fields[which], preferred_element_type=jnp.float32
                ).astype(jnp.bfloat16)
                for which in range(2)
            )
        )
        gathered = jax.tree.map(
            lambda part, own: part.astype(own.dtype),
            lax.all_gather(for_sending(coeffs), "trace", axis=0, tiled=True),
            coeffs,
        )
        coupled = tuple(
            (
                (
                    jnp.dot(
                        coupling[0, which, 0], gathered[which], preferred_element_type=jnp.float32
                    )
                    + jnp.dot(
                        coupling[0, which, 1],
                        rotate(gathered[which]),
                        preferred_element_type=jnp.float32,
                    )
                ).astype(jnp.bfloat16)
                for which in range(2)
            )
        )
        results = []
        for which in range(2):
            block = blocks[which]
            result = jnp.dot(block[0], fields[which], preferred_element_type=jnp.float32)
            result = result + jnp.dot(
                block[1], rotate(fields[which]), preferred_element_type=jnp.float32
            )
            result = result + lax.dot_general(
                expansion[0, which],
                coupled[which],
                (((0,), (0,)), ((), ())),
                preferred_element_type=jnp.float32,
            )
            results.append(result.astype(jnp.bfloat16))
        arrived_up = shifted(results[0], "layer", 1)
        arrived_down = shifted(results[1], "layer", -1)
        upward = (source_up[0].astype(jnp.float32) + arrived_up.astype(jnp.float32)).astype(
            jnp.bfloat16
        )
        downward = (source_down[0].astype(jnp.float32) + arrived_down.astype(jnp.float32)).astype(
            jnp.bfloat16
        )
    return (upward[None], downward[None])


def solution(mesh):
    return jax.shard_map(
        shards,
        mesh=mesh,
        in_specs=(
            P("layer", "trace", None),
            P("layer", "trace", None),
            P("layer", None, "trace", None),
            P("layer", None, "trace", None),
            P("layer", None, None, "trace"),
            P("layer", None, None, "trace"),
            P("layer", None, None, "trace", None),
        ),
        out_specs=(P("layer", "trace", None), P("layer", "trace", None)),
        check_vma=False,
    )
```

profile of v0, /device:TPU:1, one launch (start us, length us, event | category | flops | bytes accessed | tf_op | source)
XLA Modules:
  0.0 253.0 jit_solution(6183681967207409304)
XLA Ops:
  0.7 1.1 slice_negate_fusion.2
  1.8 2.5 %fusion.10 = f32[1024,256]{1,0:T(8,128)S(1)} fusion(bf16[1,2,1024,1024]{3,2,1,0:T(8,128)(2,1)} %param.10, bf16[1,1024,256]{2,1,0:T(8,128)(2,1)} %param.8), kind=kOutput, calls=%fused_computation.10 | convolution fusion | flops 536870912 | bytes 3670016 | tf_op jit(solution)/shard_map/dot_general | solution.py:65
  4.6 25.6 %all_gather.21 = bf16[256,256]{1,0:T(8,128)(2,1)S(1)} all-gather(bf16[32,256]{1,0:T(8,128)(2,1)S(1)} %convolution_convert_fusion.4), channel_id=1, replica_groups=mesh['layer'=4,'trace'=8] {'trace'}, dimensions={0}, use_global_device_ids=true | all-gather | bytes 147456 | tf_op jit(solution)/shard_map/all_gather | solution.py:44
  30.2 0.2 fusion.210
  30.5 0.7 fusion.44
  31.2 1.3 fusion.87
  32.5 8.7 %collective-permute-start.3 = (bf16[1024,256]{1,0:T(8,128)(2,1)}, bf16[1024,256]{1,0:T(8,128)(2,1)S(1)}, u32[]{:S(2)}, u32[]{:S(2)}) collective-permute-start(bf16[1024,256]{1,0:T(8,128)(2,1)} %fusion.87), channel_id=1, source_target_pairs={{8,0},{16,8},{24,16},{9,1},{17,9},{25,17},{10,2},{18,10},{26,18},{... | collective-permute-start | bytes 1572872 | tf_op jit(solution)/shard_map/ppermute | solution.py:20
  41.2 0.2 convolution_convert_fusion.5
  41.5 2.5 fusion.22
  43.9 24.4 %all_gather.18 = bf16[256,256]{1,0:T(8,128)(2,1)S(1)} all-gather(bf16[32,256]{1,0:T(8,128)(2,1)S(1)} %convolution_convert_fusion.5), channel_id=1, replica_groups=mesh['layer'=4,'trace'=8] {'trace'}, dimensions={0}, use_global_device_ids=true | all-gather | bytes 147456 | tf_op jit(solution)/shard_map/all_gather | solution.py:44
  68.3 0.7 fusion.47
  69.1 0.2 fusion.222
  69.3 1.3 fusion.86
  70.6 9.5 %collective-permute-start = (bf16[1024,256]{1,0:T(8,128)(2,1)}, bf16[1024,256]{1,0:T(8,128)(2,1)S(1)}, u32[]{:S(2)}, u32[]{:S(2)}) collective-permute-start(bf16[1024,256]{1,0:T(8,128)(2,1)} %fusion.86), channel_id=1, source_target_pairs={{0,8},{8,16},{16,24},{1,9},{9,17},{17,25},{2,10},{10,18},{18,26},{... | collective-permute-start | bytes 1572872 | tf_op jit(solution)/shard_map/ppermute | solution.py:20
  80.4 24.4 %all_gather.22 = bf16[256,256]{1,0:T(8,128)(2,1)S(1)} all-gather(bf16[32,256]{1,0:T(8,128)(2,1)S(1)} %fusion.112), channel_id=1, replica_groups=mesh['layer'=4,'trace'=8] {'trace'}, dimensions={0}, use_global_device_ids=true | all-gather | bytes 147456 | tf_op jit(solution)/shard_map/all_gather | solution.py:44
  104.8 0.6 slice_negate_fusion.7
  105.4 0.9 fusion.208
  106.7 24.4 %all_gather.19 = bf16[256,256]{1,0:T(8,128)(2,1)S(1)} all-gather(bf16[32,256]{1,0:T(8,128)(2,1)S(1)} %fusion.110), channel_id=1, replica_groups=mesh['layer'=4,'trace'=8] {'trace'}, dimensions={0}, use_global_device_ids=true | all-gather | bytes 147456 | tf_op jit(solution)/shard_map/all_gather | solution.py:44
  131.2 0.7 slice_negate_fusion.10
  131.8 0.9 fusion.220
  132.7 0.9 slice_negate_fusion.4
  133.6 1.7 fusion.2
  135.2 1.5 fusion.107
  136.7 3.5 %fusion.97 = bf16[1024,256]{1,0:T(8,128)(2,1)} fusion(f32[256,1024]{0,1:T(8,128)S(1)} %fusion.107, f32[256,1024]{0,1:T(8,128)} %fusion.2, bf16[1024,256]{1,0:T(8,128)(2,1)S(1)} %fusion.117, bf16[1,2,1024,1024]{3,2,1,0:T(8,128)(2,1)} %param.10), kind=kOutput, calls=%fused_computation.67 | convolution fusion | flops 537657344 | bytes 5242880 | tf_op jit(solution)/shard_map/dot_general | solution.py:65
  140.3 11.9 %collective-permute-start.4 = (bf16[1024,256]{1,0:T(8,128)(2,1)}, bf16[1024,256]{1,0:T(8,128)(2,1)}, u32[]{:S(2)}, u32[]{:S(2)}) collective-permute-start(bf16[1024,256]{1,0:T(8,128)(2,1)} %fusion.97), channel_id=1, source_target_pairs={{8,0},{16,8},{24,16},{9,1},{17,9},{25,17},{10,2},{18,10},{26,18},{... | collective-permute-start | bytes 1572872 | tf_op jit(solution)/shard_map/ppermute | solution.py:20
  152.2 1.7 fusion.14
  153.9 0.5 fusion.109
  154.4 2.6 %fusion.91 = bf16[1024,256]{1,0:T(8,128)(2,1)S(1)} fusion(f32[256,1024]{0,1:T(8,128)S(1)} %fusion.109, f32[256,1024]{0,1:T(8,128)} %fusion.14, bf16[1024,256]{1,0:T(8,128)(2,1)S(1)} %fusion.114, bf16[1,2,1024,1024]{3,2,1,0:T(8,128)(2,1)} %param.9), kind=kOutput, calls=%fused_computation.65 | convolution fusion | flops 537657344 | bytes 5242880 | tf_op jit(solution)/shard_map/dot_general | solution.py:65
  157.0 4.5 %collective-permute-start.1 = (bf16[1024,256]{1,0:T(8,128)(2,1)S(1)}, bf16[1024,256]{1,0:T(8,128)(2,1)S(1)}, u32[]{:S(2)}, u32[]{:S(2)}) collective-permute-start(bf16[1024,256]{1,0:T(8,128)(2,1)S(1)} %fusion.91), channel_id=1, source_target_pairs={{0,8},{8,16},{16,24},{1,9},{9,17},{17,25},{2,10},{10,18},{18,26},{... | collective-permute-start | bytes 1572872 | tf_op jit(solution)/shard_map/ppermute | solution.py:20
  161.7 1.2 fusion.118
  163.1 24.4 %all_gather.23 = bf16[256,256]{1,0:T(8,128)(2,1)S(1)} all-gather(bf16[32,256]{1,0:T(8,128)(2,1)S(1)} %fusion.113), channel_id=1, replica_groups=mesh['layer'=4,'trace'=8] {'trace'}, dimensions={0}, use_global_device_ids=true | all-gather | bytes 147456 | tf_op jit(solution)/shard_map/all_gather | solution.py:44
  187.5 0.6 slice_negate_fusion.6
  188.1 0.9 fusion.206
  189.2 0.9 slice_negate_fusion.3
  190.3 24.4 %all_gather.20 = bf16[256,256]{1,0:T(8,128)(2,1)S(1)} all-gather(bf16[32,256]{1,0:T(8,128)(2,1)S(1)} %fusion.111), channel_id=1, replica_groups=mesh['layer'=4,'trace'=8] {'trace'}, dimensions={0}, use_global_device_ids=true | all-gather | bytes 147456 | tf_op jit(solution)/shard_map/all_gather | solution.py:44
  214.6 0.7 slice_negate_fusion.9
  215.3 0.9 fusion.218
  216.2 1.7 fusion.4
  217.9 1.4 fusion.106
  219.3 3.5 %fusion.94 = bf16[1024,256]{1,0:T(8,128)(2,1)} fusion(f32[256,1024]{0,1:T(8,128)S(1)} %fusion.106, f32[256,1024]{0,1:T(8,128)} %fusion.4, bf16[1024,256]{1,0:T(8,128)(2,1)S(1)} %fusion.118, bf16[1,2,1024,1024]{3,2,1,0:T(8,128)(2,1)} %param.10), kind=kOutput, calls=%fused_computation.66 | convolution fusion | flops 537657344 | bytes 5242880 | tf_op jit(solution)/shard_map/dot_general | solution.py:65
  222.8 12.4 %collective-permute-start.5 = (bf16[1024,256]{1,0:T(8,128)(2,1)}, bf16[1024,256]{1,0:T(8,128)(2,1)S(1)}, u32[]{:S(2)}, u32[]{:S(2)}) collective-permute-start(bf16[1024,256]{1,0:T(8,128)(2,1)} %fusion.94), channel_id=1, source_target_pairs={{8,0},{16,8},{24,16},{9,1},{17,9},{25,17},{10,2},{18,10},{26,18},{... | collective-permute-start | bytes 1572872 | tf_op jit(solution)/shard_map/ppermute | solution.py:20
  235.2 1.7 fusion.16
  236.9 1.4 fusion.108
  238.3 2.6 %fusion.88 = bf16[1024,256]{1,0:T(8,128)(2,1)S(1)} fusion(f32[256,1024]{0,1:T(8,128)S(1)} %fusion.108, f32[256,1024]{0,1:T(8,128)} %fusion.16, bf16[1024,256]{1,0:T(8,128)(2,1)S(1)} %fusion.115, bf16[1,2,1024,1024]{3,2,1,0:T(8,128)(2,1)} %param.9), kind=kOutput, calls=%fused_computation.64 | convolution fusion | flops 537657344 | bytes 5242880 | tf_op jit(solution)/shard_map/dot_general | solution.py:65
  240.8 5.1 %collective-permute-start.2 = (bf16[1024,256]{1,0:T(8,128)(2,1)S(1)}, bf16[1024,256]{1,0:T(8,128)(2,1)S(1)}, u32[]{:S(2)}, u32[]{:S(2)}) collective-permute-start(bf16[1024,256]{1,0:T(8,128)(2,1)S(1)} %fusion.88), channel_id=1, source_target_pairs={{0,8},{8,16},{16,24},{1,9},{9,17},{17,25},{2,10},{10,18},{18,26},{... | collective-permute-start | bytes 1572872 | tf_op jit(solution)/shard_map/ppermute | solution.py:20
  245.9 0.9 fusion.120
  246.9 5.2 %collective-permute-done.2 = bf16[1024,256]{1,0:T(8,128)(2,1)S(1)} collective-permute-done((bf16[1024,256]{1,0:T(8,128)(2,1)S(1)}, bf16[1024,256]{1,0:T(8,128)(2,1)S(1)}, u32[]{:S(2)}, u32[]{:S(2)}) %collective-permute-start.2) | collective-permute-done | bytes 524320 | tf_op jit(solution)/shard_map/ppermute | solution.py:20
  252.0 0.9 fusion.121
  (60 shorter events, 1.8 us)
Async XLA Ops:
  0.6 3.7 %copy-start = (bf16[1,1024,256]{2,1,0:T(8,128)(2,1)S(1)}, bf16[1,1024,256]{2,1,0:T(8,128)(2,1)}, u32[]{:S(2)}) copy-start(bf16[1,1024,256]{2,1,0:T(8,128)(2,1)} %param.8) | copy-start | bytes 1572868
  0.6 3.7 %copy-start.8 = (bf16[1,2,32,1024]{3,2,1,0:T(8,128)(2,1)S(1)}, bf16[1,2,32,1024]{3,2,1,0:T(8,128)(2,1)}, u32[]{:S(2)}) copy-start(bf16[1,2,32,1024]{3,2,1,0:T(8,128)(2,1)} %param.11) | copy-start | bytes 393220
  1.8 28.4 %copy-start.10 = (bf16[1,2,2,32,256]{4,3,2,1,0:T(8,128)(2,1)S(1)}, bf16[1,2,2,32,256]{4,3,2,1,0:T(8,128)(2,1)}, u32[]{:S(2)}) copy-start(bf16[1,2,2,32,256]{4,3,2,1,0:T(8,128)(2,1)} %param.13) | copy-start | bytes 196612
  1.8 28.6 %copy-start.2 = (bf16[1,2,1024,1024]{3,2,1,0:T(8,128)(2,1)S(1)}, bf16[1,2,1024,1024]{3,2,1,0:T(8,128)(2,1)}, u32[]{:S(2)}) copy-start(bf16[1,2,1024,1024]{3,2,1,0:T(8,128)(2,1)} %param.10) | copy-start | bytes 12582916
  4.4 26.8 %copy-start.9 = (bf16[1,2,32,1024]{3,2,1,0:T(8,128)(2,1)S(1)}, bf16[1,2,32,1024]{3,2,1,0:T(8,128)(2,1)}, u32[]{:S(2)}) copy-start(bf16[1,2,32,1024]{3,2,1,0:T(8,128)(2,1)} %param.12) | copy-start | bytes 393220
  4.4 36.8 %copy-start.1 = (bf16[1,1024,256]{2,1,0:T(8,128)(2,1)S(1)}, bf16[1,1024,256]{2,1,0:T(8,128)(2,1)}, u32[]{:S(2)}) copy-start(bf16[1,1024,256]{2,1,0:T(8,128)(2,1)} %param.7) | copy-start | bytes 1572868
  32.5 47.6 %collective-permute-start.3 = (bf16[1024,256]{1,0:T(8,128)(2,1)}, bf16[1024,256]{1,0:T(8,128)(2,1)S(1)}, u32[]{:S(2)}, u32[]{:S(2)}) collective-permute-start(bf16[1024,256]{1,0:T(8,128)(2,1)} %fusion.87), channel_id=1, source_target_pairs={{8,0},{16,8},{24,16},{9,1},{17,9},{25,17},{10,2},{18,10},{26,18},{... | collective-permute-start | bytes 1572872 | tf_op jit(solution)/shard_map/ppermute | solution.py:20
  41.4 26.9 %copy-start.5 = (bf16[1,2,1024,1024]{3,2,1,0:T(8,128)(2,1)S(1)}, bf16[1,2,1024,1024]{3,2,1,0:T(8,128)(2,1)}, u32[]{:S(2)}) copy-start(bf16[1,2,1024,1024]{3,2,1,0:T(8,128)(2,1)} %param.9) | copy-start | bytes 12582916
  70.6 62.9 %copy-start.3 = (bf16[1,2,1024,1024]{3,2,1,0:T(8,128)(2,1)S(1)}, bf16[1,2,1024,1024]{3,2,1,0:T(8,128)(2,1)}, u32[]{:S(2)}) copy-start(bf16[1,2,1024,1024]{3,2,1,0:T(8,128)(2,1)} %param.10) | copy-start | bytes 12582916
  70.6 35.8 %collective-permute-start = (bf16[1024,256]{1,0:T(8,128)(2,1)}, bf16[1024,256]{1,0:T(8,128)(2,1)S(1)}, u32[]{:S(2)}, u32[]{:S(2)}) collective-permute-start(bf16[1024,256]{1,0:T(8,128)(2,1)} %fusion.86), channel_id=1, source_target_pairs={{0,8},{8,16},{16,24},{1,9},{9,17},{17,25},{2,10},{10,18},{18,26},{... | collective-permute-start | bytes 1572872 | tf_op jit(solution)/shard_map/ppermute | solution.py:20
  136.7 15.5 %copy-start.6 = (bf16[1,2,1024,1024]{3,2,1,0:T(8,128)(2,1)S(1)}, bf16[1,2,1024,1024]{3,2,1,0:T(8,128)(2,1)}, u32[]{:S(2)}) copy-start(bf16[1,2,1024,1024]{3,2,1,0:T(8,128)(2,1)} %param.9) | copy-start | bytes 12582916
  136.7 15.5 %copy-start.19 = (bf16[1024,128]{1,0:T(8,128)(2,1)S(1)}, bf16[1024,128]{1,0:T(8,128)(2,1)}, u32[]{:S(2)}) copy-start(bf16[1024,128]{1,0:T(8,128)(2,1)} %get-tuple-element.10) | copy-start | bytes 786436
  136.7 15.5 %copy-start.20 = (bf16[1024,128]{1,0:T(8,128)(2,1)S(1)}, bf16[1024,128]{1,0:T(8,128)(2,1)}, u32[]{:S(2)}) copy-start(bf16[1024,128]{1,0:T(8,128)(2,1)} %get-tuple-element.11) | copy-start | bytes 786436
  140.3 13.7 %copy-start.11 = (f32[256,32]{1,0:T(8,128)S(1)}, f32[256,32]{1,0:T(8,128)}, u32[]{:S(2)}) copy-start(f32[256,32]{1,0:T(8,128)} %fusion.220) | copy-start | bytes 98308
  140.3 13.7 %copy-start.14 = (bf16[256,128]{1,0:T(8,128)(2,1)S(1)}, bf16[256,128]{1,0:T(8,128)(2,1)}, u32[]{:S(2)}) copy-start(bf16[256,128]{1,0:T(8,128)(2,1)} %get-tuple-element.22) | copy-start | bytes 196612
  140.3 13.7 %copy-start.15 = (bf16[256,128]{1,0:T(8,128)(2,1)S(1)}, bf16[256,128]{1,0:T(8,128)(2,1)}, u32[]{:S(2)}) copy-start(bf16[256,128]{1,0:T(8,128)(2,1)} %get-tuple-element.23) | copy-start | bytes 196612
  140.3 21.5 %collective-permute-start.4 = (bf16[1024,256]{1,0:T(8,128)(2,1)}, bf16[1024,256]{1,0:T(8,128)(2,1)}, u32[]{:S(2)}, u32[]{:S(2)}) collective-permute-start(bf16[1024,256]{1,0:T(8,128)(2,1)} %fusion.97), channel_id=1, source_target_pairs={{8,0},{16,8},{24,16},{9,1},{17,9},{25,17},{10,2},{18,10},{26,18},{... | collective-permute-start | bytes 1572872 | tf_op jit(solution)/shard_map/ppermute | solution.py:20
  157.0 59.2 %copy-start.4 = (bf16[1,2,1024,1024]{3,2,1,0:T(8,128)(2,1)S(1)}, bf16[1,2,1024,1024]{3,2,1,0:T(8,128)(2,1)}, u32[]{:S(2)}) copy-start(bf16[1,2,1024,1024]{3,2,1,0:T(8,128)(2,1)} %param.10) | copy-start | bytes 12582916
  157.0 32.0 %collective-permute-start.1 = (bf16[1024,256]{1,0:T(8,128)(2,1)S(1)}, bf16[1024,256]{1,0:T(8,128)(2,1)S(1)}, u32[]{:S(2)}, u32[]{:S(2)}) collective-permute-start(bf16[1024,256]{1,0:T(8,128)(2,1)S(1)} %fusion.91), channel_id=1, source_target_pairs={{0,8},{8,16},{16,24},{1,9},{9,17},{17,25},{2,10},{10,18},{18,26},{... | collective-permute-start | bytes 1572872 | tf_op jit(solution)/shard_map/ppermute | solution.py:20
  215.3 2.6 %copy-start.12 = (f32[256,32]{1,0:T(8,128)S(1)}, f32[256,32]{1,0:T(8,128)}, u32[]{:S(2)}) copy-start(f32[256,32]{1,0:T(8,128)} %fusion.206) | copy-start | bytes 98308
  219.3 15.9 %copy-start.7 = (bf16[1,2,1024,1024]{3,2,1,0:T(8,128)(2,1)S(1)}, bf16[1,2,1024,1024]{3,2,1,0:T(8,128)(2,1)}, u32[]{:S(2)}) copy-start(bf16[1,2,1024,1024]{3,2,1,0:T(8,128)(2,1)} %param.9) | copy-start | bytes 12582916
  219.3 15.9 %copy-start.17 = (bf16[1024,128]{1,0:T(8,128)(2,1)S(1)}, bf16[1024,128]{1,0:T(8,128)(2,1)}, u32[]{:S(2)}) copy-start(bf16[1024,128]{1,0:T(8,128)(2,1)} %get-tuple-element.8) | copy-start | bytes 786436
  219.3 15.9 %copy-start.18 = (bf16[1024,128]{1,0:T(8,128)(2,1)S(1)}, bf16[1024,128]{1,0:T(8,128)(2,1)}, u32[]{:S(2)}) copy-start(bf16[1024,128]{1,0:T(8,128)(2,1)} %get-tuple-element.9) | copy-start | bytes 786436
  222.8 14.1 %copy-start.13 = (f32[256,32]{1,0:T(8,128)S(1)}, f32[256,32]{1,0:T(8,128)}, u32[]{:S(2)}) copy-start(f32[256,32]{1,0:T(8,128)} %fusion.218) | copy-start | bytes 98308
  222.8 14.1 %copy-start.16 = (bf16[256,128]{1,0:T(8,128)(2,1)S(1)}, bf16[256,128]{1,0:T(8,128)(2,1)}, u32[]{:S(2)}) copy-start(bf16[256,128]{1,0:T(8,128)(2,1)} %get-tuple-element.20) | copy-start | bytes 196612
  222.8 23.1 %collective-permute-start.5 = (bf16[1024,256]{1,0:T(8,128)(2,1)}, bf16[1024,256]{1,0:T(8,128)(2,1)S(1)}, u32[]{:S(2)}, u32[]{:S(2)}) collective-permute-start(bf16[1024,256]{1,0:T(8,128)(2,1)} %fusion.94), channel_id=1, source_target_pairs={{8,0},{16,8},{24,16},{9,1},{17,9},{25,17},{10,2},{18,10},{26,18},{... | collective-permute-start | bytes 1572872 | tf_op jit(solution)/shard_map/ppermute | solution.py:20
  240.8 11.2 %collective-permute-start.2 = (bf16[1024,256]{1,0:T(8,128)(2,1)S(1)}, bf16[1024,256]{1,0:T(8,128)(2,1)S(1)}, u32[]{:S(2)}, u32[]{:S(2)}) collective-permute-start(bf16[1024,256]{1,0:T(8,128)(2,1)S(1)} %fusion.88), channel_id=1, source_target_pairs={{0,8},{8,16},{16,24},{1,9},{9,17},{17,25},{2,10},{10,18},{18,26},{... | collective-permute-start | bytes 1572872 | tf_op jit(solution)/shard_map/ppermute | solution.py:20
where the time goes:
time: 253 us
  blocking collectives  147 us (58%)
  starting transfers between devices  52 us (21%)
  matrix products  37.8 us (15%)
  other arithmetic  9.13 us (4%)
  waiting for transfers between devices  5.32 us (2%)
    all_gather x6, blocking collectives, shards(): lax.all_gather(for_sending(coeffs), 'trace', axis=0, tiled=True)  147 us
    ppermute x6, starting transfers between devices, shifted(): lax.ppermute(value, axis, [(source, source + steps) for source in range(i...  52 us
    dot_general x6, matrix products, shards(): jnp.dot(block[0], fields[which], preferred_element_type=jnp.float32)  17.2 us
    dot_general x6, matrix products, shards(): jnp.dot(block[1], rotate(fields[which]), preferred_element_type=jnp.float32)  8.16 us
    dot_general x6, matrix products, shards(): lax.dot_general(expansion[0, which], coupled[which], (((0,), (0,)), ((),...  7.35 us
    neg x12, other arithmetic, rotate(): return jnp.concatenate([-field[..., half:], field[..., :half]], axis=-1)  5.71 us
    ppermute x6, waiting for transfers between devices, shifted(): lax.ppermute(value, axis, [(source, source + steps) for source in range(i...  5.32 us
  transfers between devices with their start and end apart: 6, of which 2 were waited for; matrix products, arithmetic and copies ran while one was open for 8% of the time, Pallas kernels for 0%

commit v1 on v0

v1 whole, which is shorter than its diff:
```python
import jax
import jax.numpy as jnp
from jax import lax
from jax.experimental import pallas as pl
from jax.experimental.pallas import tpu as pltpu
from jax.sharding import PartitionSpec as P

ITERS = 3
BF16 = jnp.bfloat16
F32 = jnp.float32


def rotate(field):
    half = field.shape[-1] // 2
    return jnp.concatenate([-field[..., half:], field[..., :half]], axis=-1)


def dot(a, b):
    return jnp.dot(a, b, preferred_element_type=F32)


def shifted(value, axis, steps):
    count = lax.axis_size(axis)
    initial, last = (max(0, -steps), min(count, count - steps))
    return lax.ppermute(value, axis, [(source, source + steps) for source in range(initial, last)])


def jacobi(source_up, source_down, diag_up, diag_down, projection, expansion, coupling):
    sources = (source_up[0], source_down[0])
    blocks = (diag_up[0], diag_down[0])
    fields = sources
    for step in range(ITERS):
        coeffs = [dot(projection[0, d], fields[d]).astype(BF16) for d in range(2)]
        gathered = lax.all_gather(jnp.stack(coeffs), "trace", axis=1, tiled=True)
        arrived = []
        for d in range(2):
            coupled = dot(coupling[0, d, 0], gathered[d])
            coupled = (coupled + dot(coupling[0, d, 1], rotate(gathered[d]))).astype(BF16)
            result = dot(blocks[d][0], fields[d]) + dot(blocks[d][1], rotate(fields[d]))
            result = result + lax.dot_general(
                expansion[0, d], coupled, (((0,), (0,)), ((), ())), preferred_element_type=F32
            )
            arrived.append(shifted(result.astype(BF16), "layer", 1 - 2 * d))
        fields = tuple(
            (sources[d].astype(F32) + arrived[d].astype(F32)).astype(BF16) for d in range(2)
        )
    return fields[0][None], fields[1][None]


CHUNKS = 4
HBM = pl.BlockSpec(memory_space=pltpu.HBM)
VMEM = pl.BlockSpec(memory_space=pltpu.VMEM)


def call(body, outs, far, near, scratch, sems, flops=0, moved=0):
    kept = [isinstance(out, tuple) for out in outs]
    return pl.pallas_call(
        body,
        out_shape=tuple(pltpu.VMEM(*out) if keep else out for out, keep in zip(outs, kept)),
        in_specs=[HBM] * len(far) + [VMEM] * len(near),
        out_specs=tuple(VMEM if keep else HBM for keep in kept),
        scratch_shapes=[pltpu.VMEM(shape, BF16) for shape in scratch]
        + [pltpu.SemaphoreType.DMA((sems,))],
        cost_estimate=pl.CostEstimate(flops=flops, bytes_accessed=moved, transcendentals=0),
        compiler_params=pltpu.CompilerParams(vmem_limit_bytes=24 * 2**20),
    )(*far, *near)


def roles():
    layer, layers = lax.axis_index("layer"), lax.axis_size("layer")
    outer = jnp.logical_or(layer == 0, layer == layers - 1)
    return outer, jnp.where(layer >= layers // 2, 1, 0)


def start(source, target, sem):
    copy = pltpu.make_async_copy(source, target, sem)
    copy.start()
    return copy


def pick(which, up_ref, down_ref, target, sem):
    @pl.when(which == 0)
    def _():
        start(up_ref, target, sem)

    @pl.when(which != 0)
    def _():
        start(down_ref, target, sem)


def arrive(target, sem):
    pltpu.make_async_copy(target, target, sem).wait()


def chunk(c, size):
    step = size // CHUNKS
    return pl.ds(pl.multiple_of(c * step, step), step)


def each_chunk(size, body):
    def one(c, carry):
        body(c, chunk(c, size))
        return carry

    lax.fori_loop(0, CHUNKS, one, 0)


def load_block(which, up_ref, down_ref, block, sems, base):
    def one(c, rows):
        pick(
            which,
            up_ref.at[0, :, rows, :],
            down_ref.at[0, :, rows, :],
            block.at[:, rows, :],
            sems.at[base + c],
        )

    each_chunk(block.shape[1], one)


def block_rows(block, rows, field, turned):
    return dot(block[0, rows, :], field[...]) + dot(block[1, rows, :], turned[...])


def dot_rows(a, b):
    return lax.dot_general(a, b, (((1,), (1,)), ((), ())), preferred_element_type=F32)


def expand(basis, coupled):
    return lax.dot_general(basis, coupled, (((0,), (0,)), ((), ())), preferred_element_type=F32)


def fold(wide, target, base):
    k, width = wide.shape[0], target.shape[1]
    for p in range(wide.shape[1] // width):
        target[base + p * k : base + (p + 1) * k, :] = wide[:, p * width : (p + 1) * width]


def unfold(source, base, k, points):
    width = source.shape[1]
    rows = [source[base + p * k : base + (p + 1) * k, :] for p in range(points // width)]
    return jnp.concatenate(rows, axis=1)


def first_kernel(
    sup, sdn, proj, expn, coup,
    payload, pack, source1, own, expn1, couple1,
    other, after, source2, coeffs, sems,
):
    outer, first = roles()
    second = 1 - first
    k, points, total = proj.shape[2], proj.shape[3], coup.shape[4]
    owners, width = payload.shape[0], source1.shape[1]
    start(coup.at[0, first], couple1, sems.at[0])
    start(proj.at[0, first], own, sems.at[1])
    pick(first, sup.at[0], sdn.at[0], source1, sems.at[2])
    start(expn.at[0, first], expn1, sems.at[3])

    @pl.when(outer)
    def _():
        arrive(own, sems.at[1])
        arrive(source1, sems.at[2])
        coeffs[...] = dot(own[...], source1[...]).astype(BF16)
        for o in range(owners):
            start(coeffs, payload.at[o, 0, :, pl.ds(0, width)], sems.at[4])
        arrive(couple1, sems.at[0])
        arrive(expn1, sems.at[3])
        arrive(payload.at[:, 0, :, pl.ds(0, width)], sems.at[4])

    @pl.when(jnp.logical_not(outer))
    def _():
        start(proj.at[0, second], other, sems.at[5])
        start(coup.at[0, second], after, sems.at[6])
        pick(second, sup.at[0], sdn.at[0], source2, sems.at[7])
        arrive(couple1, sems.at[0])
        for o in range(owners):
            start(couple1, payload.at[o, :, :, pl.ds(0, total)], sems.at[4])
        arrive(expn1, sems.at[3])
        arrive(other, sems.at[5])
        arrive(after, sems.at[6])
        pack[:k, :points] = other[...]
        for part in range(2):
            pack[k:, part * total : (part + 1) * total] = after[part]
        arrive(source2, sems.at[7])
        beyond = dot(other[...], source2[...]).astype(BF16)
        pack[k:, 2 * total : 2 * total + width] = beyond
        arrive(own, sems.at[1])
        arrive(source1, sems.at[2])
        arrive(payload.at[:, :, :, pl.ds(0, total)], sems.at[4])


def outer_apply_kernel(dup, ddn, source1, *refs):
    hops, (block, turned, sems) = refs[:CHUNKS], refs[CHUNKS:]
    outer, first = roles()

    @pl.when(outer)
    def _():
        load_block(first, dup, ddn, block, sems, 0)
        step = source1.shape[0] // CHUNKS
        turned[...] = rotate(source1[...])
        for c, hop in enumerate(hops):
            rows = pl.ds(c * step, step)
            arrive(block.at[:, rows, :], sems.at[c])
            hop[...] = block_rows(block, rows, source1, turned).astype(BF16)


def inner_prepare_kernel(dup, ddn, *refs):
    arrived, refs = refs[:CHUNKS], refs[CHUNKS:]
    packed, source1, own, expn1, before, sums, mixed, block, field, turned, sems = refs
    outer, first = roles()

    @pl.when(jnp.logical_not(outer))
    def _():
        load_block(first, dup, ddn, block, sems, 0)
        k, points = own.shape

        step = points // CHUNKS
        for c, part in enumerate(arrived):
            rows = slice(c * step, (c + 1) * step)
            value = (source1[rows, :].astype(F32) + part[...].astype(F32)).astype(BF16)
            field[rows, :] = value
            turned[rows, :] = rotate(value)
        other = packed[:k, :points]
        sums[:k, :] = dot(own[...], field[...])
        mixed[:, :k] = dot_rows(other, expn1[...]).astype(BF16)
        mixed[:, k : 2 * k] = dot_rows(own[...], before[...]).astype(BF16)
        parts = [0.0, 0.0]
        for c in range(CHUNKS):
            rows = pl.ds(c * step, step)
            arrive(block.at[:, rows, :], sems.at[c])
            for part in range(2):
                columns = other[:, c * step : (c + 1) * step]
                parts[part] = parts[part] + dot(columns, block[part, rows, :])
        parts = [part.astype(BF16) for part in parts]
        sums[k:, :] = dot(parts[0], field[...]) + dot(parts[1], turned[...])
        for part in range(2):
            place = (2 + part) * k
            mixed[:, place : place + k] = dot_rows(parts[part], before[...]).astype(BF16)


def outer_couple_kernel(gathered, couple1, mixed, out, sems):
    del mixed, sems
    outer, _ = roles()

    @pl.when(outer)
    def _():
        total = couple1.shape[2]
        coeffs = gathered[:, 0, :, : out.shape[1]].reshape(total, out.shape[1])
        out[...] = (dot(couple1[0], coeffs) + dot(couple1[1], rotate(coeffs))).astype(BF16)


def inner_gather_kernel(before, sums, mixed, packed, payload, small, sems):
    outer, _ = roles()

    @pl.when(jnp.logical_not(outer))
    def _():
        k, width = before.shape
        half, place = k // 2, 2 * k * payload.shape[0]
        coeffs = before[...]
        small[:k, :] = (sums[:k, :] + dot(mixed[:, k : 2 * k], coeffs)).astype(BF16)
        added = dot(mixed[:, 2 * k : 3 * k], coeffs)
        added = added + dot(mixed[:, 3 * k : 4 * k], rotate(coeffs))
        added = added + packed[k:, place : place + width].astype(F32)
        small[k : 2 * k, :] = (sums[k:, :] + added).astype(BF16)
        small[2 * k :, :k] = mixed[:half, :k]
        small[2 * k :, k : 2 * k] = mixed[half:, :k]
        for o in range(payload.shape[0]):
            start(small, payload.at[o], sems.at[0])
        arrive(payload, sems.at[0])


def inner_apply_kernel(dup, ddn, payload, *refs):
    del payload
    arrived, refs = refs[:CHUNKS], refs[CHUNKS:]
    before, other, expn1, source1, product, trace, block, turned, sems = refs
    outer, first = roles()

    @pl.when(jnp.logical_not(outer))
    def _():
        load_block(first, dup, ddn, block, sems, 0)
        points = source1.shape[0]
        step = points // CHUNKS
        fold(expn1[...], product, points)
        added = expand(other[...], before[...])
        for c, part in enumerate(arrived):
            rows = slice(c * step, (c + 1) * step)
            value = source1[rows, :].astype(F32) + part[...].astype(F32)
            value = (value + added[rows, :]).astype(BF16)
            trace[rows, :] = value
            turned[rows, :] = rotate(value)

        def one(c, rows):
            arrive(block.at[:, rows, :], sems.at[c])
            product[rows, :] = block_rows(block, rows, trace, turned).astype(BF16)

        each_chunk(points, one)


def inner_couple_kernel(gathered, second, packed, couple1, out, inner, later, sems):
    del sems
    outer, _ = roles()

    @pl.when(jnp.logical_not(outer))
    def _():
        owners, width = second.shape[0], second.shape[2]
        k, total = couple1.shape[1:]
        coeffs = second[:, :k, :].reshape(total, width)
        turned = rotate(coeffs)
        real = gathered[:, 0, :, :total].reshape(total, total)
        imag = gathered[:, 1, :, :total].reshape(total, total)
        inner[...] = (dot(real, coeffs) + dot(imag, turned)).astype(BF16)
        out[:k, :] = (dot(couple1[0], coeffs) + dot(couple1[1], turned)).astype(BF16)
        for o in range(owners):
            rows = slice(o * k, (o + 1) * k)
            own = inner[rows, :]
            added = [dot(second[o, 2 * k :, h * k : (h + 1) * k], own) for h in range(2)]
            added = jnp.concatenate(added, axis=0)
            later[rows, :] = (second[o, k : 2 * k, :].astype(F32) + added).astype(BF16)
        coeffs = later[...]
        result = dot(packed[k:, :total], coeffs)
        result = result + dot(packed[k:, total : 2 * total], rotate(coeffs))
        out[k:, :] = result.astype(BF16)


def settle_kernel(sup, sdn, expn, dup, ddn, coupled, block2, expn2, source2, sems):
    del coupled
    outer, first = roles()
    pick(1 - first, sup.at[0], sdn.at[0], source2, sems.at[CHUNKS + 1])

    @pl.when(jnp.logical_not(outer))
    def _():
        start(expn.at[0, 1 - first], expn2, sems.at[CHUNKS])
        load_block(1 - first, dup, ddn, block2, sems, 0)
        arrive(expn2, sems.at[CHUNKS])
        each_chunk(
            block2.shape[1], lambda c, rows: arrive(block2.at[:, rows, :], sems.at[c])
        )

    arrive(source2, sems.at[CHUNKS + 1])


def inner_second_kernel(
    crossed, coupled, source2, block2, expn2, out, trace, turned, sems
):
    del sems
    outer, _ = roles()

    @pl.when(jnp.logical_not(outer))
    def _():
        k, points = expn2.shape
        step = points // CHUNKS
        added = expand(unfold(crossed, points, k, points), coupled[:k, :])
        for c in range(CHUNKS):
            rows = slice(c * step, (c + 1) * step)
            value = source2[rows, :].astype(F32) + crossed[rows, :].astype(F32)
            value = (value + added[rows, :]).astype(BF16)
            trace[rows, :] = value
            turned[rows, :] = rotate(value)
        out[...] = expand(expn2[...], coupled[k:, :]).astype(BF16)

        def apply(c, rows):
            value = block_rows(block2, rows, trace, turned) + out[rows, :].astype(F32)
            out[rows, :] = value.astype(BF16)

        each_chunk(points, apply)


def last_kernel(arrived, one, two, source1, source2, up, down, sums, sems):
    outer, first = roles()

    def put(which, source, sem):
        @pl.when(which == 0)
        def _():
            start(source, up.at[0], sem)

        @pl.when(which != 0)
        def _():
            start(source, down.at[0], sem)

    @pl.when(outer)
    def _():
        put(first, source1, sems.at[0])

        def add(c, rows):
            value = source2[rows, :].astype(F32) + arrived[rows, :].astype(F32)
            sums[rows, :] = value.astype(BF16)

        each_chunk(sums.shape[0], add)
        put(1 - first, sums, sems.at[1])

    @pl.when(jnp.logical_not(outer))
    def _():
        put(first, one, sems.at[0])
        put(1 - first, two, sems.at[1])

    arrive(sums, sems.at[0])
    arrive(sums, sems.at[1])


def wave(*arrays):
    layers, owners = lax.axis_size("layer"), lax.axis_size("trace")
    source_up, source_down, diag_up, diag_down, projection, expansion, coupling = (
        pltpu.with_memory_space_constraint(array, pltpu.HBM) for array in arrays
    )
    _, points, width = source_up.shape
    k, total = projection.shape[2], coupling.shape[4]
    swap = [(g, g ^ 1) for g in range(layers)]
    across = [(g, layers - 1 - g) for g in range(layers)]
    inside = across[1:-1]
    folded = k * points // width

    def like(*shape):
        return jax.ShapeDtypeStruct(shape, BF16)

    def kept(*shape, of=BF16):
        return shape, of

    field, block, basis, couple = (points, width), (2, points, points), (k, points), (2, k, total)
    small = dict(flops=2 * k * points * width, moved=4 * points * width)
    large = dict(flops=4 * points * points * width, moved=4 * points * points)
    diagonals = (diag_up, diag_down)
    packing = max(points, 2 * total + width)

    payload, pack, source1, own, expn1, couple1 = call(
        first_kernel,
        (
            like(owners, 2, k, max(total, width)),
            *(kept(2 * k, packing), kept(*field), kept(*basis), kept(*basis), kept(*couple)),
        ),
        (source_up, source_down, projection, expansion, coupling),
        (),
        [basis, couple, field, (k, width)],
        8,
        **small,
    )
    gathered = lax.all_to_all(payload, "trace", 0, 0)
    packed = lax.ppermute(pack, "layer", across)
    other = lax.ppermute(expn1, "layer", swap)
    hops = call(
        outer_apply_kernel,
        (kept(points // CHUNKS, width),) * CHUNKS,
        diagonals,
        (source1,),
        [block, field],
        CHUNKS,
        **large,
    )
    arrived = [lax.ppermute(hop, "layer", swap) for hop in hops]
    sums, mixed = call(
        inner_prepare_kernel,
        (kept(2 * k, width, of=F32), kept(k, 4 * k)),
        diagonals,
        (*arrived, packed, source1, own, expn1, other),
        [block, field, field],
        CHUNKS,
        **large,
    )
    (before,) = call(
        outer_couple_kernel, (kept(k, width),), (), (gathered, couple1, mixed), [], 1, **small
    )
    before = lax.ppermute(before, "layer", swap)
    (payload,) = call(
        inner_gather_kernel,
        (like(owners, 2 * k + k // 2, width),),
        (),
        (before, sums, mixed, packed),
        [(2 * k + k // 2, width)],
        1,
        **small,
    )
    second = lax.all_to_all(payload, "trace", 0, 0)
    product, one = call(
        inner_apply_kernel,
        (kept(points + folded, width), kept(*field)),
        (*diagonals, payload),
        (*arrived, before, other, expn1, source1),
        [block, field],
        CHUNKS,
        **large,
    )
    crossed = lax.ppermute(product, "layer", inside)
    (coupled,) = call(
        inner_couple_kernel,
        (kept(2 * k, width),),
        (),
        (gathered, second, packed, couple1),
        [(total, width), (total, width)],
        1,
        **small,
    )
    reached = lax.ppermute(coupled, "layer", across)
    block2, expn2, source2 = call(
        settle_kernel,
        (kept(*block), kept(*basis), kept(*field)),
        (source_up, source_down, expansion, *diagonals),
        (coupled,),
        [],
        CHUNKS + 2,
        **large,
    )
    result, two = call(
        inner_second_kernel,
        (kept(*field), kept(*field)),
        (),
        (crossed, reached, source2, block2, expn2),
        [field],
        1,
        **large,
    )
    arrived = lax.ppermute(result, "layer", swap)
    return call(
        last_kernel,
        (like(1, *field), like(1, *field)),
        (),
        (arrived, one, two, source1, source2),
        [field],
        2,
        **small,
    )


def solution(mesh):
    shards = wave if mesh.shape["layer"] == ITERS + 1 else jacobi
    return jax.shard_map(
        shards,
        mesh=mesh,
        in_specs=(
            P("layer", "trace", None),
            P("layer", "trace", None),
            P("layer", None, "trace", None),
            P("layer", None, "trace", None),
            P("layer", None, None, "trace"),
            P("layer", None, None, "trace"),
            P("layer", None, None, "trace", None),
        ),
        out_specs=(P("layer", "trace", None), P("layer", "trace", None)),
        check_vma=False,
    )
```

time: 253 us -> 48.5 us (0.19)
  blocking collectives: 147 us -> 0 us
  matrix products: 37.8 us -> 0 us
  starting transfers between devices: 52 us -> 22.3 us
  Pallas kernels: 0 us -> 14.6 us
  other arithmetic: 9.13 us -> 0 us
  waiting for transfers between devices: 5.32 us -> 10.4 us
    all_gather x6 -> x0, blocking collectives: 147 us -> none  [shards(): lax.all_gather(for_sending(coeffs), 'trace', axis=0, tiled=True)]
    ppermute x6 -> x10, starting transfers between devices: 52 us -> 10.2 us  [the longest x4 5.07 us: wave(): arrived = [lax.ppermute(hop, 'layer', swap) for hop in hops]]
    dot_general x30 -> x0, matrix products: 37.8 us -> none  [the longest x6 17.2 us: shards(): jnp.dot(block[0], fields[which], preferred_element_type=jnp.float32)]
    pallas_call x0 -> x10, Pallas kernels: none -> 14.6 us  [call(): pl.pallas_call(body, out_shape=tuple((pltpu.VMEM(*out) if keep else out f...]
    all_to_all x0 -> x2, starting transfers between devices: none -> 12.1 us  [the longest x1 6.37 us: wave(): gathered = lax.all_to_all(payload, 'trace', 0, 0)]
    neg x12 -> x0, other arithmetic: 5.71 us -> none  [rotate(): return jnp.concatenate([-field[..., half:], field[..., :half]], axis=-1)]
    all_to_all x0 -> x2, waiting for transfers between devices: none -> 5.06 us  [the longest x1 5.06 us: wave(): second = lax.all_to_all(payload, 'trace', 0, 0)]
    ppermute x6 -> x10, waiting for transfers between devices: 5.32 us -> 5.35 us  [the longest x1 1.9 us: wave(): arrived = lax.ppermute(result, 'layer', swap)]
  transfers between devices with their start and end apart: 6 -> 12, of which waited for: 2 -> 9; matrix products, arithmetic and copies ran while one was open for 8% -> 0% of each run, Pallas kernels for 0% -> 18%
where the time goes in v1:
time: 48.5 us; the launch traced here: 48.1 us
  starting transfers between devices  22.3 us (46%)
  Pallas kernels  14.6 us (30%)
  waiting for transfers between devices  10.4 us (21%)
  between operations  0.75 us (2%)
    pallas_call x10, Pallas kernels, call(): pl.pallas_call(body, out_shape=tuple((pltpu.VMEM(*out) if keep else out f...  14.6 us
    all_to_all x1, starting transfers between devices, wave(): gathered = lax.all_to_all(payload, 'trace', 0, 0)  6.37 us
    all_to_all x1, starting transfers between devices, wave(): second = lax.all_to_all(payload, 'trace', 0, 0)  5.73 us
    ppermute x4, starting transfers between devices, wave(): arrived = [lax.ppermute(hop, 'layer', swap) for hop in hops]  5.07 us
    all_to_all x1, waiting for transfers between devices, wave(): second = lax.all_to_all(payload, 'trace', 0, 0)  5.06 us
    ppermute x1, starting transfers between devices, wave(): crossed = lax.ppermute(product, 'layer', inside)  2.73 us
    ppermute x1, waiting for transfers between devices, wave(): arrived = lax.ppermute(result, 'layer', swap)  1.9 us
    ppermute x1, starting transfers between devices, wave(): other = lax.ppermute(expn1, 'layer', swap)  1.38 us
  transfers between devices with their start and end apart: 12, of which 9 were waited for; matrix products, arithmetic and copies ran while one was open for 0% of the time, Pallas kernels for 18%

profile of v1, /device:TPU:1, one launch (start us, length us, event | category | flops | bytes accessed | tf_op | source)
XLA Modules:
  0.0 48.1 jit_solution(2693072844415909090)
XLA Ops:
  0.6 1.6 %shard_map.86 = (bf16[8,2,32,256]{3,2,1,0:T(8,128)(2,1)}, bf16[64,1024]{1,0:T(8,128)(2,1)S(1)}, bf16[1024,256]{1,0:T(8,128)(2,1)S(1)}, bf16[32,1024]{1,0:T(8,128...) custom-call(bf16[1,1024,256]{2,1,0:T(8,128)(2,1)} %sup.3, bf16[1,1024,256]{2,1,0:T(8,128)(2,1)} %sdn.3, ...), custom_call_target="tpu_custom_call" | custom-call | flops 16777216 | bytes 1048576 | tf_op jit(solution)/shard_map/pallas_call | solution.py:57
  2.2 6.4 %all-to-all-start = ((bf16[8,2,32,256]{3,2,1,0:T(8,128)(2,1)}), bf16[8,2,32,256]{3,2,1,0:T(8,128)(2,1)S(1)}, u32[]{:S(2)}, u32[]{:S(2)}) async-start(bf16[8,2,32,256]{3,2,1,0:T(8,128)(2,1)} %get-tuple-element.21), calls=%async_computation | async-start | bytes 524288 | tf_op jit(solution)/shard_map/all_to_all | solution.py:436
  8.6 1.4 %collective-permute-start.5 = (bf16[32,1024]{1,0:T(8,128)(2,1)S(1)}, bf16[32,1024]{1,0:T(8,128)(2,1)S(1)}, u32[]{:S(2)}, u32[]{:S(2)}) collective-permute-start(bf16[32,1024]{1,0:T(8,128)(2,1)S(1)} %get-tuple-element.30.refs_7_.refs_6_), channel_id=1, source_target_pairs={{0,8},{8,0},{16,24},{24,16},{1,9},{9,1},{17,25},{25,17},{2,10},{10... | collective-permute-start | bytes 196616 | tf_op jit(solution)/shard_map/ppermute | solution.py:438
  10.0 0.8 %collective-permute-start.4 = (bf16[64,1024]{1,0:T(8,128)(2,1)S(1)}, bf16[64,1024]{1,0:T(8,128)(2,1)S(1)}, u32[]{:S(2)}, u32[]{:S(2)}) collective-permute-start(bf16[64,1024]{1,0:T(8,128)(2,1)S(1)} %get-tuple-element.28), channel_id=1, source_target_pairs={{0,24},{8,16},{16,8},{24,0},{1,25},{9,17},{17,9},{25,1},{2,26},{10... | collective-permute-start | bytes 393224 | tf_op jit(solution)/shard_map/ppermute | solution.py:437
  10.8 4.5 %collective-permute-start = (bf16[256,256]{1,0:T(8,128)(2,1)S(1)}, bf16[256,256]{1,0:T(8,128)(2,1)S(1)}, u32[]{:S(2)}, u32[]{:S(2)}) collective-permute-start(bf16[256,256]{1,0:T(8,128)(2,1)S(1)} %get-tuple-element.24), channel_id=1, source_target_pairs={{0,8},{8,0},{16,24},{24,16},{1,9},{9,1},{17,25},{25,17},{2,10},{10... | collective-permute-start | bytes 393224 | tf_op jit(solution)/shard_map/ppermute | solution.py:448
  15.3 0.1 collective-permute-start.1
  15.4 0.4 collective-permute-start.2
  15.8 0.0 collective-permute-done.5.refs_8_.refs_5_
  15.8 0.1 collective-permute-start.3
  15.9 0.0 collective-permute-done.4.refs_4_.packed
  15.9 0.4 collective-permute-done.refs_0_
  16.3 0.4 collective-permute-done.1.refs_1_
  16.6 0.2 collective-permute-done.2.refs_2_
  16.8 0.3 collective-permute-done.3.refs_3_
  17.2 2.8 %shard_map.88 = (f32[64,256]{1,0:T(8,128)S(1)}, bf16[32,128]{1,0:T(8,128)(2,1)S(1)}) custom-call(bf16[1,2,1024,1024]{3,2,1,0:T(8,128)(2,1)} %dup.7, bf16[1,2,1024,1024]{3,2,1,0:T(8,128)(2,1)} %ddn.7, bf16[256,256]{1,0:T(8,128)(2,1)S(1)} %collective-permute-done.refs_0_, bf16[256,256]{1,0:T(8,128)(2,1)S(1)} %collective-permute-done.1.refs_1_, ...), custom_call_target="tpu_custom_call" | custom-call | flops 1073741824 | bytes 4194304 | tf_op jit(solution)/shard_map/pallas_call | solution.py:57
  20.0 0.0 all-to-all-done.gathered
  20.0 0.1 collective-permute-start.6
  20.1 1.2 %collective-permute-done.6.before.refs_4_ = bf16[32,256]{1,0:T(8,128)(2,1)S(1)} collective-permute-done((bf16[32,256]{1,0:T(8,128)(2,1)S(1)}, bf16[32,256]{1,0:T(8,128)(2,1)S(1)}, u32[]{:S(2)}, u32[]{:S(2)}) %collective-permute-start.6) | collective-permute-done | bytes 16416 | tf_op jit(solution)/shard_map/ppermute | solution.py:461
  21.3 0.9 %shard_map.90.payload = bf16[8,80,256]{2,1,0:T(8,128)(2,1)} custom-call(bf16[32,256]{1,0:T(8,128)(2,1)S(1)} %collective-permute-done.6.before.refs_4_, f32[64,256]{1,0:T(8,128)S(1)} %get-tuple-element.32.sums, bf16[32,128]{1,0:T(8,128)(2,1)S(1)} %get-tuple-element.31.mixed, bf16[64,1024]{1,0:T(8,128)(2,1)S(1)} %collective-permute-done.4.refs_4_.packed), custom_call_target="tpu_custom_call" | custom-call | flops 16777216 | bytes 1048576 | tf_op jit(solution)/shard_map/pallas_call | solution.py:57
  22.2 5.7 %all-to-all-start.1 = ((bf16[8,80,256]{2,1,0:T(8,128)(2,1)}), bf16[8,80,256]{2,1,0:T(8,128)(2,1)S(1)}, u32[]{:S(2)}, u32[]{:S(2)}) async-start(bf16[8,80,256]{2,1,0:T(8,128)(2,1)} %shard_map.90.payload), calls=%async_computation.1 | async-start | bytes 655360 | tf_op jit(solution)/shard_map/all_to_all | solution.py:471
  27.9 3.0 %shard_map.91 = (bf16[1152,256]{1,0:T(8,128)(2,1)S(1)}, bf16[1024,256]{1,0:T(8,128)(2,1)S(1)}) custom-call(bf16[1,2,1024,1024]{3,2,1,0:T(8,128)(2,1)} %dup.7, bf16[1,2,1024,1024]{3,2,1,0:T(8,128)(2,1)} %ddn.7, bf16[8,80,256]{2,1,0:T(8,128)(2,1)} %shard_map.90.payload, bf16[256,256]{1,0:T(8,128)(2,1)S(1)} %collective-permute-done.refs_0_, ...), custom_call_target="tpu_custom_call" | custom-call | flops 1073741824 | bytes 4194304 | tf_op jit(solution)/shard_map/pallas_call | solution.py:57
  30.9 2.7 %collective-permute-start.7 = (bf16[1152,256]{1,0:T(8,128)(2,1)S(1)}, bf16[1152,256]{1,0:T(8,128)(2,1)S(1)}, u32[]{:S(2)}, u32[]{:S(2)}) collective-permute-start(bf16[1152,256]{1,0:T(8,128)(2,1)S(1)} %get-tuple-element.33), channel_id=1, source_target_pairs={{8,16},{16,8},{9,17},{17,9},{10,18},{18,10},{11,19},{19,11},{12,20... | collective-permute-start | bytes 1769480 | tf_op jit(solution)/shard_map/ppermute | solution.py:481
  33.7 5.1 %all-to-all-done.1.second = bf16[8,80,256]{2,1,0:T(8,128)(2,1)S(1)} async-done(((bf16[8,80,256]{2,1,0:T(8,128)(2,1)}), bf16[8,80,256]{2,1,0:T(8,128)(2,1)S(1)}, u32[]{:S(2)}, u32[]{:S(2)}) %all-to-all-start.1) | async-done | bytes 327712 | tf_op jit(solution)/shard_map/all_to_all | solution.py:471
  38.7 0.6 %shard_map.92.coupled = bf16[64,256]{1,0:T(8,128)(2,1)S(1)} custom-call(bf16[8,2,32,256]{3,2,1,0:T(8,128)(2,1)S(1)} %all-to-all-done.gathered, bf16[8,80,256]{2,1,0:T(8,128)(2,1)S(1)} %all-to-all-done.1.second, bf16[64,1024]{1,0:T(8,128)(2,1)S(1)} %collective-permute-done.4.refs_4_.packed, bf16[2,32,256]{2,1,0:T(8,128)(2,1)S(1)} %get-tuple-element.22.couple1), custom_call_target="tpu_custom_call" | custom-call | flops 16777216 | bytes 1048576 | tf_op jit(solution)/shard_map/pallas_call | solution.py:57
  39.3 0.1 collective-permute-start.8
  39.4 2.4 %shard_map.93 = (bf16[2,1024,1024]{2,1,0:T(8,128)(2,1)S(1)}, bf16[32,1024]{1,0:T(8,128)(2,1)S(1)}, bf16[1024,256]{1,0:T(8,128)(2,1)S(1)}) custom-call(bf16[1,1024,256]{2,1,0:T(8,128)(2,1)} %sup.3, bf16[1,1024,256]{2,1,0:T(8,128)(2,1)} %sdn.3, bf16[1,2,32,1024]{3,2,1,0:T(8,128)(2,1)} %expn.3, bf16[1,2,1024,1024]{3,2,1,0:T(8,128)(2,1)} %dup.7, ...), custom_call_target="tpu_custom_call" | custom-call | flops 1073741824 | bytes 4194304 | tf_op jit(solution)/shard_map/pallas_call | solution.py:57
  41.8 0.7 %collective-permute-done.7.crossed = bf16[1152,256]{1,0:T(8,128)(2,1)S(1)} collective-permute-done((bf16[1152,256]{1,0:T(8,128)(2,1)S(1)}, bf16[1152,256]{1,0:T(8,128)(2,1)S(1)}, u32[]{:S(2)}, u32[]{:S(2)}) %collective-permute-start.7) | collective-permute-done | bytes 589856 | tf_op jit(solution)/shard_map/ppermute | solution.py:481
  42.6 0.3 collective-permute-done.8.coupled
  42.8 2.2 %shard_map.94 = (bf16[1024,256]{1,0:T(8,128)(2,1)S(1)}, bf16[1024,256]{1,0:T(8,128)(2,1)S(1)}) custom-call(bf16[1152,256]{1,0:T(8,128)(2,1)S(1)} %collective-permute-done.7.crossed, bf16[64,256]{1,0:T(8,128)(2,1)S(1)} %collective-permute-done.8.coupled, bf16[1024,256]{1,0:T(8,128)(2,1)S(1)} %get-tuple-element.34.source2, ...), custom_call_target="tpu_custom_call" | custom-call | flops 1073741824 | bytes 4194304 | tf_op jit(solution)/shard_map/pallas_call | solution.py:57
  45.1 0.1 collective-permute-start.9
  45.2 1.9 %collective-permute-done.9.arrived = bf16[1024,256]{1,0:T(8,128)(2,1)S(1)} collective-permute-done((bf16[1024,256]{1,0:T(8,128)(2,1)S(1)}, bf16[1024,256]{1,0:T(8,128)(2,1)S(1)}, u32[]{:S(2)}, u32[]{:S(2)}) %collective-permute-start.9) | collective-permute-done | bytes 524320 | tf_op jit(solution)/shard_map/ppermute | solution.py:510
  47.1 1.0 %shard_map.95 = (bf16[1,1024,256]{2,1,0:T(8,128)(2,1)}, bf16[1,1024,256]{2,1,0:T(8,128)(2,1)}) custom-call(bf16[1024,256]{1,0:T(8,128)(2,1)S(1)} %collective-permute-done.9.arrived, bf16[1024,256]{1,0:T(8,128)(2,1)S(1)} %get-tuple-element.38.one, bf16[1024,256]{1,0:T(8,128)(2,1)S(1)} %get-tuple-element.39.two, ...), custom_call_target="tpu_custom_call" | custom-call | flops 16777216 | bytes 1048576 | tf_op jit(solution)/shard_map/pallas_call | solution.py:57
  (2 shorter events, 0.1 us)
Async XLA Ops:
  2.2 17.7 %all-to-all-start = ((bf16[8,2,32,256]{3,2,1,0:T(8,128)(2,1)}), bf16[8,2,32,256]{3,2,1,0:T(8,128)(2,1)S(1)}, u32[]{:S(2)}, u32[]{:S(2)}) async-start(bf16[8,2,32,256]{3,2,1,0:T(8,128)(2,1)} %get-tuple-element.21), calls=%async_computation | async-start | bytes 524288 | tf_op jit(solution)/shard_map/all_to_all | solution.py:436
  8.6 7.2 %collective-permute-start.5 = (bf16[32,1024]{1,0:T(8,128)(2,1)S(1)}, bf16[32,1024]{1,0:T(8,128)(2,1)S(1)}, u32[]{:S(2)}, u32[]{:S(2)}) collective-permute-start(bf16[32,1024]{1,0:T(8,128)(2,1)S(1)} %get-tuple-element.30.refs_7_.refs_6_), channel_id=1, source_target_pairs={{0,8},{8,0},{16,24},{24,16},{1,9},{9,1},{17,25},{25,17},{2,10},{10... | collective-permute-start | bytes 196616 | tf_op jit(solution)/shard_map/ppermute | solution.py:438
  10.0 5.9 %collective-permute-start.4 = (bf16[64,1024]{1,0:T(8,128)(2,1)S(1)}, bf16[64,1024]{1,0:T(8,128)(2,1)S(1)}, u32[]{:S(2)}, u32[]{:S(2)}) collective-permute-start(bf16[64,1024]{1,0:T(8,128)(2,1)S(1)} %get-tuple-element.28), channel_id=1, source_target_pairs={{0,24},{8,16},{16,8},{24,0},{1,25},{9,17},{17,9},{25,1},{2,26},{10... | collective-permute-start | bytes 393224 | tf_op jit(solution)/shard_map/ppermute | solution.py:437
  10.8 5.5 %collective-permute-start = (bf16[256,256]{1,0:T(8,128)(2,1)S(1)}, bf16[256,256]{1,0:T(8,128)(2,1)S(1)}, u32[]{:S(2)}, u32[]{:S(2)}) collective-permute-start(bf16[256,256]{1,0:T(8,128)(2,1)S(1)} %get-tuple-element.24), channel_id=1, source_target_pairs={{0,8},{8,0},{16,24},{24,16},{1,9},{9,1},{17,25},{25,17},{2,10},{10... | collective-permute-start | bytes 393224 | tf_op jit(solution)/shard_map/ppermute | solution.py:448
  15.3 1.3 %collective-permute-start.1 = (bf16[256,256]{1,0:T(8,128)(2,1)S(1)}, bf16[256,256]{1,0:T(8,128)(2,1)S(1)}, u32[]{:S(2)}, u32[]{:S(2)}) collective-permute-start(bf16[256,256]{1,0:T(8,128)(2,1)S(1)} %get-tuple-element.25), channel_id=1, source_target_pairs={{0,8},{8,0},{16,24},{24,16},{1,9},{9,1},{17,25},{25,17},{2,10},{10... | collective-permute-start | bytes 393224 | tf_op jit(solution)/shard_map/ppermute | solution.py:448
  15.4 1.5 %collective-permute-start.2 = (bf16[256,256]{1,0:T(8,128)(2,1)S(1)}, bf16[256,256]{1,0:T(8,128)(2,1)S(1)}, u32[]{:S(2)}, u32[]{:S(2)}) collective-permute-start(bf16[256,256]{1,0:T(8,128)(2,1)S(1)} %get-tuple-element.26), channel_id=1, source_target_pairs={{0,8},{8,0},{16,24},{24,16},{1,9},{9,1},{17,25},{25,17},{2,10},{10... | collective-permute-start | bytes 393224 | tf_op jit(solution)/shard_map/ppermute | solution.py:448
  15.8 1.3 %collective-permute-start.3 = (bf16[256,256]{1,0:T(8,128)(2,1)S(1)}, bf16[256,256]{1,0:T(8,128)(2,1)S(1)}, u32[]{:S(2)}, u32[]{:S(2)}) collective-permute-start(bf16[256,256]{1,0:T(8,128)(2,1)S(1)} %get-tuple-element.27), channel_id=1, source_target_pairs={{0,8},{8,0},{16,24},{24,16},{1,9},{9,1},{17,25},{25,17},{2,10},{10... | collective-permute-start | bytes 393224 | tf_op jit(solution)/shard_map/ppermute | solution.py:448
  20.0 1.2 %collective-permute-start.6 = (bf16[32,256]{1,0:T(8,128)(2,1)S(1)}, bf16[32,256]{1,0:T(8,128)(2,1)S(1)}, u32[]{:S(2)}, u32[]{:S(2)}) collective-permute-start(bf16[32,256]{1,0:T(8,128)(2,1)S(1)} %shard_map.89), channel_id=1, source_target_pairs={{0,8},{8,0},{16,24},{24,16},{1,9},{9,1},{17,25},{25,17},{2,10},{10... | collective-permute-start | bytes 49160 | tf_op jit(solution)/shard_map/ppermute | solution.py:461
  22.2 16.6 %all-to-all-start.1 = ((bf16[8,80,256]{2,1,0:T(8,128)(2,1)}), bf16[8,80,256]{2,1,0:T(8,128)(2,1)S(1)}, u32[]{:S(2)}, u32[]{:S(2)}) async-start(bf16[8,80,256]{2,1,0:T(8,128)(2,1)} %shard_map.90.payload), calls=%async_computation.1 | async-start | bytes 655360 | tf_op jit(solution)/shard_map/all_to_all | solution.py:471
  30.9 11.6 %collective-permute-start.7 = (bf16[1152,256]{1,0:T(8,128)(2,1)S(1)}, bf16[1152,256]{1,0:T(8,128)(2,1)S(1)}, u32[]{:S(2)}, u32[]{:S(2)}) collective-permute-start(bf16[1152,256]{1,0:T(8,128)(2,1)S(1)} %get-tuple-element.33), channel_id=1, source_target_pairs={{8,16},{16,8},{9,17},{17,9},{10,18},{18,10},{11,19},{19,11},{12,20... | collective-permute-start | bytes 1769480 | tf_op jit(solution)/shard_map/ppermute | solution.py:481
  39.3 3.5 %collective-permute-start.8 = (bf16[64,256]{1,0:T(8,128)(2,1)S(1)}, bf16[64,256]{1,0:T(8,128)(2,1)S(1)}, u32[]{:S(2)}, u32[]{:S(2)}) collective-permute-start(bf16[64,256]{1,0:T(8,128)(2,1)S(1)} %shard_map.92.coupled), channel_id=1, source_target_pairs={{0,24},{8,16},{16,8},{24,0},{1,25},{9,17},{17,9},{25,1},{2,26},{10... | collective-permute-start | bytes 98312 | tf_op jit(solution)/shard_map/ppermute | solution.py:491
  45.1 2.0 %collective-permute-start.9 = (bf16[1024,256]{1,0:T(8,128)(2,1)S(1)}, bf16[1024,256]{1,0:T(8,128)(2,1)S(1)}, u32[]{:S(2)}, u32[]{:S(2)}) collective-permute-start(bf16[1024,256]{1,0:T(8,128)(2,1)S(1)} %get-tuple-element.37), channel_id=1, source_target_pairs={{0,8},{8,0},{16,24},{24,16},{1,9},{9,1},{17,25},{25,17},{2,10},{10... | collective-permute-start | bytes 1572872 | tf_op jit(solution)/shard_map/ppermute | solution.py:510

commit v2 on v1

--- a/solution.py
+++ b/solution.py
@@ -130,18 +130,6 @@
     return lax.dot_general(basis, coupled, (((0,), (0,)), ((), ())), preferred_element_type=F32)
 
 
-def fold(wide, target, base):
-    k, width = wide.shape[0], target.shape[1]
-    for p in range(wide.shape[1] // width):
-        target[base + p * k : base + (p + 1) * k, :] = wide[:, p * width : (p + 1) * width]
-
-
-def unfold(source, base, k, points):
-    width = source.shape[1]
-    rows = [source[base + p * k : base + (p + 1) * k, :] for p in range(points // width)]
-    return jnp.concatenate(rows, axis=1)
-
-
 def first_kernel(
     sup, sdn, proj, expn, coup,
     payload, pack, source1, own, expn1, couple1,
@@ -179,18 +167,19 @@
         arrive(other, sems.at[5])
         arrive(after, sems.at[6])
         pack[:k, :points] = other[...]
+        pack[2 * k :, :points] = expn1[...]
         for part in range(2):
-            pack[k:, part * total : (part + 1) * total] = after[part]
+            pack[k : 2 * k, part * total : (part + 1) * total] = after[part]
         arrive(source2, sems.at[7])
         beyond = dot(other[...], source2[...]).astype(BF16)
-        pack[k:, 2 * total : 2 * total + width] = beyond
+        pack[k : 2 * k, 2 * total : 2 * total + width] = beyond
         arrive(own, sems.at[1])
         arrive(source1, sems.at[2])
         arrive(payload.at[:, :, :, pl.ds(0, total)], sems.at[4])
 
 
 def outer_apply_kernel(dup, ddn, source1, *refs):
-    hops, (block, turned, sems) = refs[:CHUNKS], refs[CHUNKS:]
+    hops, (block, turned, result, sems) = refs[:CHUNKS], refs[CHUNKS:]
     outer, first = roles()
 
     @pl.when(outer)
@@ -198,10 +187,14 @@
         load_block(first, dup, ddn, block, sems, 0)
         step = source1.shape[0] // CHUNKS
         turned[...] = rotate(source1[...])
+
+        def one(c, rows):
+            arrive(block.at[:, rows, :], sems.at[c])
+            result[rows, :] = block_rows(block, rows, source1, turned).astype(BF16)
+
+        each_chunk(source1.shape[0], one)
         for c, hop in enumerate(hops):
-            rows = pl.ds(c * step, step)
-            arrive(block.at[:, rows, :], sems.at[c])
-            hop[...] = block_rows(block, rows, source1, turned).astype(BF16)
+            hop[...] = result[c * step : (c + 1) * step, :]
 
 
 def inner_prepare_kernel(dup, ddn, *refs):
@@ -238,8 +231,8 @@
             mixed[:, place : place + k] = dot_rows(parts[part], before[...]).astype(BF16)
 
 
-def outer_couple_kernel(gathered, couple1, mixed, out, sems):
-    del mixed, sems
+def outer_couple_kernel(gathered, couple1, out, sems):
+    del sems
     outer, _ = roles()
 
     @pl.when(outer)
@@ -260,7 +253,7 @@
         small[:k, :] = (sums[:k, :] + dot(mixed[:, k : 2 * k], coeffs)).astype(BF16)
         added = dot(mixed[:, 2 * k : 3 * k], coeffs)
         added = added + dot(mixed[:, 3 * k : 4 * k], rotate(coeffs))
-        added = added + packed[k:, place : place + width].astype(F32)
+        added = added + packed[k : 2 * k, place : place + width].astype(F32)
         small[k : 2 * k, :] = (sums[k:, :] + added).astype(BF16)
         small[2 * k :, :k] = mixed[:half, :k]
         small[2 * k :, k : 2 * k] = mixed[half:, :k]
@@ -272,7 +265,7 @@
 def inner_apply_kernel(dup, ddn, payload, *refs):
     del payload
     arrived, refs = refs[:CHUNKS], refs[CHUNKS:]
-    before, other, expn1, source1, product, trace, block, turned, sems = refs
+    before, other, source1, product, trace, block, turned, sems = refs
     outer, first = roles()
 
     @pl.when(jnp.logical_not(outer))
@@ -280,7 +273,6 @@
         load_block(first, dup, ddn, block, sems, 0)
         points = source1.shape[0]
         step = points // CHUNKS
-        fold(expn1[...], product, points)
         added = expand(other[...], before[...])
         for c, part in enumerate(arrived):
             rows = slice(c * step, (c + 1) * step)
@@ -317,52 +309,86 @@
             added = jnp.concatenate(added, axis=0)
             later[rows, :] = (second[o, k : 2 * k, :].astype(F32) + added).astype(BF16)
         coeffs = later[...]
-        result = dot(packed[k:, :total], coeffs)
-        result = result + dot(packed[k:, total : 2 * total], rotate(coeffs))
+        result = dot(packed[k : 2 * k, :total], coeffs)
+        result = result + dot(packed[k : 2 * k, total : 2 * total], rotate(coeffs))
         out[k:, :] = result.astype(BF16)
 
 
-def settle_kernel(sup, sdn, expn, dup, ddn, coupled, block2, expn2, source2, sems):
+def load_part(first_chunk, which, up_ref, down_ref, block, size, sems, base):
+    for c in range(block.shape[1] // size):
+        source = pl.ds((first_chunk + c) * size, size)
+        pick(
+            which,
+            up_ref.at[0, :, source, :],
+            down_ref.at[0, :, source, :],
+            block.at[:, pl.ds(c * size, size), :],
+            sems.at[base + c],
+        )
+
+
+def each_chunk_of(block, size, body):
+    def one(c, carry):
+        body(c, pl.ds(pl.multiple_of(c * size, size), size))
+        return carry
+
+    lax.fori_loop(0, block.shape[1] // size, one, 0)
+
+
+def settle_kernel(
+    sup, sdn, expn, dup, ddn, coupled, packed, lower, bases, source2, sems
+):
     del coupled
     outer, first = roles()
-    pick(1 - first, sup.at[0], sdn.at[0], source2, sems.at[CHUNKS + 1])
-
-    @pl.when(jnp.logical_not(outer))
-    def _():
-        start(expn.at[0, 1 - first], expn2, sems.at[CHUNKS])
-        load_block(1 - first, dup, ddn, block2, sems, 0)
-        arrive(expn2, sems.at[CHUNKS])
-        each_chunk(
-            block2.shape[1], lambda c, rows: arrive(block2.at[:, rows, :], sems.at[c])
+    pick(1 - first, sup.at[0], sdn.at[0], source2, sems.at[0])
+
+    @pl.when(jnp.logical_not(outer))
+    def _():
+        k, points = bases.shape[0] // 2, bases.shape[1]
+        start(expn.at[0, 1 - first], bases.at[pl.ds(k, k), :], sems.at[1])
+        step = points // CHUNKS
+        load_part(0, 1 - first, dup, ddn, lower, step, sems, 2)
+        bases[:k, :] = packed[2 * k :, :points]
+        arrive(bases.at[pl.ds(k, k), :], sems.at[1])
+        each_chunk_of(
+            lower, step, lambda c, rows: arrive(lower.at[:, rows, :], sems.at[2 + c])
         )
 
-    arrive(source2, sems.at[CHUNKS + 1])
+    arrive(source2, sems.at[0])
 
 
 def inner_second_kernel(
-    crossed, coupled, source2, block2, expn2, out, trace, turned, sems
+    dup, ddn, crossed, coupled, source2, lower, bases,
+    out, trace, turned, upper, sems,
 ):
-    del sems
-    outer, _ = roles()
-
-    @pl.when(jnp.logical_not(outer))
-    def _():
-        k, points = expn2.shape
+    outer, first = roles()
+
+    @pl.when(jnp.logical_not(outer))
+    def _():
+        k, points = coupled.shape[0] // 2, bases.shape[1]
         step = points // CHUNKS
-        added = expand(unfold(crossed, points, k, points), coupled[:k, :])
+        load_part(CHUNKS // 2, 1 - first, dup, ddn, upper, step, sems, 0)
+
+        added = expand(bases[:k, :], coupled[:k, :])
         for c in range(CHUNKS):
             rows = slice(c * step, (c + 1) * step)
             value = source2[rows, :].astype(F32) + crossed[rows, :].astype(F32)
             value = (value + added[rows, :]).astype(BF16)
             trace[rows, :] = value
             turned[rows, :] = rotate(value)
-        out[...] = expand(expn2[...], coupled[k:, :]).astype(BF16)
-
-        def apply(c, rows):
-            value = block_rows(block2, rows, trace, turned) + out[rows, :].astype(F32)
-            out[rows, :] = value.astype(BF16)
-
-        each_chunk(points, apply)
+        out[...] = expand(bases[k:, :], coupled[k:, :]).astype(BF16)
+
+        def put(block, rows, base):
+            place = pl.ds(pl.multiple_of(rows.start + base, step), step)
+            value = block_rows(block, rows, trace, turned) + out[place, :].astype(F32)
+            out[place, :] = value.astype(BF16)
+
+        each_chunk_of(lower, step, lambda c, rows: put(lower, rows, 0))
+
+        def second(c, rows):
+            arrive(upper.at[:, rows, :], sems.at[c])
+            put(upper, rows, points // 2)
+
+        each_chunk_of(upper, step, second)
 
 
 def last_kernel(arrived, one, two, source1, source2, up, down, sums, sems):
@@ -377,6 +403,15 @@
         def _():
             start(source, down.at[0], sem)
 
+    def put_rows(which, rows, sem):
+        @pl.when(which == 0)
+        def _():
+            start(sums.at[rows, :], up.at[0, rows, :], sem)
+
+        @pl.when(which != 0)
+        def _():
+            start(sums.at[rows, :], down.at[0, rows, :], sem)
+
     @pl.when(outer)
     def _():
         put(first, source1, sems.at[0])
@@ -384,9 +419,9 @@
         def add(c, rows):
             value = source2[rows, :].astype(F32) + arrived[rows, :].astype(F32)
             sums[rows, :] = value.astype(BF16)
+            put_rows(1 - first, rows, sems.at[1])
 
         each_chunk(sums.shape[0], add)
-        put(1 - first, sums, sems.at[1])
 
     @pl.when(jnp.logical_not(outer))
     def _():
@@ -407,7 +442,6 @@
     swap = [(g, g ^ 1) for g in range(layers)]
     across = [(g, layers - 1 - g) for g in range(layers)]
     inside = across[1:-1]
-    folded = k * points // width
 
     def like(*shape):
         return jax.ShapeDtypeStruct(shape, BF16)
@@ -425,7 +459,7 @@
         first_kernel,
         (
             like(owners, 2, k, max(total, width)),
-            *(kept(2 * k, packing), kept(*field), kept(*basis), kept(*basis), kept(*couple)),
+            *(kept(3 * k, packing), kept(*field), kept(*basis), kept(*basis), kept(*couple)),
         ),
         (source_up, source_down, projection, expansion, coupling),
         (),
@@ -441,7 +475,7 @@
         (kept(points // CHUNKS, width),) * CHUNKS,
         diagonals,
         (source1,),
-        [block, field],
+        [block, field, field],
         CHUNKS,
         **large,
     )
@@ -456,7 +490,7 @@
         **large,
     )
     (before,) = call(
-        outer_couple_kernel, (kept(k, width),), (), (gathered, couple1, mixed), [], 1, **small
+        outer_couple_kernel, (kept(k, width),), (), (gathered, couple1), [], 1, **small
     )
     before = lax.ppermute(before, "layer", swap)
     (payload,) = call(
@@ -471,14 +505,14 @@
     second = lax.all_to_all(payload, "trace", 0, 0)
     product, one = call(
         inner_apply_kernel,
-        (kept(points + folded, width), kept(*field)),
+        (kept(*field), kept(*field)),
         (*diagonals, payload),
-        (*arrived, before, other, expn1, source1),
+        (*arrived, before, other, source1),
         [block, field],
         CHUNKS,
         **large,
     )
-    crossed = lax.ppermute(product, "layer", inside)
+    crossed = lax.ppermute(product, "layer", across)
     (coupled,) = call(
         inner_couple_kernel,
         (kept(2 * k, width),),
@@ -489,22 +523,22 @@
         **small,
     )
     reached = lax.ppermute(coupled, "layer", across)
-    block2, expn2, source2 = call(
+    lower, bases, source2 = call(
         settle_kernel,
-        (kept(*block), kept(*basis), kept(*field)),
+        (kept(2, points // 2, points), kept(2 * k, points), kept(*field)),
         (source_up, source_down, expansion, *diagonals),
-        (coupled,),
+        (coupled, packed),
         [],
-        CHUNKS + 2,
+        2 + CHUNKS // 2,
         **large,
     )
     result, two = call(
         inner_second_kernel,
         (kept(*field), kept(*field)),
-        (),
-        (crossed, reached, source2, block2, expn2),
-        [field],
-        1,
+        diagonals,
+        (crossed, reached, source2, lower, bases),
+        [field, (2, points // 2, points)],
+        CHUNKS // 2,
         **large,
     )
     arrived = lax.ppermute(result, "layer", swap)

time: 48.5 us -> 44.3 us (0.913)
  waiting for transfers between devices: 10.4 us -> 6.65 us
  Pallas kernels: 14.6 us -> 14 us
    ppermute x1, starting transfers between devices: 0.07 us -> 2.95 us  [wave(): before = lax.ppermute(before, 'layer', swap)]
    all_to_all x1, starting transfers between devices: 5.73 us -> 3.45 us  [wave(): second = lax.all_to_all(payload, 'trace', 0, 0)]
    ppermute x1, starting transfers between devices: 0.07 us -> 1.75 us  [wave(): reached = lax.ppermute(coupled, 'layer', across)]
    ppermute x4, waiting for transfers between devices: 1.26 us -> 0.01 us  [wave(): arrived = [lax.ppermute(hop, 'layer', swap) for hop in hops]]
    all_to_all x1, waiting for transfers between devices: 5.06 us -> 3.87 us  [wave(): second = lax.all_to_all(payload, 'trace', 0, 0)]
    ppermute x1, waiting for transfers between devices: 1.17 us -> 0.01 us  [wave(): before = lax.ppermute(before, 'layer', swap)]
    ppermute x1, starting transfers between devices: 2.73 us -> 1.58 us  [wave(): crossed = lax.ppermute(product, 'layer', across)]
    ppermute x4, starting transfers between devices: 5.07 us -> 4.11 us  [wave(): arrived = [lax.ppermute(hop, 'layer', swap) for hop in hops]]
  transfers between devices with their start and end apart: 12 -> 12, of which waited for: 9 -> 3; matrix products, arithmetic and copies ran while one was open for 0% -> 0% of each run, Pallas kernels for 18% -> 19%
where the time goes in v2:
time: 44.3 us; the launch traced here: 43.9 us
  starting transfers between devices  22.4 us (51%)
  Pallas kernels  14 us (32%)
  waiting for transfers between devices  6.65 us (15%)
  between operations  0.77 us (2%)
    pallas_call x10, Pallas kernels, call(): pl.pallas_call(body, out_shape=tuple((pltpu.VMEM(*out) if keep else out f...  14 us
    all_to_all x1, starting transfers between devices, wave(): gathered = lax.all_to_all(payload, 'trace', 0, 0)  6.37 us
    ppermute x4, starting transfers between devices, wave(): arrived = [lax.ppermute(hop, 'layer', swap) for hop in hops]  4.11 us
    all_to_all x1, waiting for transfers between devices, wave(): second = lax.all_to_all(payload, 'trace', 0, 0)  3.87 us
    all_to_all x1, starting transfers between devices, wave(): second = lax.all_to_all(payload, 'trace', 0, 0)  3.45 us
    ppermute x1, starting transfers between devices, wave(): before = lax.ppermute(before, 'layer', swap)  2.95 us
    ppermute x1, waiting for transfers between devices, wave(): arrived = lax.ppermute(result, 'layer', swap)  1.9 us
    ppermute x1, starting transfers between devices, wave(): reached = lax.ppermute(coupled, 'layer', across)  1.75 us
  transfers between devices with their start and end apart: 12, of which 3 were waited for; matrix products, arithmetic and copies ran while one was open for 0% of the time, Pallas kernels for 19%

profile of v2, /device:TPU:1, one launch (start us, length us, event | category | flops | bytes accessed | tf_op | source)
XLA Modules:
  0.0 43.9 jit_solution(15959804039730011631)
XLA Ops:
  0.6 1.6 %shard_map.86 = (bf16[8,2,32,256]{3,2,1,0:T(8,128)(2,1)}, bf16[96,1024]{1,0:T(8,128)(2,1)S(1)}, bf16[1024,256]{1,0:T(8,128)(2,1)S(1)}, bf16[32,1024]{1,0:T(8,128...) custom-call(bf16[1,1024,256]{2,1,0:T(8,128)(2,1)} %sup.3, bf16[1,1024,256]{2,1,0:T(8,128)(2,1)} %sdn.3, ...), custom_call_target="tpu_custom_call" | custom-call | flops 16777216 | bytes 1048576 | tf_op jit(solution)/shard_map/pallas_call | solution.py:57
  2.2 6.4 %all-to-all-start = ((bf16[8,2,32,256]{3,2,1,0:T(8,128)(2,1)}), bf16[8,2,32,256]{3,2,1,0:T(8,128)(2,1)S(1)}, u32[]{:S(2)}, u32[]{:S(2)}) async-start(bf16[8,2,32,256]{3,2,1,0:T(8,128)(2,1)} %get-tuple-element.21), calls=%async_computation | async-start | bytes 524288 | tf_op jit(solution)/shard_map/all_to_all | solution.py:470
  8.6 1.4 %collective-permute-start.6 = (bf16[32,1024]{1,0:T(8,128)(2,1)S(1)}, bf16[32,1024]{1,0:T(8,128)(2,1)S(1)}, u32[]{:S(2)}, u32[]{:S(2)}) collective-permute-start(bf16[32,1024]{1,0:T(8,128)(2,1)S(1)} %get-tuple-element.30.refs_7_), channel_id=1, source_target_pairs={{0,8},{8,0},{16,24},{24,16},{1,9},{9,1},{17,25},{25,17},{2,10},{10... | collective-permute-start | bytes 196616 | tf_op jit(solution)/shard_map/ppermute | solution.py:472
  10.0 0.8 %collective-permute-start.5 = (bf16[96,1024]{1,0:T(8,128)(2,1)S(1)}, bf16[96,1024]{1,0:T(8,128)(2,1)S(1)}, u32[]{:S(2)}, u32[]{:S(2)}) collective-permute-start(bf16[96,1024]{1,0:T(8,128)(2,1)S(1)} %get-tuple-element.28), channel_id=1, source_target_pairs={{0,24},{8,16},{16,8},{24,0},{1,25},{9,17},{17,9},{25,1},{2,26},{10... | collective-permute-start | bytes 589832 | tf_op jit(solution)/shard_map/ppermute | solution.py:471
  10.8 3.5 %collective-permute-start.1 = (bf16[256,256]{1,0:T(8,128)(2,1)S(1)}, bf16[256,256]{1,0:T(8,128)(2,1)S(1)}, u32[]{:S(2)}, u32[]{:S(2)}) collective-permute-start(bf16[256,256]{1,0:T(8,128)(2,1)S(1)} %get-tuple-element.24), channel_id=1, source_target_pairs={{0,8},{8,0},{16,24},{24,16},{1,9},{9,1},{17,25},{25,17},{2,10},{10... | collective-permute-start | bytes 393224 | tf_op jit(solution)/shard_map/ppermute | solution.py:482
  14.3 0.1 collective-permute-start.2
  14.4 0.4 collective-permute-start.3
  14.8 0.0 collective-permute-done.6.refs_8_.refs_5_
  14.8 0.1 collective-permute-start.4
  14.9 0.9 %all-to-all-done.gathered = bf16[8,2,32,256]{3,2,1,0:T(8,128)(2,1)S(1)} async-done(((bf16[8,2,32,256]{3,2,1,0:T(8,128)(2,1)}), bf16[8,2,32,256]{3,2,1,0:T(8,128)(2,1)S(1)}, u32[]{:S(2)}, u32[]{:S(2)}) %all-to-all-start) | async-done | bytes 262176 | tf_op jit(solution)/shard_map/all_to_all | solution.py:470
  15.8 0.0 collective-permute-done.1.refs_0_
  15.8 3.0 %collective-permute-start = (bf16[32,256]{1,0:T(8,128)(2,1)S(1)}, bf16[32,256]{1,0:T(8,128)(2,1)S(1)}, u32[]{:S(2)}, u32[]{:S(2)}) collective-permute-start(bf16[32,256]{1,0:T(8,128)(2,1)S(1)} %shard_map.87), channel_id=1, source_target_pairs={{0,8},{8,0},{16,24},{24,16},{1,9},{9,1},{17,25},{25,17},{2,10},{10... | collective-permute-start | bytes 49160 | tf_op jit(solution)/shard_map/ppermute | solution.py:495
  18.8 0.0 collective-permute-done.2.refs_1_
  18.8 0.0 collective-permute-done.3.refs_2_
  18.8 0.0 collective-permute-done.4.refs_3_
  18.8 0.0 collective-permute-done.5.refs_4_.packed
  18.8 2.8 %shard_map.89 = (f32[64,256]{1,0:T(8,128)S(1)}, bf16[32,128]{1,0:T(8,128)(2,1)S(1)}) custom-call(bf16[1,2,1024,1024]{3,2,1,0:T(8,128)(2,1)} %dup.9, bf16[1,2,1024,1024]{3,2,1,0:T(8,128)(2,1)} %ddn.9, bf16[256,256]{1,0:T(8,128)(2,1)S(1)} %collective-permute-done.1.refs_0_, bf16[256,256]{1,0:T(8,128)(2,1)S(1)} %collective-permute-done.2.refs_1_, ...), custom_call_target="tpu_custom_call" | custom-call | flops 1073741824 | bytes 4194304 | tf_op jit(solution)/shard_map/pallas_call | solution.py:57
  21.6 0.0 collective-permute-done.before.refs_4_
  21.6 0.9 %shard_map.90.payload = bf16[8,80,256]{2,1,0:T(8,128)(2,1)} custom-call(bf16[32,256]{1,0:T(8,128)(2,1)S(1)} %collective-permute-done.before.refs_4_, f32[64,256]{1,0:T(8,128)S(1)} %get-tuple-element.31.sums, bf16[32,128]{1,0:T(8,128)(2,1)S(1)} %get-tuple-element.32.mixed, bf16[96,1024]{1,0:T(8,128)(2,1)S(1)} %collective-permute-done.5.refs_4_.packed), custom_call_target="tpu_custom_call" | custom-call | flops 16777216 | bytes 1048576 | tf_op jit(solution)/shard_map/pallas_call | solution.py:57
  22.6 3.4 %all-to-all-start.1 = ((bf16[8,80,256]{2,1,0:T(8,128)(2,1)}), bf16[8,80,256]{2,1,0:T(8,128)(2,1)S(1)}, u32[]{:S(2)}, u32[]{:S(2)}) async-start(bf16[8,80,256]{2,1,0:T(8,128)(2,1)} %shard_map.90.payload), calls=%async_computation.1 | async-start | bytes 655360 | tf_op jit(solution)/shard_map/all_to_all | solution.py:505
  26.0 3.0 %shard_map.91 = (bf16[1024,256]{1,0:T(8,128)(2,1)S(1)}, bf16[1024,256]{1,0:T(8,128)(2,1)S(1)}) custom-call(bf16[1,2,1024,1024]{3,2,1,0:T(8,128)(2,1)} %dup.9, bf16[1,2,1024,1024]{3,2,1,0:T(8,128)(2,1)} %ddn.9, bf16[8,80,256]{2,1,0:T(8,128)(2,1)} %shard_map.90.payload, bf16[256,256]{1,0:T(8,128)(2,1)S(1)} %collective-permute-done.1.refs_0_, ...), custom_call_target="tpu_custom_call" | custom-call | flops 1073741824 | bytes 4194304 | tf_op jit(solution)/shard_map/pallas_call | solution.py:57
  29.1 1.6 %collective-permute-start.7 = (bf16[1024,256]{1,0:T(8,128)(2,1)S(1)}, bf16[1024,256]{1,0:T(8,128)(2,1)S(1)}, u32[]{:S(2)}, u32[]{:S(2)}) collective-permute-start(bf16[1024,256]{1,0:T(8,128)(2,1)S(1)} %get-tuple-element.33), channel_id=1, source_target_pairs={{0,24},{8,16},{16,8},{24,0},{1,25},{9,17},{17,9},{25,1},{2,26},{10... | collective-permute-start | bytes 1572872 | tf_op jit(solution)/shard_map/ppermute | solution.py:515
  30.7 3.9 %all-to-all-done.1.second = bf16[8,80,256]{2,1,0:T(8,128)(2,1)S(1)} async-done(((bf16[8,80,256]{2,1,0:T(8,128)(2,1)}), bf16[8,80,256]{2,1,0:T(8,128)(2,1)S(1)}, u32[]{:S(2)}, u32[]{:S(2)}) %all-to-all-start.1) | async-done | bytes 327712 | tf_op jit(solution)/shard_map/all_to_all | solution.py:505
  34.5 0.6 %shard_map.92.coupled = bf16[64,256]{1,0:T(8,128)(2,1)S(1)} custom-call(bf16[8,2,32,256]{3,2,1,0:T(8,128)(2,1)S(1)} %all-to-all-done.gathered, bf16[8,80,256]{2,1,0:T(8,128)(2,1)S(1)} %all-to-all-done.1.second, bf16[96,1024]{1,0:T(8,128)(2,1)S(1)} %collective-permute-done.5.refs_4_.packed, bf16[2,32,256]{2,1,0:T(8,128)(2,1)S(1)} %get-tuple-element.22.couple1), custom_call_target="tpu_custom_call" | custom-call | flops 16777216 | bytes 1048576 | tf_op jit(solution)/shard_map/pallas_call | solution.py:57
  35.1 1.8 %collective-permute-start.8 = (bf16[64,256]{1,0:T(8,128)(2,1)S(1)}, bf16[64,256]{1,0:T(8,128)(2,1)S(1)}, u32[]{:S(2)}, u32[]{:S(2)}) collective-permute-start(bf16[64,256]{1,0:T(8,128)(2,1)S(1)} %shard_map.92.coupled), channel_id=1, source_target_pairs={{0,24},{8,16},{16,8},{24,0},{1,25},{9,17},{17,9},{25,1},{2,26},{10... | collective-permute-start | bytes 98312 | tf_op jit(solution)/shard_map/ppermute | solution.py:525
  36.9 1.8 %shard_map.93 = (bf16[2,512,1024]{2,1,0:T(8,128)(2,1)S(1)}, bf16[64,1024]{1,0:T(8,128)(2,1)S(1)}, bf16[1024,256]{1,0:T(8,128)(2,1)S(1)}) custom-call(bf16[1,1024,256]{2,1,0:T(8,128)(2,1)} %sup.3, bf16[1,1024,256]{2,1,0:T(8,128)(2,1)} %sdn.3, bf16[1,2,32,1024]{3,2,1,0:T(8,128)(2,1)} %expn.3, bf16[1,2,1024,1024]{3,2,1,0:T(8,128)(2,1)} %dup.9, ...), custom_call_target="tpu_custom_call" | custom-call | flops 1073741824 | bytes 4194304 | tf_op jit(solution)/shard_map/pallas_call | solution.py:57
  38.6 0.0 collective-permute-done.7.crossed
  38.6 0.0 collective-permute-done.8.coupled
  38.7 2.3 %shard_map.94 = (bf16[1024,256]{1,0:T(8,128)(2,1)S(1)}, bf16[1024,256]{1,0:T(8,128)(2,1)S(1)}) custom-call(bf16[1,2,1024,1024]{3,2,1,0:T(8,128)(2,1)} %dup.9, bf16[1,2,1024,1024]{3,2,1,0:T(8,128)(2,1)} %ddn.9, bf16[1024,256]{1,0:T(8,128)(2,1)S(1)} %collective-permute-done.7.crossed, bf16[64,256]{1,0:T(8,128)(2,1)S(1)} %collective-permute-done.8.coupled, ...), custom_call_target="tpu_custom_call" | custom-call | flops 1073741824 | bytes 4194304 | tf_op jit(solution)/shard_map/pallas_call | solution.py:57
  40.9 0.1 collective-permute-start.9
  41.0 1.9 %collective-permute-done.9.arrived = bf16[1024,256]{1,0:T(8,128)(2,1)S(1)} collective-permute-done((bf16[1024,256]{1,0:T(8,128)(2,1)S(1)}, bf16[1024,256]{1,0:T(8,128)(2,1)S(1)}, u32[]{:S(2)}, u32[]{:S(2)}) %collective-permute-start.9) | collective-permute-done | bytes 524320 | tf_op jit(solution)/shard_map/ppermute | solution.py:544
  42.9 1.0 %shard_map.95 = (bf16[1,1024,256]{2,1,0:T(8,128)(2,1)}, bf16[1,1024,256]{2,1,0:T(8,128)(2,1)}) custom-call(bf16[1024,256]{1,0:T(8,128)(2,1)S(1)} %collective-permute-done.9.arrived, bf16[1024,256]{1,0:T(8,128)(2,1)S(1)} %get-tuple-element.38.one, bf16[1024,256]{1,0:T(8,128)(2,1)S(1)} %get-tuple-element.39.two, ...), custom_call_target="tpu_custom_call" | custom-call | flops 16777216 | bytes 1048576 | tf_op jit(solution)/shard_map/pallas_call | solution.py:57
  (2 shorter events, 0.0 us)
Async XLA Ops:
  2.2 13.5 %all-to-all-start = ((bf16[8,2,32,256]{3,2,1,0:T(8,128)(2,1)}), bf16[8,2,32,256]{3,2,1,0:T(8,128)(2,1)S(1)}, u32[]{:S(2)}, u32[]{:S(2)}) async-start(bf16[8,2,32,256]{3,2,1,0:T(8,128)(2,1)} %get-tuple-element.21), calls=%async_computation | async-start | bytes 524288 | tf_op jit(solution)/shard_map/all_to_all | solution.py:470
  8.6 6.2 %collective-permute-start.6 = (bf16[32,1024]{1,0:T(8,128)(2,1)S(1)}, bf16[32,1024]{1,0:T(8,128)(2,1)S(1)}, u32[]{:S(2)}, u32[]{:S(2)}) collective-permute-start(bf16[32,1024]{1,0:T(8,128)(2,1)S(1)} %get-tuple-element.30.refs_7_), channel_id=1, source_target_pairs={{0,8},{8,0},{16,24},{24,16},{1,9},{9,1},{17,25},{25,17},{2,10},{10... | collective-permute-start | bytes 196616 | tf_op jit(solution)/shard_map/ppermute | solution.py:472
  10.0 8.8 %collective-permute-start.5 = (bf16[96,1024]{1,0:T(8,128)(2,1)S(1)}, bf16[96,1024]{1,0:T(8,128)(2,1)S(1)}, u32[]{:S(2)}, u32[]{:S(2)}) collective-permute-start(bf16[96,1024]{1,0:T(8,128)(2,1)S(1)} %get-tuple-element.28), channel_id=1, source_target_pairs={{0,24},{8,16},{16,8},{24,0},{1,25},{9,17},{17,9},{25,1},{2,26},{10... | collective-permute-start | bytes 589832 | tf_op jit(solution)/shard_map/ppermute | solution.py:471
  10.8 5.0 %collective-permute-start.1 = (bf16[256,256]{1,0:T(8,128)(2,1)S(1)}, bf16[256,256]{1,0:T(8,128)(2,1)S(1)}, u32[]{:S(2)}, u32[]{:S(2)}) collective-permute-start(bf16[256,256]{1,0:T(8,128)(2,1)S(1)} %get-tuple-element.24), channel_id=1, source_target_pairs={{0,8},{8,0},{16,24},{24,16},{1,9},{9,1},{17,25},{25,17},{2,10},{10... | collective-permute-start | bytes 393224 | tf_op jit(solution)/shard_map/ppermute | solution.py:482
  14.3 4.4 %collective-permute-start.2 = (bf16[256,256]{1,0:T(8,128)(2,1)S(1)}, bf16[256,256]{1,0:T(8,128)(2,1)S(1)}, u32[]{:S(2)}, u32[]{:S(2)}) collective-permute-start(bf16[256,256]{1,0:T(8,128)(2,1)S(1)} %get-tuple-element.25), channel_id=1, source_target_pairs={{0,8},{8,0},{16,24},{24,16},{1,9},{9,1},{17,25},{25,17},{2,10},{10... | collective-permute-start | bytes 393224 | tf_op jit(solution)/shard_map/ppermute | solution.py:482
  14.4 4.4 %collective-permute-start.3 = (bf16[256,256]{1,0:T(8,128)(2,1)S(1)}, bf16[256,256]{1,0:T(8,128)(2,1)S(1)}, u32[]{:S(2)}, u32[]{:S(2)}) collective-permute-start(bf16[256,256]{1,0:T(8,128)(2,1)S(1)} %get-tuple-element.26), channel_id=1, source_target_pairs={{0,8},{8,0},{16,24},{24,16},{1,9},{9,1},{17,25},{25,17},{2,10},{10... | collective-permute-start | bytes 393224 | tf_op jit(solution)/shard_map/ppermute | solution.py:482
  14.8 3.9 %collective-permute-start.4 = (bf16[256,256]{1,0:T(8,128)(2,1)S(1)}, bf16[256,256]{1,0:T(8,128)(2,1)S(1)}, u32[]{:S(2)}, u32[]{:S(2)}) collective-permute-start(bf16[256,256]{1,0:T(8,128)(2,1)S(1)} %get-tuple-element.27), channel_id=1, source_target_pairs={{0,8},{8,0},{16,24},{24,16},{1,9},{9,1},{17,25},{25,17},{2,10},{10... | collective-permute-start | bytes 393224 | tf_op jit(solution)/shard_map/ppermute | solution.py:482
  15.8 5.8 %collective-permute-start = (bf16[32,256]{1,0:T(8,128)(2,1)S(1)}, bf16[32,256]{1,0:T(8,128)(2,1)S(1)}, u32[]{:S(2)}, u32[]{:S(2)}) collective-permute-start(bf16[32,256]{1,0:T(8,128)(2,1)S(1)} %shard_map.87), channel_id=1, source_target_pairs={{0,8},{8,0},{16,24},{24,16},{1,9},{9,1},{17,25},{25,17},{2,10},{10... | collective-permute-start | bytes 49160 | tf_op jit(solution)/shard_map/ppermute | solution.py:495
  22.6 12.0 %all-to-all-start.1 = ((bf16[8,80,256]{2,1,0:T(8,128)(2,1)}), bf16[8,80,256]{2,1,0:T(8,128)(2,1)S(1)}, u32[]{:S(2)}, u32[]{:S(2)}) async-start(bf16[8,80,256]{2,1,0:T(8,128)(2,1)} %shard_map.90.payload), calls=%async_computation.1 | async-start | bytes 655360 | tf_op jit(solution)/shard_map/all_to_all | solution.py:505
  29.1 9.6 %collective-permute-start.7 = (bf16[1024,256]{1,0:T(8,128)(2,1)S(1)}, bf16[1024,256]{1,0:T(8,128)(2,1)S(1)}, u32[]{:S(2)}, u32[]{:S(2)}) collective-permute-start(bf16[1024,256]{1,0:T(8,128)(2,1)S(1)} %get-tuple-element.33), channel_id=1, source_target_pairs={{0,24},{8,16},{16,8},{24,0},{1,25},{9,17},{17,9},{25,1},{2,26},{10... | collective-permute-start | bytes 1572872 | tf_op jit(solution)/shard_map/ppermute | solution.py:515
  35.1 3.5 %collective-permute-start.8 = (bf16[64,256]{1,0:T(8,128)(2,1)S(1)}, bf16[64,256]{1,0:T(8,128)(2,1)S(1)}, u32[]{:S(2)}, u32[]{:S(2)}) collective-permute-start(bf16[64,256]{1,0:T(8,128)(2,1)S(1)} %shard_map.92.coupled), channel_id=1, source_target_pairs={{0,24},{8,16},{16,8},{24,0},{1,25},{9,17},{17,9},{25,1},{2,26},{10... | collective-permute-start | bytes 98312 | tf_op jit(solution)/shard_map/ppermute | solution.py:525
  40.9 2.0 %collective-permute-start.9 = (bf16[1024,256]{1,0:T(8,128)(2,1)S(1)}, bf16[1024,256]{1,0:T(8,128)(2,1)S(1)}, u32[]{:S(2)}, u32[]{:S(2)}) collective-permute-start(bf16[1024,256]{1,0:T(8,128)(2,1)S(1)} %get-tuple-element.37), channel_id=1, source_target_pairs={{0,8},{8,0},{16,24},{24,16},{1,9},{9,1},{17,25},{25,17},{2,10},{10... | collective-permute-start | bytes 1572872 | tf_op jit(solution)/shard_map/ppermute | solution.py:544

commit v3 on v2

--- a/solution.py
+++ b/solution.py
@@ -181,10 +181,10 @@
 def outer_apply_kernel(dup, ddn, source1, *refs):
     hops, (block, turned, result, sems) = refs[:CHUNKS], refs[CHUNKS:]
     outer, first = roles()
+    load_block(first, dup, ddn, block, sems, 0)
 
     @pl.when(outer)
     def _():
-        load_block(first, dup, ddn, block, sems, 0)
         step = source1.shape[0] // CHUNKS
         turned[...] = rotate(source1[...])
 
@@ -196,43 +196,58 @@
         for c, hop in enumerate(hops):
             hop[...] = result[c * step : (c + 1) * step, :]
 
-
-def inner_prepare_kernel(dup, ddn, *refs):
+    @pl.when(jnp.logical_not(outer))
+    def _():
+        each_chunk(
+            block.shape[1], lambda c, rows: arrive(block.at[:, rows, :], sems.at[c])
+        )
+
+
+def inner_mix_kernel(block, packed, own, expn1, before, basis, mixed, sems):
+    del sems
+    outer, _ = roles()
+
+    @pl.when(jnp.logical_not(outer))
+    def _():
+        k, points = own.shape
+        other = packed[:k, :points]
+        mixed[:, :k] = dot_rows(other, expn1[...]).astype(BF16)
+        step = points // CHUNKS
+        parts = [0.0, 0.0]
+        for c in range(CHUNKS):
+            rows = pl.ds(c * step, step)
+            for part in range(2):
+                columns = other[:, c * step : (c + 1) * step]
+                parts[part] = parts[part] + dot(columns, block[part, rows, :])
+        basis[:k, :] = own[...]
+        for part in range(2):
+            basis[(1 + part) * k : (2 + part) * k, :] = parts[part].astype(BF16)
+        value = dot_rows(basis[...], before[...]).astype(BF16)
+        for part in range(3):
+            mixed[:, (1 + part) * k : (2 + part) * k] = value[part * k : (part + 1) * k, :]
+
+
+def inner_prepare_kernel(*refs):
     arrived, refs = refs[:CHUNKS], refs[CHUNKS:]
-    packed, source1, own, expn1, before, sums, mixed, block, field, turned, sems = refs
-    outer, first = roles()
-
-    @pl.when(jnp.logical_not(outer))
-    def _():
-        load_block(first, dup, ddn, block, sems, 0)
-        k, points = own.shape
-
+    source1, basis, sums, field, turned, sems = refs
+    del sems
+    outer, _ = roles()
+
+    @pl.when(jnp.logical_not(outer))
+    def _():
+        k, points = basis.shape[0] // 3, basis.shape[1]
         step = points // CHUNKS
         for c, part in enumerate(arrived):
             rows = slice(c * step, (c + 1) * step)
             value = (source1[rows, :].astype(F32) + part[...].astype(F32)).astype(BF16)
             field[rows, :] = value
             turned[rows, :] = rotate(value)
-        other = packed[:k, :points]
-        sums[:k, :] = dot(own[...], field[...])
-        mixed[:, :k] = dot_rows(other, expn1[...]).astype(BF16)
-        mixed[:, k : 2 * k] = dot_rows(own[...], before[...]).astype(BF16)
-        parts = [0.0, 0.0]
-        for c in range(CHUNKS):
-            rows = pl.ds(c * step, step)
-            arrive(block.at[:, rows, :], sems.at[c])
-            for part in range(2):
-                columns = other[:, c * step : (c + 1) * step]
-                parts[part] = parts[part] + dot(columns, block[part, rows, :])
-        parts = [part.astype(BF16) for part in parts]
-        sums[k:, :] = dot(parts[0], field[...]) + dot(parts[1], turned[...])
-        for part in range(2):
-            place = (2 + part) * k
-            mixed[:, place : place + k] = dot_rows(parts[part], before[...]).astype(BF16)
-
-
-def outer_couple_kernel(gathered, couple1, out, sems):
-    del sems
+        sums[...] = dot(basis[: 2 * k, :], field[...])
+        sums[k:, :] += dot(basis[2 * k :, :], turned[...])
+
+
+def outer_couple_kernel(gathered, couple1, mixed, out, sems):
+    del mixed, sems
     outer, _ = roles()
 
     @pl.when(outer)
@@ -468,31 +483,42 @@
         **small,
     )
     gathered = lax.all_to_all(payload, "trace", 0, 0)
-    packed = lax.ppermute(pack, "layer", across)
+    pairs = [(a * owners + o, b * owners + o) for a, b in inside for o in range(owners)]
+    pairs += [(g * owners + o, g * owners + (o ^ 1)) for g in (0, layers - 1) for o in range(owners)]
+    packed = lax.ppermute(pack, ("layer", "trace"), pairs)
     other = lax.ppermute(expn1, "layer", swap)
-    hops = call(
+    *hops, block1 = call(
         outer_apply_kernel,
-        (kept(points // CHUNKS, width),) * CHUNKS,
+        (kept(points // CHUNKS, width),) * CHUNKS + (kept(*block),),
         diagonals,
         (source1,),
-        [block, field, field],
+        [field, field],
         CHUNKS,
         **large,
     )
     arrived = [lax.ppermute(hop, "layer", swap) for hop in hops]
-    sums, mixed = call(
+    basis1, mixed = call(
+        inner_mix_kernel,
+        (kept(3 * k, points), kept(k, 4 * k)),
+        (),
+        (block1, packed, own, expn1, other),
+        [],
+        1,
+        **large,
+    )
+    (before,) = call(
+        outer_couple_kernel, (kept(k, width),), (), (gathered, couple1, mixed), [], 1, **small
+    )
+    before = lax.ppermute(before, "layer", swap)
+    (sums,) = call(
         inner_prepare_kernel,
-        (kept(2 * k, width, of=F32), kept(k, 4 * k)),
-        diagonals,
-        (*arrived, packed, source1, own, expn1, other),
-        [block, field, field],
-        CHUNKS,
-        **large,
-    )
-    (before,) = call(
-        outer_couple_kernel, (kept(k, width),), (), (gathered, couple1), [], 1, **small
-    )
-    before = lax.ppermute(before, "layer", swap)
+        (kept(2 * k, width, of=F32),),
+        (),
+        (*arrived, source1, basis1),
+        [field, field],
+        1,
+        **small,
+    )
     (payload,) = call(
         inner_gather_kernel,
         (like(owners, 2 * k + k // 2, width),),
@@ -502,7 +528,10 @@
         1,
         **small,
     )
-    second = lax.all_to_all(payload, "trace", 0, 0)
+    half = owners // 2
+    ends = [[g * owners + p * half + o for g in (0, layers - 1) for o in range(half)] for p in range(2)]
+    groups = [[g * owners + o for o in range(owners)] for g in range(1, layers - 1)] + ends
+    second = lax.all_to_all(payload, ("layer", "trace"), 0, 0, axis_index_groups=groups)
     product, one = call(
         inner_apply_kernel,
         (kept(*field), kept(*field)),
@@ -512,7 +541,7 @@
         CHUNKS,
         **large,
     )
-    crossed = lax.ppermute(product, "layer", across)
+    crossed = lax.ppermute(product, ("layer", "trace"), pairs)
     (coupled,) = call(
         inner_couple_kernel,
         (kept(2 * k, width),),

time: 44.3 us -> 42.7 us (0.964)
  starting transfers between devices: 22.4 us -> 20.6 us
  Pallas kernels: 14 us -> 14.8 us
  waiting for transfers between devices: 6.65 us -> 6.13 us
    ppermute x4, starting transfers between devices: 4.11 us -> 1.59 us  [wave(): arrived = [lax.ppermute(hop, 'layer', swap) for hop in hops]]
    ppermute x2, starting transfers between devices: 2.36 us -> 3.9 us  [the longest x1 2.08 us: wave(): packed = lax.ppermute(pack, ('layer', 'trace'), pairs)]
    ppermute x1, starting transfers between devices: 2.95 us -> 1.78 us  [wave(): before = lax.ppermute(before, 'layer', swap)]
    all_to_all x1, waiting for transfers between devices: 0.86 us -> 0.01 us  [wave(): gathered = lax.all_to_all(payload, 'trace', 0, 0)]
    pallas_call x10 -> x11, Pallas kernels: 14 us -> 14.8 us  [call(): pl.pallas_call(body, out_shape=tuple((pltpu.VMEM(*out) if keep else out f...]
    ppermute x1, waiting for transfers between devices: 0.01 us -> 0.48 us  [wave(): before = lax.ppermute(before, 'layer', swap)]
  transfers between devices with their start and end apart: 12 -> 12, of which waited for: 3 -> 3; matrix products, arithmetic and copies ran while one was open for 0% -> 0% of each run, Pallas kernels for 19% -> 21%
where the time goes in v3:
time: 42.7 us; the launch traced here: 42.3 us
  starting transfers between devices  20.6 us (48%)
  Pallas kernels  14.8 us (35%)
  waiting for transfers between devices  6.13 us (14%)
  between operations  0.76 us (2%)
    pallas_call x11, Pallas kernels, call(): pl.pallas_call(body, out_shape=tuple((pltpu.VMEM(*out) if keep else out f...  14.8 us
    all_to_all x1, starting transfers between devices, wave(): gathered = lax.all_to_all(payload, 'trace', 0, 0)  6.37 us
    all_to_all x1, waiting for transfers between devices, wave(): lax.all_to_all(payload, ('layer', 'trace'), 0, 0, axis_index_groups=groups)  3.73 us
    all_to_all x1, starting transfers between devices, wave(): lax.all_to_all(payload, ('layer', 'trace'), 0, 0, axis_index_groups=groups)  3.55 us
    ppermute x1, starting transfers between devices, wave(): packed = lax.ppermute(pack, ('layer', 'trace'), pairs)  2.08 us
    ppermute x1, starting transfers between devices, wave(): reached = lax.ppermute(coupled, 'layer', across)  2.01 us
    ppermute x1, waiting for transfers between devices, wave(): arrived = lax.ppermute(result, 'layer', swap)  1.9 us
    ppermute x1, starting transfers between devices, wave(): crossed = lax.ppermute(product, ('layer', 'trace'), pairs)  1.82 us
  transfers between devices with their start and end apart: 12, of which 3 were waited for; matrix products, arithmetic and copies ran while one was open for 0% of the time, Pallas kernels for 21%

profile of v3, /device:TPU:1, one launch (start us, length us, event | category | flops | bytes accessed | tf_op | source)
XLA Modules:
  0.0 42.3 jit_solution(8013765869826695630)
XLA Ops:
  0.6 1.6 %shard_map.86 = (bf16[8,2,32,256]{3,2,1,0:T(8,128)(2,1)}, bf16[96,1024]{1,0:T(8,128)(2,1)S(1)}, bf16[1024,256]{1,0:T(8,128)(2,1)S(1)}, bf16[32,1024]{1,0:T(8,128...) custom-call(bf16[1,1024,256]{2,1,0:T(8,128)(2,1)} %sup.3, bf16[1,1024,256]{2,1,0:T(8,128)(2,1)} %sdn.3, ...), custom_call_target="tpu_custom_call" | custom-call | flops 16777216 | bytes 1048576 | tf_op jit(solution)/shard_map/pallas_call | solution.py:57
  2.2 6.4 %all-to-all-start = ((bf16[8,2,32,256]{3,2,1,0:T(8,128)(2,1)}), bf16[8,2,32,256]{3,2,1,0:T(8,128)(2,1)S(1)}, u32[]{:S(2)}, u32[]{:S(2)}) async-start(bf16[8,2,32,256]{3,2,1,0:T(8,128)(2,1)} %get-tuple-element.22), calls=%async_computation | async-start | bytes 524288 | tf_op jit(solution)/shard_map/all_to_all | solution.py:485
  8.6 2.1 %collective-permute-start = (bf16[96,1024]{1,0:T(8,128)(2,1)S(1)}, bf16[96,1024]{1,0:T(8,128)(2,1)S(1)}, u32[]{:S(2)}, u32[]{:S(2)}) collective-permute-start(bf16[96,1024]{1,0:T(8,128)(2,1)S(1)} %get-tuple-element.26), channel_id=1, source_target_pairs={{8,16},{9,17},{10,18},{11,19},{12,20},{13,21},{14,22},{15,23},{16,... | collective-permute-start | bytes 589832 | tf_op jit(solution)/shard_map/ppermute | solution.py:488
  10.7 1.3 %collective-permute-start.1 = (bf16[32,1024]{1,0:T(8,128)(2,1)S(1)}, bf16[32,1024]{1,0:T(8,128)(2,1)S(1)}, u32[]{:S(2)}, u32[]{:S(2)}) collective-permute-start(bf16[32,1024]{1,0:T(8,128)(2,1)S(1)} %get-tuple-element.28.expn1), channel_id=1, source_target_pairs={{0,8},{8,0},{16,24},{24,16},{1,9},{9,1},{17,25},{25,17},{2,10},{10... | collective-permute-start | bytes 196616 | tf_op jit(solution)/shard_map/ppermute | solution.py:489
  12.0 2.2 %shard_map.87 = (bf16[256,256]{1,0:T(8,128)(2,1)S(1)}, bf16[256,256]{1,0:T(8,128)(2,1)S(1)}, bf16[256,256]{1,0:T(8,128)(2,1)S(1)}, bf16[256,256]{1,0:T(8,128)(2,1)S(1)}, bf16[2,1024,1024]{2,1,0:T(8,128)(2,1)S(1)}) custom-call(bf16[1,2,1024,1024]{3,2,1,0:T(8,128)(2,1)} %dup.7, bf16[1,2,1024,1024]{3,2,1,0:T(8,128)(2,1)} %ddn.7, ...), custom_call_target="tpu_custom_call" | custom-call | flops 1073741824 | bytes 4194304 | tf_op jit(solution)/shard_map/pallas_call | solution.py:57
  14.2 1.0 %collective-permute-start.3 = (bf16[256,256]{1,0:T(8,128)(2,1)S(1)}, bf16[256,256]{1,0:T(8,128)(2,1)S(1)}, u32[]{:S(2)}, u32[]{:S(2)}) collective-permute-start(bf16[256,256]{1,0:T(8,128)(2,1)S(1)} %get-tuple-element.30), channel_id=1, source_target_pairs={{0,8},{8,0},{16,24},{24,16},{1,9},{9,1},{17,25},{25,17},{2,10},{10... | collective-permute-start | bytes 393224 | tf_op jit(solution)/shard_map/ppermute | solution.py:499
  15.2 0.1 collective-permute-start.4
  15.3 0.4 %collective-permute-start.5 = (bf16[256,256]{1,0:T(8,128)(2,1)S(1)}, bf16[256,256]{1,0:T(8,128)(2,1)S(1)}, u32[]{:S(2)}, u32[]{:S(2)}) collective-permute-start(bf16[256,256]{1,0:T(8,128)(2,1)S(1)} %get-tuple-element.32), channel_id=1, source_target_pairs={{0,8},{8,0},{16,24},{24,16},{1,9},{9,1},{17,25},{25,17},{2,10},{10... | collective-permute-start | bytes 393224 | tf_op jit(solution)/shard_map/ppermute | solution.py:499
  15.7 0.0 collective-permute-done.1.before.refs_5_
  15.7 0.1 collective-permute-start.6
  15.8 0.0 collective-permute-done.packed
  15.8 1.1 %shard_map.88 = (bf16[96,1024]{1,0:T(8,128)(2,1)S(1)}, bf16[32,128]{1,0:T(8,128)(2,1)S(1)}) custom-call(bf16[2,1024,1024]{2,1,0:T(8,128)(2,1)S(1)} %get-tuple-element.25.block, bf16[96,1024]{1,0:T(8,128)(2,1)S(1)} %collective-permute-done.packed, bf16[32,1024]{1,0:T(8,128)(2,1)S(1)} %get-tuple-element.27.own, bf16[32,1024]{1,0:T(8,128)(2,1)S(1)} %get-tuple-element.28.expn1, ...), custom_call_target="tpu_custom_call" | custom-call | flops 1073741824 | bytes 4194304 | tf_op jit(solution)/shard_map/pallas_call | solution.py:57
  16.9 0.0 all-to-all-done.gathered
  17.0 1.8 %collective-permute-start.2 = (bf16[32,256]{1,0:T(8,128)(2,1)S(1)}, bf16[32,256]{1,0:T(8,128)(2,1)S(1)}, u32[]{:S(2)}, u32[]{:S(2)}) collective-permute-start(bf16[32,256]{1,0:T(8,128)(2,1)S(1)} %shard_map.89), channel_id=1, source_target_pairs={{0,8},{8,0},{16,24},{24,16},{1,9},{9,1},{17,25},{25,17},{2,10},{10... | collective-permute-start | bytes 49160 | tf_op jit(solution)/shard_map/ppermute | solution.py:512
  18.8 0.0 collective-permute-done.3.refs_0_
  18.8 0.0 collective-permute-done.4.refs_1_
  18.8 0.0 collective-permute-done.5.refs_2_
  18.8 0.0 collective-permute-done.6.refs_3_
  18.8 0.3 shard_map.90.sums
  19.1 0.5 %collective-permute-done.2.before.refs_4_ = bf16[32,256]{1,0:T(8,128)(2,1)S(1)} collective-permute-done((bf16[32,256]{1,0:T(8,128)(2,1)S(1)}, bf16[32,256]{1,0:T(8,128)(2,1)S(1)}, u32[]{:S(2)}, u32[]{:S(2)}) %collective-permute-start.2) | collective-permute-done | bytes 16416 | tf_op jit(solution)/shard_map/ppermute | solution.py:512
  19.6 0.9 %shard_map.91.payload = bf16[8,80,256]{2,1,0:T(8,128)(2,1)} custom-call(bf16[32,256]{1,0:T(8,128)(2,1)S(1)} %collective-permute-done.2.before.refs_4_, f32[64,256]{1,0:T(8,128)S(1)} %shard_map.90.sums, bf16[32,128]{1,0:T(8,128)(2,1)S(1)} %get-tuple-element.29.mixed, bf16[96,1024]{1,0:T(8,128)(2,1)S(1)} %collective-permute-done.packed), custom_call_target="tpu_custom_call" | custom-call | flops 16777216 | bytes 1048576 | tf_op jit(solution)/shard_map/pallas_call | solution.py:57
  20.5 3.5 %all-to-all-start.1 = ((bf16[8,80,256]{2,1,0:T(8,128)(2,1)}), bf16[8,80,256]{2,1,0:T(8,128)(2,1)S(1)}, u32[]{:S(2)}, u32[]{:S(2)}) async-start(bf16[8,80,256]{2,1,0:T(8,128)(2,1)} %shard_map.91.payload), calls=%async_computation.1 | async-start | bytes 655360 | tf_op jit(solution)/shard_map/all_to_all | solution.py:534
  24.1 3.0 %shard_map.92 = (bf16[1024,256]{1,0:T(8,128)(2,1)S(1)}, bf16[1024,256]{1,0:T(8,128)(2,1)S(1)}) custom-call(bf16[1,2,1024,1024]{3,2,1,0:T(8,128)(2,1)} %dup.7, bf16[1,2,1024,1024]{3,2,1,0:T(8,128)(2,1)} %ddn.7, bf16[8,80,256]{2,1,0:T(8,128)(2,1)} %shard_map.91.payload, bf16[256,256]{1,0:T(8,128)(2,1)S(1)} %collective-permute-done.3.refs_0_, ...), custom_call_target="tpu_custom_call" | custom-call | flops 1073741824 | bytes 4194304 | tf_op jit(solution)/shard_map/pallas_call | solution.py:57
  27.1 1.8 %collective-permute-start.7 = (bf16[1024,256]{1,0:T(8,128)(2,1)S(1)}, bf16[1024,256]{1,0:T(8,128)(2,1)S(1)}, u32[]{:S(2)}, u32[]{:S(2)}) collective-permute-start(bf16[1024,256]{1,0:T(8,128)(2,1)S(1)} %get-tuple-element.35), channel_id=1, source_target_pairs={{8,16},{9,17},{10,18},{11,19},{12,20},{13,21},{14,22},{15,23},{16,... | collective-permute-start | bytes 1572872 | tf_op jit(solution)/shard_map/ppermute | solution.py:544
  28.9 3.7 %all-to-all-done.1.second = bf16[8,80,256]{2,1,0:T(8,128)(2,1)S(1)} async-done(((bf16[8,80,256]{2,1,0:T(8,128)(2,1)}), bf16[8,80,256]{2,1,0:T(8,128)(2,1)S(1)}, u32[]{:S(2)}, u32[]{:S(2)}) %all-to-all-start.1) | async-done | bytes 327712 | tf_op jit(solution)/shard_map/all_to_all | solution.py:534
  32.6 0.6 %shard_map.93.coupled = bf16[64,256]{1,0:T(8,128)(2,1)S(1)} custom-call(bf16[8,2,32,256]{3,2,1,0:T(8,128)(2,1)S(1)} %all-to-all-done.gathered, bf16[8,80,256]{2,1,0:T(8,128)(2,1)S(1)} %all-to-all-done.1.second, bf16[96,1024]{1,0:T(8,128)(2,1)S(1)} %collective-permute-done.packed, bf16[2,32,256]{2,1,0:T(8,128)(2,1)S(1)} %get-tuple-element.23.couple1), custom_call_target="tpu_custom_call" | custom-call | flops 16777216 | bytes 1048576 | tf_op jit(solution)/shard_map/pallas_call | solution.py:57
  33.2 2.0 %collective-permute-start.8 = (bf16[64,256]{1,0:T(8,128)(2,1)S(1)}, bf16[64,256]{1,0:T(8,128)(2,1)S(1)}, u32[]{:S(2)}, u32[]{:S(2)}) collective-permute-start(bf16[64,256]{1,0:T(8,128)(2,1)S(1)} %shard_map.93.coupled), channel_id=1, source_target_pairs={{0,24},{8,16},{16,8},{24,0},{1,25},{9,17},{17,9},{25,1},{2,26},{10... | collective-permute-start | bytes 98312 | tf_op jit(solution)/shard_map/ppermute | solution.py:554
  35.2 1.8 %shard_map.94 = (bf16[2,512,1024]{2,1,0:T(8,128)(2,1)S(1)}, bf16[64,1024]{1,0:T(8,128)(2,1)S(1)}, bf16[1024,256]{1,0:T(8,128)(2,1)S(1)}) custom-call(bf16[1,1024,256]{2,1,0:T(8,128)(2,1)} %sup.3, bf16[1,1024,256]{2,1,0:T(8,128)(2,1)} %sdn.3, bf16[1,2,32,1024]{3,2,1,0:T(8,128)(2,1)} %expn.3, bf16[1,2,1024,1024]{3,2,1,0:T(8,128)(2,1)} %dup.7, ...), custom_call_target="tpu_custom_call" | custom-call | flops 1073741824 | bytes 4194304 | tf_op jit(solution)/shard_map/pallas_call | solution.py:57
  37.0 0.0 collective-permute-done.7.crossed
  37.0 0.0 collective-permute-done.8.coupled
  37.0 2.3 %shard_map.95 = (bf16[1024,256]{1,0:T(8,128)(2,1)S(1)}, bf16[1024,256]{1,0:T(8,128)(2,1)S(1)}) custom-call(bf16[1,2,1024,1024]{3,2,1,0:T(8,128)(2,1)} %dup.7, bf16[1,2,1024,1024]{3,2,1,0:T(8,128)(2,1)} %ddn.7, bf16[1024,256]{1,0:T(8,128)(2,1)S(1)} %collective-permute-done.7.crossed, bf16[64,256]{1,0:T(8,128)(2,1)S(1)} %collective-permute-done.8.coupled, ...), custom_call_target="tpu_custom_call" | custom-call | flops 1073741824 | bytes 4194304 | tf_op jit(solution)/shard_map/pallas_call | solution.py:57
  39.3 0.1 collective-permute-start.9
  39.4 1.9 %collective-permute-done.9.arrived = bf16[1024,256]{1,0:T(8,128)(2,1)S(1)} collective-permute-done((bf16[1024,256]{1,0:T(8,128)(2,1)S(1)}, bf16[1024,256]{1,0:T(8,128)(2,1)S(1)}, u32[]{:S(2)}, u32[]{:S(2)}) %collective-permute-start.9) | collective-permute-done | bytes 524320 | tf_op jit(solution)/shard_map/ppermute | solution.py:573
  41.3 1.0 %shard_map.96 = (bf16[1,1024,256]{2,1,0:T(8,128)(2,1)}, bf16[1,1024,256]{2,1,0:T(8,128)(2,1)}) custom-call(bf16[1024,256]{1,0:T(8,128)(2,1)S(1)} %collective-permute-done.9.arrived, bf16[1024,256]{1,0:T(8,128)(2,1)S(1)} %get-tuple-element.40.one, bf16[1024,256]{1,0:T(8,128)(2,1)S(1)} %get-tuple-element.41.two, ...), custom_call_target="tpu_custom_call" | custom-call | flops 16777216 | bytes 1048576 | tf_op jit(solution)/shard_map/pallas_call | solution.py:57
  (1 shorter events, 0.0 us)
Async XLA Ops:
  2.2 14.7 %all-to-all-start = ((bf16[8,2,32,256]{3,2,1,0:T(8,128)(2,1)}), bf16[8,2,32,256]{3,2,1,0:T(8,128)(2,1)S(1)}, u32[]{:S(2)}, u32[]{:S(2)}) async-start(bf16[8,2,32,256]{3,2,1,0:T(8,128)(2,1)} %get-tuple-element.22), calls=%async_computation | async-start | bytes 524288 | tf_op jit(solution)/shard_map/all_to_all | solution.py:485
  8.6 7.2 %collective-permute-start = (bf16[96,1024]{1,0:T(8,128)(2,1)S(1)}, bf16[96,1024]{1,0:T(8,128)(2,1)S(1)}, u32[]{:S(2)}, u32[]{:S(2)}) collective-permute-start(bf16[96,1024]{1,0:T(8,128)(2,1)S(1)} %get-tuple-element.26), channel_id=1, source_target_pairs={{8,16},{9,17},{10,18},{11,19},{12,20},{13,21},{14,22},{15,23},{16,... | collective-permute-start | bytes 589832 | tf_op jit(solution)/shard_map/ppermute | solution.py:488
  10.7 5.0 %collective-permute-start.1 = (bf16[32,1024]{1,0:T(8,128)(2,1)S(1)}, bf16[32,1024]{1,0:T(8,128)(2,1)S(1)}, u32[]{:S(2)}, u32[]{:S(2)}) collective-permute-start(bf16[32,1024]{1,0:T(8,128)(2,1)S(1)} %get-tuple-element.28.expn1), channel_id=1, source_target_pairs={{0,8},{8,0},{16,24},{24,16},{1,9},{9,1},{17,25},{25,17},{2,10},{10... | collective-permute-start | bytes 196616 | tf_op jit(solution)/shard_map/ppermute | solution.py:489
  14.2 4.5 %collective-permute-start.3 = (bf16[256,256]{1,0:T(8,128)(2,1)S(1)}, bf16[256,256]{1,0:T(8,128)(2,1)S(1)}, u32[]{:S(2)}, u32[]{:S(2)}) collective-permute-start(bf16[256,256]{1,0:T(8,128)(2,1)S(1)} %get-tuple-element.30), channel_id=1, source_target_pairs={{0,8},{8,0},{16,24},{24,16},{1,9},{9,1},{17,25},{25,17},{2,10},{10... | collective-permute-start | bytes 393224 | tf_op jit(solution)/shard_map/ppermute | solution.py:499
  15.2 3.5 %collective-permute-start.4 = (bf16[256,256]{1,0:T(8,128)(2,1)S(1)}, bf16[256,256]{1,0:T(8,128)(2,1)S(1)}, u32[]{:S(2)}, u32[]{:S(2)}) collective-permute-start(bf16[256,256]{1,0:T(8,128)(2,1)S(1)} %get-tuple-element.31), channel_id=1, source_target_pairs={{0,8},{8,0},{16,24},{24,16},{1,9},{9,1},{17,25},{25,17},{2,10},{10... | collective-permute-start | bytes 393224 | tf_op jit(solution)/shard_map/ppermute | solution.py:499
  15.3 3.5 %collective-permute-start.5 = (bf16[256,256]{1,0:T(8,128)(2,1)S(1)}, bf16[256,256]{1,0:T(8,128)(2,1)S(1)}, u32[]{:S(2)}, u32[]{:S(2)}) collective-permute-start(bf16[256,256]{1,0:T(8,128)(2,1)S(1)} %get-tuple-element.32), channel_id=1, source_target_pairs={{0,8},{8,0},{16,24},{24,16},{1,9},{9,1},{17,25},{25,17},{2,10},{10... | collective-permute-start | bytes 393224 | tf_op jit(solution)/shard_map/ppermute | solution.py:499
  15.7 3.0 %collective-permute-start.6 = (bf16[256,256]{1,0:T(8,128)(2,1)S(1)}, bf16[256,256]{1,0:T(8,128)(2,1)S(1)}, u32[]{:S(2)}, u32[]{:S(2)}) collective-permute-start(bf16[256,256]{1,0:T(8,128)(2,1)S(1)} %get-tuple-element.33), channel_id=1, source_target_pairs={{0,8},{8,0},{16,24},{24,16},{1,9},{9,1},{17,25},{25,17},{2,10},{10... | collective-permute-start | bytes 393224 | tf_op jit(solution)/shard_map/ppermute | solution.py:499
  17.0 2.6 %collective-permute-start.2 = (bf16[32,256]{1,0:T(8,128)(2,1)S(1)}, bf16[32,256]{1,0:T(8,128)(2,1)S(1)}, u32[]{:S(2)}, u32[]{:S(2)}) collective-permute-start(bf16[32,256]{1,0:T(8,128)(2,1)S(1)} %shard_map.89), channel_id=1, source_target_pairs={{0,8},{8,0},{16,24},{24,16},{1,9},{9,1},{17,25},{25,17},{2,10},{10... | collective-permute-start | bytes 49160 | tf_op jit(solution)/shard_map/ppermute | solution.py:512
  20.5 12.1 %all-to-all-start.1 = ((bf16[8,80,256]{2,1,0:T(8,128)(2,1)}), bf16[8,80,256]{2,1,0:T(8,128)(2,1)S(1)}, u32[]{:S(2)}, u32[]{:S(2)}) async-start(bf16[8,80,256]{2,1,0:T(8,128)(2,1)} %shard_map.91.payload), calls=%async_computation.1 | async-start | bytes 655360 | tf_op jit(solution)/shard_map/all_to_all | solution.py:534
  27.1 9.9 %collective-permute-start.7 = (bf16[1024,256]{1,0:T(8,128)(2,1)S(1)}, bf16[1024,256]{1,0:T(8,128)(2,1)S(1)}, u32[]{:S(2)}, u32[]{:S(2)}) collective-permute-start(bf16[1024,256]{1,0:T(8,128)(2,1)S(1)} %get-tuple-element.35), channel_id=1, source_target_pairs={{8,16},{9,17},{10,18},{11,19},{12,20},{13,21},{14,22},{15,23},{16,... | collective-permute-start | bytes 1572872 | tf_op jit(solution)/shard_map/ppermute | solution.py:544
  33.2 3.8 %collective-permute-start.8 = (bf16[64,256]{1,0:T(8,128)(2,1)S(1)}, bf16[64,256]{1,0:T(8,128)(2,1)S(1)}, u32[]{:S(2)}, u32[]{:S(2)}) collective-permute-start(bf16[64,256]{1,0:T(8,128)(2,1)S(1)} %shard_map.93.coupled), channel_id=1, source_target_pairs={{0,24},{8,16},{16,8},{24,0},{1,25},{9,17},{17,9},{25,1},{2,26},{10... | collective-permute-start | bytes 98312 | tf_op jit(solution)/shard_map/ppermute | solution.py:554
  39.3 2.0 %collective-permute-start.9 = (bf16[1024,256]{1,0:T(8,128)(2,1)S(1)}, bf16[1024,256]{1,0:T(8,128)(2,1)S(1)}, u32[]{:S(2)}, u32[]{:S(2)}) collective-permute-start(bf16[1024,256]{1,0:T(8,128)(2,1)S(1)} %get-tuple-element.39), channel_id=1, source_target_pairs={{0,8},{8,0},{16,24},{24,16},{1,9},{9,1},{17,25},{25,17},{2,10},{10... | collective-permute-start | bytes 1572872 | tf_op jit(solution)/shard_map/ppermute | solution.py:573

commit v4 on v3

--- a/solution.py
+++ b/solution.py
@@ -277,11 +277,12 @@
         arrive(payload, sems.at[0])
 
 
-def inner_apply_kernel(dup, ddn, payload, *refs):
+def inner_apply_kernel(sup, sdn, dup, ddn, payload, *refs):
     del payload
     arrived, refs = refs[:CHUNKS], refs[CHUNKS:]
-    before, other, source1, product, trace, block, turned, sems = refs
+    before, other, source1, product, trace, source2, block, turned, sems = refs
     outer, first = roles()
+    pick(1 - first, sup.at[0], sdn.at[0], source2, sems.at[CHUNKS])
 
     @pl.when(jnp.logical_not(outer))
     def _():
@@ -301,6 +302,8 @@
             product[rows, :] = block_rows(block, rows, trace, turned).astype(BF16)
 
         each_chunk(points, one)
+
+    arrive(source2, sems.at[CHUNKS])
 
 
 def inner_couple_kernel(gathered, second, packed, couple1, out, inner, later, sems):
@@ -350,11 +353,10 @@
 
 
 def settle_kernel(
-    sup, sdn, expn, dup, ddn, coupled, packed, lower, bases, source2, sems
+    expn, dup, ddn, coupled, packed, lower, bases, sems
 ):
     del coupled
     outer, first = roles()
-    pick(1 - first, sup.at[0], sdn.at[0], source2, sems.at[0])
 
     @pl.when(jnp.logical_not(outer))
     def _():
@@ -368,12 +370,10 @@
             lower, step, lambda c, rows: arrive(lower.at[:, rows, :], sems.at[2 + c])
         )
 
-    arrive(source2, sems.at[0])
-
 
 def inner_second_kernel(
     dup, ddn, crossed, coupled, source2, lower, bases,
-    out, trace, turned, upper, sems,
+    out, trace, turned, rest, tail, added2, upper, sems,
 ):
     outer, first = roles()
 
@@ -382,6 +382,7 @@
         k, points = coupled.shape[0] // 2, bases.shape[1]
         step = points // CHUNKS
         load_part(CHUNKS // 2, 1 - first, dup, ddn, upper, step, sems, 0)
+        load_part(CHUNKS - 1, 1 - first, dup, ddn, rest, step, sems, CHUNKS)
 
         added = expand(bases[:k, :], coupled[:k, :])
         for c in range(CHUNKS):
@@ -390,11 +391,12 @@
             value = (value + added[rows, :]).astype(BF16)
             trace[rows, :] = value
             turned[rows, :] = rotate(value)
-        out[...] = expand(bases[k:, :], coupled[k:, :]).astype(BF16)
+        added2[...] = expand(bases[k:, :], coupled[k:, :]).astype(BF16)
+        tail[...] = added2[points - step :, :]
 
         def put(block, rows, base):
             place = pl.ds(pl.multiple_of(rows.start + base, step), step)
-            value = block_rows(block, rows, trace, turned) + out[place, :].astype(F32)
+            value = block_rows(block, rows, trace, turned) + added2[place, :].astype(F32)
             out[place, :] = value.astype(BF16)
 
         each_chunk_of(lower, step, lambda c, rows: put(lower, rows, 0))
@@ -404,9 +406,20 @@
             put(upper, rows, points // 2)
 
         each_chunk_of(upper, step, second)
-
-
-def last_kernel(arrived, one, two, source1, source2, up, down, sums, sems):
+        arrive(rest, sems.at[CHUNKS])
+
+
+def inner_rest_kernel(rest, trace, turned, tail, out, sems):
+    del sems
+    outer, _ = roles()
+
+    @pl.when(jnp.logical_not(outer))
+    def _():
+        value = dot(rest[0], trace[...]) + dot(rest[1], turned[...])
+        out[...] = (value + tail[...].astype(F32)).astype(BF16)
+
+
+def last_kernel(most, last, one, two, source1, source2, up, down, sums, sems):
     outer, first = roles()
 
     def put(which, source, sem):
@@ -431,12 +444,11 @@
     def _():
         put(first, source1, sems.at[0])
 
-        def add(c, rows):
-            value = source2[rows, :].astype(F32) + arrived[rows, :].astype(F32)
+        cut = most.shape[0]
+        for part, rows in ((most, pl.ds(0, cut)), (last, pl.ds(cut, sums.shape[0] - cut))):
+            value = source2[rows, :].astype(F32) + part[...].astype(F32)
             sums[rows, :] = value.astype(BF16)
             put_rows(1 - first, rows, sems.at[1])
-
-        each_chunk(sums.shape[0], add)
 
     @pl.when(jnp.logical_not(outer))
     def _():
@@ -532,13 +544,13 @@
     ends = [[g * owners + p * half + o for g in (0, layers - 1) for o in range(half)] for p in range(2)]
     groups = [[g * owners + o for o in range(owners)] for g in range(1, layers - 1)] + ends
     second = lax.all_to_all(payload, ("layer", "trace"), 0, 0, axis_index_groups=groups)
-    product, one = call(
+    product, one, source2 = call(
         inner_apply_kernel,
-        (kept(*field), kept(*field)),
-        (*diagonals, payload),
+        (kept(*field), kept(*field), kept(*field)),
+        (source_up, source_down, *diagonals, payload),
         (*arrived, before, other, source1),
         [block, field],
-        CHUNKS,
+        CHUNKS + 1,
         **large,
     )
     crossed = lax.ppermute(product, ("layer", "trace"), pairs)
@@ -552,30 +564,37 @@
         **small,
     )
     reached = lax.ppermute(coupled, "layer", across)
-    lower, bases, source2 = call(
+    lower, bases = call(
         settle_kernel,
-        (kept(2, points // 2, points), kept(2 * k, points), kept(*field)),
-        (source_up, source_down, expansion, *diagonals),
+        (kept(2, points // 2, points), kept(2 * k, points)),
+        (expansion, *diagonals),
         (coupled, packed),
         [],
         2 + CHUNKS // 2,
         **large,
     )
-    result, two = call(
+    step = points // CHUNKS
+    most, two, turned, rest, tail = call(
         inner_second_kernel,
-        (kept(*field), kept(*field)),
+        (
+            *(kept(points - step, width), kept(*field), kept(*field)),
+            *(kept(2, step, points), kept(step, width)),
+        ),
         diagonals,
         (crossed, reached, source2, lower, bases),
-        [field, (2, points // 2, points)],
-        CHUNKS // 2,
+        [field, (2, points // 2 - step, points)],
+        CHUNKS + 1,
         **large,
     )
-    arrived = lax.ppermute(result, "layer", swap)
+    (last,) = call(
+        inner_rest_kernel, (kept(step, width),), (), (rest, two, turned, tail), [], 1, **small
+    )
+    arrived = [lax.ppermute(part, "layer", swap) for part in (most, last)]
     return call(
         last_kernel,
         (like(1, *field), like(1, *field)),
         (),
-        (arrived, one, two, source1, source2),
+        (*arrived, one, two, source1, source2),
         [field],
         2,
         **small,

time: 42.7 us -> 42.2 us (0.988)
  waiting for transfers between devices: 6.13 us -> 5.38 us
    ppermute x1 -> x2, waiting for transfers between devices: 1.9 us -> 1.32 us  [wave(): arrived = [lax.ppermute(part, 'layer', swap) for part in (most, last)]]
    pallas_call x11 -> x12, Pallas kernels: 14.8 us -> 14.9 us  [call(): pl.pallas_call(body, out_shape=tuple((pltpu.VMEM(*out) if keep else out f...]
  transfers between devices with their start and end apart: 12 -> 13, of which waited for: 3 -> 3; matrix products, arithmetic and copies ran while one was open for 0% -> 0% of each run, Pallas kernels for 21% -> 23%
where the time goes in v4:
time: 42.2 us; the launch traced here: 41.7 us
  starting transfers between devices  20.7 us (49%)
  Pallas kernels  14.9 us (35%)
  waiting for transfers between devices  5.38 us (13%)
  between operations  0.77 us (2%)
    pallas_call x12, Pallas kernels, call(): pl.pallas_call(body, out_shape=tuple((pltpu.VMEM(*out) if keep else out f...  14.9 us
    all_to_all x1, starting transfers between devices, wave(): gathered = lax.all_to_all(payload, 'trace', 0, 0)  6.37 us
    all_to_all x1, waiting for transfers between devices, wave(): lax.all_to_all(payload, ('layer', 'trace'), 0, 0, axis_index_groups=groups)  3.55 us
    all_to_all x1, starting transfers between devices, wave(): lax.all_to_all(payload, ('layer', 'trace'), 0, 0, axis_index_groups=groups)  3.55 us
    ppermute x1, starting transfers between devices, wave(): packed = lax.ppermute(pack, ('layer', 'trace'), pairs)  2.08 us
    ppermute x1, starting transfers between devices, wave(): reached = lax.ppermute(coupled, 'layer', across)  2.01 us
    ppermute x1, starting transfers between devices, wave(): crossed = lax.ppermute(product, ('layer', 'trace'), pairs)  1.82 us
    ppermute x1, starting transfers between devices, wave(): before = lax.ppermute(before, 'layer', swap)  1.78 us
  transfers between devices with their start and end apart: 13, of which 3 were waited for; matrix products, arithmetic and copies ran while one was open for 0% of the time, Pallas kernels for 23%

profile of v4, /device:TPU:1, one launch (start us, length us, event | category | flops | bytes accessed | tf_op | source)
XLA Modules:
  0.0 41.7 jit_solution(11411612387526990146)
XLA Ops:
  0.6 1.6 %shard_map.86 = (bf16[8,2,32,256]{3,2,1,0:T(8,128)(2,1)}, bf16[96,1024]{1,0:T(8,128)(2,1)S(1)}, bf16[1024,256]{1,0:T(8,128)(2,1)S(1)}, bf16[32,1024]{1,0:T(8,128...) custom-call(bf16[1,1024,256]{2,1,0:T(8,128)(2,1)} %sup.3, bf16[1,1024,256]{2,1,0:T(8,128)(2,1)} %sdn.3, ...), custom_call_target="tpu_custom_call" | custom-call | flops 16777216 | bytes 1048576 | tf_op jit(solution)/shard_map/pallas_call | solution.py:57
  2.2 6.4 %all-to-all-start = ((bf16[8,2,32,256]{3,2,1,0:T(8,128)(2,1)}), bf16[8,2,32,256]{3,2,1,0:T(8,128)(2,1)S(1)}, u32[]{:S(2)}, u32[]{:S(2)}) async-start(bf16[8,2,32,256]{3,2,1,0:T(8,128)(2,1)} %get-tuple-element.25), calls=%async_computation | async-start | bytes 524288 | tf_op jit(solution)/shard_map/all_to_all | solution.py:497
  8.6 2.1 %collective-permute-start = (bf16[96,1024]{1,0:T(8,128)(2,1)S(1)}, bf16[96,1024]{1,0:T(8,128)(2,1)S(1)}, u32[]{:S(2)}, u32[]{:S(2)}) collective-permute-start(bf16[96,1024]{1,0:T(8,128)(2,1)S(1)} %get-tuple-element.29), channel_id=1, source_target_pairs={{8,16},{9,17},{10,18},{11,19},{12,20},{13,21},{14,22},{15,23},{16,... | collective-permute-start | bytes 589832 | tf_op jit(solution)/shard_map/ppermute | solution.py:500
  10.7 1.3 %collective-permute-start.1 = (bf16[32,1024]{1,0:T(8,128)(2,1)S(1)}, bf16[32,1024]{1,0:T(8,128)(2,1)S(1)}, u32[]{:S(2)}, u32[]{:S(2)}) collective-permute-start(bf16[32,1024]{1,0:T(8,128)(2,1)S(1)} %get-tuple-element.31.expn1), channel_id=1, source_target_pairs={{0,8},{8,0},{16,24},{24,16},{1,9},{9,1},{17,25},{25,17},{2,10},{10... | collective-permute-start | bytes 196616 | tf_op jit(solution)/shard_map/ppermute | solution.py:501
  12.0 2.2 %shard_map.87 = (bf16[256,256]{1,0:T(8,128)(2,1)S(1)}, bf16[256,256]{1,0:T(8,128)(2,1)S(1)}, bf16[256,256]{1,0:T(8,128)(2,1)S(1)}, bf16[256,256]{1,0:T(8,128)(2,1)S(1)}, bf16[2,1024,1024]{2,1,0:T(8,128)(2,1)S(1)}) custom-call(bf16[1,2,1024,1024]{3,2,1,0:T(8,128)(2,1)} %dup.7, bf16[1,2,1024,1024]{3,2,1,0:T(8,128)(2,1)} %ddn.7, ...), custom_call_target="tpu_custom_call" | custom-call | flops 1073741824 | bytes 4194304 | tf_op jit(solution)/shard_map/pallas_call | solution.py:57
  14.2 1.0 %collective-permute-start.3 = (bf16[256,256]{1,0:T(8,128)(2,1)S(1)}, bf16[256,256]{1,0:T(8,128)(2,1)S(1)}, u32[]{:S(2)}, u32[]{:S(2)}) collective-permute-start(bf16[256,256]{1,0:T(8,128)(2,1)S(1)} %get-tuple-element.33), channel_id=1, source_target_pairs={{0,8},{8,0},{16,24},{24,16},{1,9},{9,1},{17,25},{25,17},{2,10},{10... | collective-permute-start | bytes 393224 | tf_op jit(solution)/shard_map/ppermute | solution.py:511
  15.2 0.1 collective-permute-start.4
  15.3 0.4 %collective-permute-start.5 = (bf16[256,256]{1,0:T(8,128)(2,1)S(1)}, bf16[256,256]{1,0:T(8,128)(2,1)S(1)}, u32[]{:S(2)}, u32[]{:S(2)}) collective-permute-start(bf16[256,256]{1,0:T(8,128)(2,1)S(1)} %get-tuple-element.35), channel_id=1, source_target_pairs={{0,8},{8,0},{16,24},{24,16},{1,9},{9,1},{17,25},{25,17},{2,10},{10... | collective-permute-start | bytes 393224 | tf_op jit(solution)/shard_map/ppermute | solution.py:511
  15.7 0.0 collective-permute-done.1.before.refs_5_
  15.7 0.1 collective-permute-start.6
  15.8 0.0 collective-permute-done.packed
  15.8 1.1 %shard_map.88 = (bf16[96,1024]{1,0:T(8,128)(2,1)S(1)}, bf16[32,128]{1,0:T(8,128)(2,1)S(1)}) custom-call(bf16[2,1024,1024]{2,1,0:T(8,128)(2,1)S(1)} %get-tuple-element.28.block, bf16[96,1024]{1,0:T(8,128)(2,1)S(1)} %collective-permute-done.packed, bf16[32,1024]{1,0:T(8,128)(2,1)S(1)} %get-tuple-element.30.own, bf16[32,1024]{1,0:T(8,128)(2,1)S(1)} %get-tuple-element.31.expn1, ...), custom_call_target="tpu_custom_call" | custom-call | flops 1073741824 | bytes 4194304 | tf_op jit(solution)/shard_map/pallas_call | solution.py:57
  16.9 0.0 all-to-all-done.gathered
  17.0 1.8 %collective-permute-start.2 = (bf16[32,256]{1,0:T(8,128)(2,1)S(1)}, bf16[32,256]{1,0:T(8,128)(2,1)S(1)}, u32[]{:S(2)}, u32[]{:S(2)}) collective-permute-start(bf16[32,256]{1,0:T(8,128)(2,1)S(1)} %shard_map.89), channel_id=1, source_target_pairs={{0,8},{8,0},{16,24},{24,16},{1,9},{9,1},{17,25},{25,17},{2,10},{10... | collective-permute-start | bytes 49160 | tf_op jit(solution)/shard_map/ppermute | solution.py:524
  18.8 0.0 collective-permute-done.3.refs_0_
  18.8 0.0 collective-permute-done.4.refs_1_
  18.8 0.0 collective-permute-done.5.refs_2_
  18.8 0.0 collective-permute-done.6.refs_3_
  18.8 0.3 shard_map.90.sums
  19.1 0.5 %collective-permute-done.2.before.refs_4_ = bf16[32,256]{1,0:T(8,128)(2,1)S(1)} collective-permute-done((bf16[32,256]{1,0:T(8,128)(2,1)S(1)}, bf16[32,256]{1,0:T(8,128)(2,1)S(1)}, u32[]{:S(2)}, u32[]{:S(2)}) %collective-permute-start.2) | collective-permute-done | bytes 16416 | tf_op jit(solution)/shard_map/ppermute | solution.py:524
  19.6 0.9 %shard_map.91.payload = bf16[8,80,256]{2,1,0:T(8,128)(2,1)} custom-call(bf16[32,256]{1,0:T(8,128)(2,1)S(1)} %collective-permute-done.2.before.refs_4_, f32[64,256]{1,0:T(8,128)S(1)} %shard_map.90.sums, bf16[32,128]{1,0:T(8,128)(2,1)S(1)} %get-tuple-element.32.mixed, bf16[96,1024]{1,0:T(8,128)(2,1)S(1)} %collective-permute-done.packed), custom_call_target="tpu_custom_call" | custom-call | flops 16777216 | bytes 1048576 | tf_op jit(solution)/shard_map/pallas_call | solution.py:57
  20.5 3.5 %all-to-all-start.1 = ((bf16[8,80,256]{2,1,0:T(8,128)(2,1)}), bf16[8,80,256]{2,1,0:T(8,128)(2,1)S(1)}, u32[]{:S(2)}, u32[]{:S(2)}) async-start(bf16[8,80,256]{2,1,0:T(8,128)(2,1)} %shard_map.91.payload), calls=%async_computation.1 | async-start | bytes 655360 | tf_op jit(solution)/shard_map/all_to_all | solution.py:546
  24.1 3.2 %shard_map.92 = (bf16[1024,256]{1,0:T(8,128)(2,1)S(1)}, bf16[1024,256]{1,0:T(8,128)(2,1)S(1)}, bf16[1024,256]{1,0:T(8,128)(2,1)S(1)}) custom-call(bf16[1,1024,256]{2,1,0:T(8,128)(2,1)} %sup.3, bf16[1,1024,256]{2,1,0:T(8,128)(2,1)} %sdn.3, bf16[1,2,1024,1024]{3,2,1,0:T(8,128)(2,1)} %dup.7, bf16[1,2,1024,1024]{3,2,1,0:T(8,128)(2,1)} %ddn.7, ...), custom_call_target="tpu_custom_call" | custom-call | flops 1073741824 | bytes 4194304 | tf_op jit(solution)/shard_map/pallas_call | solution.py:57
  27.3 1.8 %collective-permute-start.7 = (bf16[1024,256]{1,0:T(8,128)(2,1)S(1)}, bf16[1024,256]{1,0:T(8,128)(2,1)S(1)}, u32[]{:S(2)}, u32[]{:S(2)}) collective-permute-start(bf16[1024,256]{1,0:T(8,128)(2,1)S(1)} %get-tuple-element.38), channel_id=1, source_target_pairs={{8,16},{9,17},{10,18},{11,19},{12,20},{13,21},{14,22},{15,23},{16,... | collective-permute-start | bytes 1572872 | tf_op jit(solution)/shard_map/ppermute | solution.py:556
  29.1 3.6 %all-to-all-done.1.second = bf16[8,80,256]{2,1,0:T(8,128)(2,1)S(1)} async-done(((bf16[8,80,256]{2,1,0:T(8,128)(2,1)}), bf16[8,80,256]{2,1,0:T(8,128)(2,1)S(1)}, u32[]{:S(2)}, u32[]{:S(2)}) %all-to-all-start.1) | async-done | bytes 327712 | tf_op jit(solution)/shard_map/all_to_all | solution.py:546
  32.6 0.6 %shard_map.93.coupled = bf16[64,256]{1,0:T(8,128)(2,1)S(1)} custom-call(bf16[8,2,32,256]{3,2,1,0:T(8,128)(2,1)S(1)} %all-to-all-done.gathered, bf16[8,80,256]{2,1,0:T(8,128)(2,1)S(1)} %all-to-all-done.1.second, bf16[96,1024]{1,0:T(8,128)(2,1)S(1)} %collective-permute-done.packed, bf16[2,32,256]{2,1,0:T(8,128)(2,1)S(1)} %get-tuple-element.26.couple1), custom_call_target="tpu_custom_call" | custom-call | flops 16777216 | bytes 1048576 | tf_op jit(solution)/shard_map/pallas_call | solution.py:57
  33.2 2.0 %collective-permute-start.8 = (bf16[64,256]{1,0:T(8,128)(2,1)S(1)}, bf16[64,256]{1,0:T(8,128)(2,1)S(1)}, u32[]{:S(2)}, u32[]{:S(2)}) collective-permute-start(bf16[64,256]{1,0:T(8,128)(2,1)S(1)} %shard_map.93.coupled), channel_id=1, source_target_pairs={{0,24},{8,16},{16,8},{24,0},{1,25},{9,17},{17,9},{25,1},{2,26},{10... | collective-permute-start | bytes 98312 | tf_op jit(solution)/shard_map/ppermute | solution.py:566
  35.2 1.6 %shard_map.94 = (bf16[2,512,1024]{2,1,0:T(8,128)(2,1)S(1)}, bf16[64,1024]{1,0:T(8,128)(2,1)S(1)}) custom-call(bf16[1,2,32,1024]{3,2,1,0:T(8,128)(2,1)} %expn.3, bf16[1,2,1024,1024]{3,2,1,0:T(8,128)(2,1)} %dup.7, bf16[1,2,1024,1024]{3,2,1,0:T(8,128)(2,1)} %ddn.7, bf16[64,256]{1,0:T(8,128)(2,1)S(1)} %shard_map.93.coupled, ...), custom_call_target="tpu_custom_call" | custom-call | flops 1073741824 | bytes 4194304 | tf_op jit(solution)/shard_map/pallas_call | solution.py:57
  36.8 0.0 collective-permute-done.7.crossed
  36.9 0.0 collective-permute-done.8.coupled
  36.9 1.9 %shard_map.95 = (bf16[768,256]{1,0:T(8,128)(2,1)S(1)}, bf16[1024,256]{1,0:T(8,128)(2,1)S(1)}, bf16[1024,256]{1,0:T(8,128)(2,1)S(1)}, bf16[2,256,1024]{2,1,0:T(8,128)(2,1)S(1)}, bf16[256,256]{1,0:T(8,128)(2,1)S(1)}) custom-call(bf16[1,2,1024,1024]{3,2,1,0:T(8,128)(2,1)} %dup.7, bf16[1,2,1024,1024]{3,2,1,0:T(8,128)(2,1)} %ddn.7, ...), custom_call_target="tpu_custom_call" | custom-call | flops 1073741824 | bytes 4194304 | tf_op jit(solution)/shard_map/pallas_call | solution.py:57
  38.7 0.1 collective-permute-start.9
  38.8 0.5 %shard_map.96 = bf16[256,256]{1,0:T(8,128)(2,1)S(1)} custom-call(bf16[2,256,1024]{2,1,0:T(8,128)(2,1)S(1)} %get-tuple-element.43.rest, bf16[1024,256]{1,0:T(8,128)(2,1)S(1)} %get-tuple-element.44.trace.two, bf16[1024,256]{1,0:T(8,128)(2,1)S(1)} %get-tuple-element.45.turned, bf16[256,256]{1,0:T(8,128)(2,1)S(1)} %get-tuple-element.46.tail), custom_call_target="tpu_custom_call" | custom-call | flops 16777216 | bytes 1048576 | tf_op jit(solution)/shard_map/pallas_call | solution.py:57
  39.3 0.1 collective-permute-start.10
  39.4 1.3 %collective-permute-done.10.last = bf16[256,256]{1,0:T(8,128)(2,1)S(1)} collective-permute-done((bf16[256,256]{1,0:T(8,128)(2,1)S(1)}, bf16[256,256]{1,0:T(8,128)(2,1)S(1)}, u32[]{:S(2)}, u32[]{:S(2)}) %collective-permute-start.10) | collective-permute-done | bytes 131104 | tf_op jit(solution)/shard_map/ppermute | solution.py:592
  40.7 0.0 collective-permute-done.9.most
  40.7 1.0 %shard_map.97 = (bf16[1,1024,256]{2,1,0:T(8,128)(2,1)}, bf16[1,1024,256]{2,1,0:T(8,128)(2,1)}) custom-call(bf16[768,256]{1,0:T(8,128)(2,1)S(1)} %collective-permute-done.9.most, bf16[256,256]{1,0:T(8,128)(2,1)S(1)} %collective-permute-done.10.last, bf16[1024,256]{1,0:T(8,128)(2,1)S(1)} %get-tuple-element.47.one, ...), custom_call_target="tpu_custom_call" | custom-call | flops 16777216 | bytes 1048576 | tf_op jit(solution)/shard_map/pallas_call | solution.py:57
  (1 shorter events, 0.0 us)
Async XLA Ops:
  2.2 14.7 %all-to-all-start = ((bf16[8,2,32,256]{3,2,1,0:T(8,128)(2,1)}), bf16[8,2,32,256]{3,2,1,0:T(8,128)(2,1)S(1)}, u32[]{:S(2)}, u32[]{:S(2)}) async-start(bf16[8,2,32,256]{3,2,1,0:T(8,128)(2,1)} %get-tuple-element.25), calls=%async_computation | async-start | bytes 524288 | tf_op jit(solution)/shard_map/all_to_all | solution.py:497
  8.6 7.2 %collective-permute-start = (bf16[96,1024]{1,0:T(8,128)(2,1)S(1)}, bf16[96,1024]{1,0:T(8,128)(2,1)S(1)}, u32[]{:S(2)}, u32[]{:S(2)}) collective-permute-start(bf16[96,1024]{1,0:T(8,128)(2,1)S(1)} %get-tuple-element.29), channel_id=1, source_target_pairs={{8,16},{9,17},{10,18},{11,19},{12,20},{13,21},{14,22},{15,23},{16,... | collective-permute-start | bytes 589832 | tf_op jit(solution)/shard_map/ppermute | solution.py:500
  10.7 5.0 %collective-permute-start.1 = (bf16[32,1024]{1,0:T(8,128)(2,1)S(1)}, bf16[32,1024]{1,0:T(8,128)(2,1)S(1)}, u32[]{:S(2)}, u32[]{:S(2)}) collective-permute-start(bf16[32,1024]{1,0:T(8,128)(2,1)S(1)} %get-tuple-element.31.expn1), channel_id=1, source_target_pairs={{0,8},{8,0},{16,24},{24,16},{1,9},{9,1},{17,25},{25,17},{2,10},{10... | collective-permute-start | bytes 196616 | tf_op jit(solution)/shard_map/ppermute | solution.py:501
  14.2 4.5 %collective-permute-start.3 = (bf16[256,256]{1,0:T(8,128)(2,1)S(1)}, bf16[256,256]{1,0:T(8,128)(2,1)S(1)}, u32[]{:S(2)}, u32[]{:S(2)}) collective-permute-start(bf16[256,256]{1,0:T(8,128)(2,1)S(1)} %get-tuple-element.33), channel_id=1, source_target_pairs={{0,8},{8,0},{16,24},{24,16},{1,9},{9,1},{17,25},{25,17},{2,10},{10... | collective-permute-start | bytes 393224 | tf_op jit(solution)/shard_map/ppermute | solution.py:511
  15.2 3.5 %collective-permute-start.4 = (bf16[256,256]{1,0:T(8,128)(2,1)S(1)}, bf16[256,256]{1,0:T(8,128)(2,1)S(1)}, u32[]{:S(2)}, u32[]{:S(2)}) collective-permute-start(bf16[256,256]{1,0:T(8,128)(2,1)S(1)} %get-tuple-element.34), channel_id=1, source_target_pairs={{0,8},{8,0},{16,24},{24,16},{1,9},{9,1},{17,25},{25,17},{2,10},{10... | collective-permute-start | bytes 393224 | tf_op jit(solution)/shard_map/ppermute | solution.py:511
  15.3 3.5 %collective-permute-start.5 = (bf16[256,256]{1,0:T(8,128)(2,1)S(1)}, bf16[256,256]{1,0:T(8,128)(2,1)S(1)}, u32[]{:S(2)}, u32[]{:S(2)}) collective-permute-start(bf16[256,256]{1,0:T(8,128)(2,1)S(1)} %get-tuple-element.35), channel_id=1, source_target_pairs={{0,8},{8,0},{16,24},{24,16},{1,9},{9,1},{17,25},{25,17},{2,10},{10... | collective-permute-start | bytes 393224 | tf_op jit(solution)/shard_map/ppermute | solution.py:511
  15.7 3.0 %collective-permute-start.6 = (bf16[256,256]{1,0:T(8,128)(2,1)S(1)}, bf16[256,256]{1,0:T(8,128)(2,1)S(1)}, u32[]{:S(2)}, u32[]{:S(2)}) collective-permute-start(bf16[256,256]{1,0:T(8,128)(2,1)S(1)} %get-tuple-element.36), channel_id=1, source_target_pairs={{0,8},{8,0},{16,24},{24,16},{1,9},{9,1},{17,25},{25,17},{2,10},{10... | collective-permute-start | bytes 393224 | tf_op jit(solution)/shard_map/ppermute | solution.py:511
  17.0 2.6 %collective-permute-start.2 = (bf16[32,256]{1,0:T(8,128)(2,1)S(1)}, bf16[32,256]{1,0:T(8,128)(2,1)S(1)}, u32[]{:S(2)}, u32[]{:S(2)}) collective-permute-start(bf16[32,256]{1,0:T(8,128)(2,1)S(1)} %shard_map.89), channel_id=1, source_target_pairs={{0,8},{8,0},{16,24},{24,16},{1,9},{9,1},{17,25},{25,17},{2,10},{10... | collective-permute-start | bytes 49160 | tf_op jit(solution)/shard_map/ppermute | solution.py:524
  20.5 12.1 %all-to-all-start.1 = ((bf16[8,80,256]{2,1,0:T(8,128)(2,1)}), bf16[8,80,256]{2,1,0:T(8,128)(2,1)S(1)}, u32[]{:S(2)}, u32[]{:S(2)}) async-start(bf16[8,80,256]{2,1,0:T(8,128)(2,1)} %shard_map.91.payload), calls=%async_computation.1 | async-start | bytes 655360 | tf_op jit(solution)/shard_map/all_to_all | solution.py:546
  27.3 9.6 %collective-permute-start.7 = (bf16[1024,256]{1,0:T(8,128)(2,1)S(1)}, bf16[1024,256]{1,0:T(8,128)(2,1)S(1)}, u32[]{:S(2)}, u32[]{:S(2)}) collective-permute-start(bf16[1024,256]{1,0:T(8,128)(2,1)S(1)} %get-tuple-element.38), channel_id=1, source_target_pairs={{8,16},{9,17},{10,18},{11,19},{12,20},{13,21},{14,22},{15,23},{16,... | collective-permute-start | bytes 1572872 | tf_op jit(solution)/shard_map/ppermute | solution.py:556
  33.2 3.6 %collective-permute-start.8 = (bf16[64,256]{1,0:T(8,128)(2,1)S(1)}, bf16[64,256]{1,0:T(8,128)(2,1)S(1)}, u32[]{:S(2)}, u32[]{:S(2)}) collective-permute-start(bf16[64,256]{1,0:T(8,128)(2,1)S(1)} %shard_map.93.coupled), channel_id=1, source_target_pairs={{0,24},{8,16},{16,8},{24,0},{1,25},{9,17},{17,9},{25,1},{2,26},{10... | collective-permute-start | bytes 98312 | tf_op jit(solution)/shard_map/ppermute | solution.py:566
  38.7 2.0 %collective-permute-start.9 = (bf16[768,256]{1,0:T(8,128)(2,1)S(1)}, bf16[768,256]{1,0:T(8,128)(2,1)S(1)}, u32[]{:S(2)}, u32[]{:S(2)}) collective-permute-start(bf16[768,256]{1,0:T(8,128)(2,1)S(1)} %get-tuple-element.42), channel_id=1, source_target_pairs={{0,8},{8,0},{16,24},{24,16},{1,9},{9,1},{17,25},{25,17},{2,10},{10... | collective-permute-start | bytes 1179656 | tf_op jit(solution)/shard_map/ppermute | solution.py:592
  39.3 1.4 %collective-permute-start.10 = (bf16[256,256]{1,0:T(8,128)(2,1)S(1)}, bf16[256,256]{1,0:T(8,128)(2,1)S(1)}, u32[]{:S(2)}, u32[]{:S(2)}) collective-permute-start(bf16[256,256]{1,0:T(8,128)(2,1)S(1)} %shard_map.96), channel_id=1, source_target_pairs={{0,8},{8,0},{16,24},{24,16},{1,9},{9,1},{17,25},{25,17},{2,10},{10... | collective-permute-start | bytes 393224 | tf_op jit(solution)/shard_map/ppermute | solution.py:592

commit v5 on v4

--- a/solution.py
+++ b/solution.py
@@ -52,7 +52,7 @@
 VMEM = pl.BlockSpec(memory_space=pltpu.VMEM)
 
 
-def call(body, outs, far, near, scratch, sems, flops=0, moved=0):
+def call(body, outs, far, near, scratch, sems, flops=0, moved=0, aliases=None):
     kept = [isinstance(out, tuple) for out in outs]
     return pl.pallas_call(
         body,
@@ -61,6 +61,7 @@
         out_specs=tuple(VMEM if keep else HBM for keep in kept),
         scratch_shapes=[pltpu.VMEM(shape, BF16) for shape in scratch]
         + [pltpu.SemaphoreType.DMA((sems,))],
+        input_output_aliases=aliases or {},
         cost_estimate=pl.CostEstimate(flops=flops, bytes_accessed=moved, transcendentals=0),
         compiler_params=pltpu.CompilerParams(vmem_limit_bytes=24 * 2**20),
     )(*far, *near)
@@ -352,6 +353,16 @@
     lax.fori_loop(0, block.shape[1] // size, one, 0)
 
 
+def put(which, source, up, down, sem):
+    @pl.when(which == 0)
+    def _():
+        start(source, up.at[0], sem)
+
+    @pl.when(which != 0)
+    def _():
+        start(source, down.at[0], sem)
+
+
 def settle_kernel(
     expn, dup, ddn, coupled, packed, lower, bases, sems
 ):
@@ -372,10 +383,18 @@
 
 
 def inner_second_kernel(
-    dup, ddn, crossed, coupled, source2, lower, bases,
-    out, trace, turned, rest, tail, added2, upper, sems,
+    dup, ddn, crossed, coupled, source2, lower, bases, source1, one,
+    up, down, out, trace, turned, rest, tail, added2, upper, sems,
 ):
     outer, first = roles()
+
+    @pl.when(outer)
+    def _():
+        put(first, source1, up, down, sems.at[CHUNKS + 1])
+
+    @pl.when(jnp.logical_not(outer))
+    def _():
+        put(first, one, up, down, sems.at[CHUNKS + 1])
 
     @pl.when(jnp.logical_not(outer))
     def _():
@@ -408,6 +427,8 @@
         each_chunk_of(upper, step, second)
         arrive(rest, sems.at[CHUNKS])
 
+    arrive(source1, sems.at[CHUNKS + 1])
+
 
 def inner_rest_kernel(rest, trace, turned, tail, out, sems):
     del sems
@@ -419,17 +440,9 @@
         out[...] = (value + tail[...].astype(F32)).astype(BF16)
 
 
-def last_kernel(most, last, one, two, source1, source2, up, down, sums, sems):
+def last_kernel(before_up, before_down, most, last, two, source2, up, down, sums, sems):
+    del before_up, before_down
     outer, first = roles()
-
-    def put(which, source, sem):
-        @pl.when(which == 0)
-        def _():
-            start(source, up.at[0], sem)
-
-        @pl.when(which != 0)
-        def _():
-            start(source, down.at[0], sem)
 
     def put_rows(which, rows, sem):
         @pl.when(which == 0)
@@ -442,21 +455,17 @@
 
     @pl.when(outer)
     def _():
-        put(first, source1, sems.at[0])
-
         cut = most.shape[0]
         for part, rows in ((most, pl.ds(0, cut)), (last, pl.ds(cut, sums.shape[0] - cut))):
             value = source2[rows, :].astype(F32) + part[...].astype(F32)
             sums[rows, :] = value.astype(BF16)
-            put_rows(1 - first, rows, sems.at[1])
-
-    @pl.when(jnp.logical_not(outer))
-    def _():
-        put(first, one, sems.at[0])
-        put(1 - first, two, sems.at[1])
+            put_rows(1 - first, rows, sems.at[0])
+
+    @pl.when(jnp.logical_not(outer))
+    def _():
+        put(1 - first, two, up, down, sems.at[0])
 
     arrive(sums, sems.at[0])
-    arrive(sums, sems.at[1])
 
 
 def wave(*arrays):
@@ -574,16 +583,17 @@
         **large,
     )
     step = points // CHUNKS
-    most, two, turned, rest, tail = call(
+    up, down, most, two, turned, rest, tail = call(
         inner_second_kernel,
         (
+            *(like(1, *field), like(1, *field)),
             *(kept(points - step, width), kept(*field), kept(*field)),
             *(kept(2, step, points), kept(step, width)),
         ),
         diagonals,
-        (crossed, reached, source2, lower, bases),
+        (crossed, reached, source2, lower, bases, source1, one),
         [field, (2, points // 2 - step, points)],
-        CHUNKS + 1,
+        CHUNKS + 2,
         **large,
     )
     (last,) = call(
@@ -593,10 +603,11 @@
     return call(
         last_kernel,
         (like(1, *field), like(1, *field)),
-        (),
-        (*arrived, one, two, source1, source2),
+        (up, down),
+        (*arrived, two, source2),
         [field],
-        2,
+        1,
+        aliases={0: 0, 1: 1},
         **small,
     )
 

time: 42.2 us -> 42.1 us (level)
  no operation moved by 1% of the time
where the time goes in v5:
time: 42.1 us; the launch traced here: 41.6 us
  starting transfers between devices  20.7 us (49%)
  Pallas kernels  14.8 us (35%)
  waiting for transfers between devices  5.38 us (13%)
  between operations  0.77 us (2%)
    pallas_call x12, Pallas kernels, call(): pl.pallas_call(body, out_shape=tuple((pltpu.VMEM(*out) if keep else out f...  14.8 us
    all_to_all x1, starting transfers between devices, wave(): gathered = lax.all_to_all(payload, 'trace', 0, 0)  6.37 us
    all_to_all x1, waiting for transfers between devices, wave(): lax.all_to_all(payload, ('layer', 'trace'), 0, 0, axis_index_groups=groups)  3.55 us
    all_to_all x1, starting transfers between devices, wave(): lax.all_to_all(payload, ('layer', 'trace'), 0, 0, axis_index_groups=groups)  3.55 us
    ppermute x1, starting transfers between devices, wave(): packed = lax.ppermute(pack, ('layer', 'trace'), pairs)  2.08 us
    ppermute x1, starting transfers between devices, wave(): reached = lax.ppermute(coupled, 'layer', across)  2.01 us
    ppermute x1, starting transfers between devices, wave(): crossed = lax.ppermute(product, ('layer', 'trace'), pairs)  1.82 us
    ppermute x1, starting transfers between devices, wave(): before = lax.ppermute(before, 'layer', swap)  1.78 us
  transfers between devices with their start and end apart: 13, of which 3 were waited for; matrix products, arithmetic and copies ran while one was open for 0% of the time, Pallas kernels for 23%

profile of v5, /device:TPU:1, one launch (start us, length us, event | category | flops | bytes accessed | tf_op | source)
XLA Modules:
  0.0 41.6 jit_solution(13245205282615326738)
XLA Ops:
  0.6 1.6 %shard_map.86 = (bf16[8,2,32,256]{3,2,1,0:T(8,128)(2,1)}, bf16[96,1024]{1,0:T(8,128)(2,1)S(1)}, bf16[1024,256]{1,0:T(8,128)(2,1)S(1)}, bf16[32,1024]{1,0:T(8,128...) custom-call(bf16[1,1024,256]{2,1,0:T(8,128)(2,1)} %sup.3, bf16[1,1024,256]{2,1,0:T(8,128)(2,1)} %sdn.3, ...), custom_call_target="tpu_custom_call" | custom-call | flops 16777216 | bytes 1048576 | tf_op jit(solution)/shard_map/pallas_call | solution.py:57
  2.2 6.4 %all-to-all-start = ((bf16[8,2,32,256]{3,2,1,0:T(8,128)(2,1)}), bf16[8,2,32,256]{3,2,1,0:T(8,128)(2,1)S(1)}, u32[]{:S(2)}, u32[]{:S(2)}) async-start(bf16[8,2,32,256]{3,2,1,0:T(8,128)(2,1)} %get-tuple-element.27), calls=%async_computation | async-start | bytes 524288 | tf_op jit(solution)/shard_map/all_to_all | solution.py:506
  8.6 2.1 %collective-permute-start = (bf16[96,1024]{1,0:T(8,128)(2,1)S(1)}, bf16[96,1024]{1,0:T(8,128)(2,1)S(1)}, u32[]{:S(2)}, u32[]{:S(2)}) collective-permute-start(bf16[96,1024]{1,0:T(8,128)(2,1)S(1)} %get-tuple-element.31), channel_id=1, source_target_pairs={{8,16},{9,17},{10,18},{11,19},{12,20},{13,21},{14,22},{15,23},{16,... | collective-permute-start | bytes 589832 | tf_op jit(solution)/shard_map/ppermute | solution.py:509
  10.7 1.3 %collective-permute-start.1 = (bf16[32,1024]{1,0:T(8,128)(2,1)S(1)}, bf16[32,1024]{1,0:T(8,128)(2,1)S(1)}, u32[]{:S(2)}, u32[]{:S(2)}) collective-permute-start(bf16[32,1024]{1,0:T(8,128)(2,1)S(1)} %get-tuple-element.33.expn1), channel_id=1, source_target_pairs={{0,8},{8,0},{16,24},{24,16},{1,9},{9,1},{17,25},{25,17},{2,10},{10... | collective-permute-start | bytes 196616 | tf_op jit(solution)/shard_map/ppermute | solution.py:510
  12.0 2.2 %shard_map.87 = (bf16[256,256]{1,0:T(8,128)(2,1)S(1)}, bf16[256,256]{1,0:T(8,128)(2,1)S(1)}, bf16[256,256]{1,0:T(8,128)(2,1)S(1)}, bf16[256,256]{1,0:T(8,128)(2,1)S(1)}, bf16[2,1024,1024]{2,1,0:T(8,128)(2,1)S(1)}) custom-call(bf16[1,2,1024,1024]{3,2,1,0:T(8,128)(2,1)} %dup.7, bf16[1,2,1024,1024]{3,2,1,0:T(8,128)(2,1)} %ddn.7, ...), custom_call_target="tpu_custom_call" | custom-call | flops 1073741824 | bytes 4194304 | tf_op jit(solution)/shard_map/pallas_call | solution.py:57
  14.2 1.0 %collective-permute-start.3 = (bf16[256,256]{1,0:T(8,128)(2,1)S(1)}, bf16[256,256]{1,0:T(8,128)(2,1)S(1)}, u32[]{:S(2)}, u32[]{:S(2)}) collective-permute-start(bf16[256,256]{1,0:T(8,128)(2,1)S(1)} %get-tuple-element.35), channel_id=1, source_target_pairs={{0,8},{8,0},{16,24},{24,16},{1,9},{9,1},{17,25},{25,17},{2,10},{10... | collective-permute-start | bytes 393224 | tf_op jit(solution)/shard_map/ppermute | solution.py:520
  15.2 0.1 collective-permute-start.4
  15.3 0.4 %collective-permute-start.5 = (bf16[256,256]{1,0:T(8,128)(2,1)S(1)}, bf16[256,256]{1,0:T(8,128)(2,1)S(1)}, u32[]{:S(2)}, u32[]{:S(2)}) collective-permute-start(bf16[256,256]{1,0:T(8,128)(2,1)S(1)} %get-tuple-element.37), channel_id=1, source_target_pairs={{0,8},{8,0},{16,24},{24,16},{1,9},{9,1},{17,25},{25,17},{2,10},{10... | collective-permute-start | bytes 393224 | tf_op jit(solution)/shard_map/ppermute | solution.py:520
  15.7 0.0 collective-permute-done.1.before.refs_5_
  15.7 0.1 collective-permute-start.6
  15.8 0.0 collective-permute-done.packed
  15.8 1.1 %shard_map.88 = (bf16[96,1024]{1,0:T(8,128)(2,1)S(1)}, bf16[32,128]{1,0:T(8,128)(2,1)S(1)}) custom-call(bf16[2,1024,1024]{2,1,0:T(8,128)(2,1)S(1)} %get-tuple-element.30.block, bf16[96,1024]{1,0:T(8,128)(2,1)S(1)} %collective-permute-done.packed, bf16[32,1024]{1,0:T(8,128)(2,1)S(1)} %get-tuple-element.32.own, bf16[32,1024]{1,0:T(8,128)(2,1)S(1)} %get-tuple-element.33.expn1, ...), custom_call_target="tpu_custom_call" | custom-call | flops 1073741824 | bytes 4194304 | tf_op jit(solution)/shard_map/pallas_call | solution.py:57
  16.9 0.0 all-to-all-done.gathered
  17.0 1.8 %collective-permute-start.2 = (bf16[32,256]{1,0:T(8,128)(2,1)S(1)}, bf16[32,256]{1,0:T(8,128)(2,1)S(1)}, u32[]{:S(2)}, u32[]{:S(2)}) collective-permute-start(bf16[32,256]{1,0:T(8,128)(2,1)S(1)} %shard_map.89), channel_id=1, source_target_pairs={{0,8},{8,0},{16,24},{24,16},{1,9},{9,1},{17,25},{25,17},{2,10},{10... | collective-permute-start | bytes 49160 | tf_op jit(solution)/shard_map/ppermute | solution.py:533
  18.8 0.0 collective-permute-done.3.refs_0_
  18.8 0.0 collective-permute-done.4.refs_1_
  18.8 0.0 collective-permute-done.5.refs_2_
  18.8 0.0 collective-permute-done.6.refs_3_
  18.8 0.3 shard_map.90.sums
  19.1 0.5 %collective-permute-done.2.before.refs_4_ = bf16[32,256]{1,0:T(8,128)(2,1)S(1)} collective-permute-done((bf16[32,256]{1,0:T(8,128)(2,1)S(1)}, bf16[32,256]{1,0:T(8,128)(2,1)S(1)}, u32[]{:S(2)}, u32[]{:S(2)}) %collective-permute-start.2) | collective-permute-done | bytes 16416 | tf_op jit(solution)/shard_map/ppermute | solution.py:533
  19.6 0.9 %shard_map.91.payload = bf16[8,80,256]{2,1,0:T(8,128)(2,1)} custom-call(bf16[32,256]{1,0:T(8,128)(2,1)S(1)} %collective-permute-done.2.before.refs_4_, f32[64,256]{1,0:T(8,128)S(1)} %shard_map.90.sums, bf16[32,128]{1,0:T(8,128)(2,1)S(1)} %get-tuple-element.34.mixed, bf16[96,1024]{1,0:T(8,128)(2,1)S(1)} %collective-permute-done.packed), custom_call_target="tpu_custom_call" | custom-call | flops 16777216 | bytes 1048576 | tf_op jit(solution)/shard_map/pallas_call | solution.py:57
  20.5 3.5 %all-to-all-start.1 = ((bf16[8,80,256]{2,1,0:T(8,128)(2,1)}), bf16[8,80,256]{2,1,0:T(8,128)(2,1)S(1)}, u32[]{:S(2)}, u32[]{:S(2)}) async-start(bf16[8,80,256]{2,1,0:T(8,128)(2,1)} %shard_map.91.payload), calls=%async_computation.1 | async-start | bytes 655360 | tf_op jit(solution)/shard_map/all_to_all | solution.py:555
  24.1 3.2 %shard_map.92 = (bf16[1024,256]{1,0:T(8,128)(2,1)S(1)}, bf16[1024,256]{1,0:T(8,128)(2,1)S(1)}, bf16[1024,256]{1,0:T(8,128)(2,1)S(1)}) custom-call(bf16[1,1024,256]{2,1,0:T(8,128)(2,1)} %sup.3, bf16[1,1024,256]{2,1,0:T(8,128)(2,1)} %sdn.3, bf16[1,2,1024,1024]{3,2,1,0:T(8,128)(2,1)} %dup.7, bf16[1,2,1024,1024]{3,2,1,0:T(8,128)(2,1)} %ddn.7, ...), custom_call_target="tpu_custom_call" | custom-call | flops 1073741824 | bytes 4194304 | tf_op jit(solution)/shard_map/pallas_call | solution.py:57
  27.3 1.8 %collective-permute-start.7 = (bf16[1024,256]{1,0:T(8,128)(2,1)S(1)}, bf16[1024,256]{1,0:T(8,128)(2,1)S(1)}, u32[]{:S(2)}, u32[]{:S(2)}) collective-permute-start(bf16[1024,256]{1,0:T(8,128)(2,1)S(1)} %get-tuple-element.40), channel_id=1, source_target_pairs={{8,16},{9,17},{10,18},{11,19},{12,20},{13,21},{14,22},{15,23},{16,... | collective-permute-start | bytes 1572872 | tf_op jit(solution)/shard_map/ppermute | solution.py:565
  29.1 3.6 %all-to-all-done.1.second = bf16[8,80,256]{2,1,0:T(8,128)(2,1)S(1)} async-done(((bf16[8,80,256]{2,1,0:T(8,128)(2,1)}), bf16[8,80,256]{2,1,0:T(8,128)(2,1)S(1)}, u32[]{:S(2)}, u32[]{:S(2)}) %all-to-all-start.1) | async-done | bytes 327712 | tf_op jit(solution)/shard_map/all_to_all | solution.py:555
  32.6 0.6 %shard_map.93.coupled = bf16[64,256]{1,0:T(8,128)(2,1)S(1)} custom-call(bf16[8,2,32,256]{3,2,1,0:T(8,128)(2,1)S(1)} %all-to-all-done.gathered, bf16[8,80,256]{2,1,0:T(8,128)(2,1)S(1)} %all-to-all-done.1.second, bf16[96,1024]{1,0:T(8,128)(2,1)S(1)} %collective-permute-done.packed, bf16[2,32,256]{2,1,0:T(8,128)(2,1)S(1)} %get-tuple-element.28.couple1), custom_call_target="tpu_custom_call" | custom-call | flops 16777216 | bytes 1048576 | tf_op jit(solution)/shard_map/pallas_call | solution.py:57
  33.2 2.0 %collective-permute-start.8 = (bf16[64,256]{1,0:T(8,128)(2,1)S(1)}, bf16[64,256]{1,0:T(8,128)(2,1)S(1)}, u32[]{:S(2)}, u32[]{:S(2)}) collective-permute-start(bf16[64,256]{1,0:T(8,128)(2,1)S(1)} %shard_map.93.coupled), channel_id=1, source_target_pairs={{0,24},{8,16},{16,8},{24,0},{1,25},{9,17},{17,9},{25,1},{2,26},{10... | collective-permute-start | bytes 98312 | tf_op jit(solution)/shard_map/ppermute | solution.py:575
  35.2 1.6 %shard_map.94 = (bf16[2,512,1024]{2,1,0:T(8,128)(2,1)S(1)}, bf16[64,1024]{1,0:T(8,128)(2,1)S(1)}) custom-call(bf16[1,2,32,1024]{3,2,1,0:T(8,128)(2,1)} %expn.3, bf16[1,2,1024,1024]{3,2,1,0:T(8,128)(2,1)} %dup.7, bf16[1,2,1024,1024]{3,2,1,0:T(8,128)(2,1)} %ddn.7, bf16[64,256]{1,0:T(8,128)(2,1)S(1)} %shard_map.93.coupled, ...), custom_call_target="tpu_custom_call" | custom-call | flops 1073741824 | bytes 4194304 | tf_op jit(solution)/shard_map/pallas_call | solution.py:57
  36.8 0.0 collective-permute-done.7.crossed
  36.9 0.0 collective-permute-done.8.coupled
  36.9 1.9 %shard_map.95 = (bf16[1,1024,256]{2,1,0:T(8,128)(2,1)}, bf16[1,1024,256]{2,1,0:T(8,128)(2,1)}, bf16[768,256]{1,0:T(8,128)(2,1)S(1)}, bf16[1024,256]{1,0:T(8,128)...) custom-call(bf16[1,2,1024,1024]{3,2,1,0:T(8,128)(2,1)} %dup.7, ...), custom_call_target="tpu_custom_call" | custom-call | flops 1073741824 | bytes 4194304 | tf_op jit(solution)/shard_map/pallas_call | solution.py:57
  38.8 0.1 collective-permute-start.9
  38.9 0.5 %shard_map.96 = bf16[256,256]{1,0:T(8,128)(2,1)S(1)} custom-call(bf16[2,256,1024]{2,1,0:T(8,128)(2,1)S(1)} %get-tuple-element.48.rest, bf16[1024,256]{1,0:T(8,128)(2,1)S(1)} %get-tuple-element.49.trace.two, bf16[1024,256]{1,0:T(8,128)(2,1)S(1)} %get-tuple-element.50.turned, bf16[256,256]{1,0:T(8,128)(2,1)S(1)} %get-tuple-element.51.tail), custom_call_target="tpu_custom_call" | custom-call | flops 16777216 | bytes 1048576 | tf_op jit(solution)/shard_map/pallas_call | solution.py:57
  39.4 0.1 collective-permute-start.10
  39.5 1.3 %collective-permute-done.10.last = bf16[256,256]{1,0:T(8,128)(2,1)S(1)} collective-permute-done((bf16[256,256]{1,0:T(8,128)(2,1)S(1)}, bf16[256,256]{1,0:T(8,128)(2,1)S(1)}, u32[]{:S(2)}, u32[]{:S(2)}) %collective-permute-start.10) | collective-permute-done | bytes 131104 | tf_op jit(solution)/shard_map/ppermute | solution.py:602
  40.8 0.0 collective-permute-done.9.most
  40.8 0.8 %shard_map.97 = (bf16[1,1024,256]{2,1,0:T(8,128)(2,1)}, bf16[1,1024,256]{2,1,0:T(8,128)(2,1)}) custom-call(bf16[1,1024,256]{2,1,0:T(8,128)(2,1)} %get-tuple-element.45.before_up, bf16[1,1024,256]{2,1,0:T(8,128)(2,1)} %get-tuple-element.46.before_down, ...), custom_call_target="tpu_custom_call", output_to_operand_aliasing={{0}: (0, {}), {1}: (1, {})} | custom-call | flops 16777216 | bytes 1048576 | tf_op jit(solution)/shard_map/pallas_call | solution.py:57
  (1 shorter events, 0.0 us)
Async XLA Ops:
  2.2 14.7 %all-to-all-start = ((bf16[8,2,32,256]{3,2,1,0:T(8,128)(2,1)}), bf16[8,2,32,256]{3,2,1,0:T(8,128)(2,1)S(1)}, u32[]{:S(2)}, u32[]{:S(2)}) async-start(bf16[8,2,32,256]{3,2,1,0:T(8,128)(2,1)} %get-tuple-element.27), calls=%async_computation | async-start | bytes 524288 | tf_op jit(solution)/shard_map/all_to_all | solution.py:506
  8.6 7.2 %collective-permute-start = (bf16[96,1024]{1,0:T(8,128)(2,1)S(1)}, bf16[96,1024]{1,0:T(8,128)(2,1)S(1)}, u32[]{:S(2)}, u32[]{:S(2)}) collective-permute-start(bf16[96,1024]{1,0:T(8,128)(2,1)S(1)} %get-tuple-element.31), channel_id=1, source_target_pairs={{8,16},{9,17},{10,18},{11,19},{12,20},{13,21},{14,22},{15,23},{16,... | collective-permute-start | bytes 589832 | tf_op jit(solution)/shard_map/ppermute | solution.py:509
  10.7 5.0 %collective-permute-start.1 = (bf16[32,1024]{1,0:T(8,128)(2,1)S(1)}, bf16[32,1024]{1,0:T(8,128)(2,1)S(1)}, u32[]{:S(2)}, u32[]{:S(2)}) collective-permute-start(bf16[32,1024]{1,0:T(8,128)(2,1)S(1)} %get-tuple-element.33.expn1), channel_id=1, source_target_pairs={{0,8},{8,0},{16,24},{24,16},{1,9},{9,1},{17,25},{25,17},{2,10},{10... | collective-permute-start | bytes 196616 | tf_op jit(solution)/shard_map/ppermute | solution.py:510
  14.2 4.5 %collective-permute-start.3 = (bf16[256,256]{1,0:T(8,128)(2,1)S(1)}, bf16[256,256]{1,0:T(8,128)(2,1)S(1)}, u32[]{:S(2)}, u32[]{:S(2)}) collective-permute-start(bf16[256,256]{1,0:T(8,128)(2,1)S(1)} %get-tuple-element.35), channel_id=1, source_target_pairs={{0,8},{8,0},{16,24},{24,16},{1,9},{9,1},{17,25},{25,17},{2,10},{10... | collective-permute-start | bytes 393224 | tf_op jit(solution)/shard_map/ppermute | solution.py:520
  15.2 3.5 %collective-permute-start.4 = (bf16[256,256]{1,0:T(8,128)(2,1)S(1)}, bf16[256,256]{1,0:T(8,128)(2,1)S(1)}, u32[]{:S(2)}, u32[]{:S(2)}) collective-permute-start(bf16[256,256]{1,0:T(8,128)(2,1)S(1)} %get-tuple-element.36), channel_id=1, source_target_pairs={{0,8},{8,0},{16,24},{24,16},{1,9},{9,1},{17,25},{25,17},{2,10},{10... | collective-permute-start | bytes 393224 | tf_op jit(solution)/shard_map/ppermute | solution.py:520
  15.3 3.5 %collective-permute-start.5 = (bf16[256,256]{1,0:T(8,128)(2,1)S(1)}, bf16[256,256]{1,0:T(8,128)(2,1)S(1)}, u32[]{:S(2)}, u32[]{:S(2)}) collective-permute-start(bf16[256,256]{1,0:T(8,128)(2,1)S(1)} %get-tuple-element.37), channel_id=1, source_target_pairs={{0,8},{8,0},{16,24},{24,16},{1,9},{9,1},{17,25},{25,17},{2,10},{10... | collective-permute-start | bytes 393224 | tf_op jit(solution)/shard_map/ppermute | solution.py:520
  15.7 3.0 %collective-permute-start.6 = (bf16[256,256]{1,0:T(8,128)(2,1)S(1)}, bf16[256,256]{1,0:T(8,128)(2,1)S(1)}, u32[]{:S(2)}, u32[]{:S(2)}) collective-permute-start(bf16[256,256]{1,0:T(8,128)(2,1)S(1)} %get-tuple-element.38), channel_id=1, source_target_pairs={{0,8},{8,0},{16,24},{24,16},{1,9},{9,1},{17,25},{25,17},{2,10},{10... | collective-permute-start | bytes 393224 | tf_op jit(solution)/shard_map/ppermute | solution.py:520
  17.0 2.6 %collective-permute-start.2 = (bf16[32,256]{1,0:T(8,128)(2,1)S(1)}, bf16[32,256]{1,0:T(8,128)(2,1)S(1)}, u32[]{:S(2)}, u32[]{:S(2)}) collective-permute-start(bf16[32,256]{1,0:T(8,128)(2,1)S(1)} %shard_map.89), channel_id=1, source_target_pairs={{0,8},{8,0},{16,24},{24,16},{1,9},{9,1},{17,25},{25,17},{2,10},{10... | collective-permute-start | bytes 49160 | tf_op jit(solution)/shard_map/ppermute | solution.py:533
  20.5 12.1 %all-to-all-start.1 = ((bf16[8,80,256]{2,1,0:T(8,128)(2,1)}), bf16[8,80,256]{2,1,0:T(8,128)(2,1)S(1)}, u32[]{:S(2)}, u32[]{:S(2)}) async-start(bf16[8,80,256]{2,1,0:T(8,128)(2,1)} %shard_map.91.payload), calls=%async_computation.1 | async-start | bytes 655360 | tf_op jit(solution)/shard_map/all_to_all | solution.py:555
  27.3 9.6 %collective-permute-start.7 = (bf16[1024,256]{1,0:T(8,128)(2,1)S(1)}, bf16[1024,256]{1,0:T(8,128)(2,1)S(1)}, u32[]{:S(2)}, u32[]{:S(2)}) collective-permute-start(bf16[1024,256]{1,0:T(8,128)(2,1)S(1)} %get-tuple-element.40), channel_id=1, source_target_pairs={{8,16},{9,17},{10,18},{11,19},{12,20},{13,21},{14,22},{15,23},{16,... | collective-permute-start | bytes 1572872 | tf_op jit(solution)/shard_map/ppermute | solution.py:565
  33.2 3.6 %collective-permute-start.8 = (bf16[64,256]{1,0:T(8,128)(2,1)S(1)}, bf16[64,256]{1,0:T(8,128)(2,1)S(1)}, u32[]{:S(2)}, u32[]{:S(2)}) collective-permute-start(bf16[64,256]{1,0:T(8,128)(2,1)S(1)} %shard_map.93.coupled), channel_id=1, source_target_pairs={{0,24},{8,16},{16,8},{24,0},{1,25},{9,17},{17,9},{25,1},{2,26},{10... | collective-permute-start | bytes 98312 | tf_op jit(solution)/shard_map/ppermute | solution.py:575
  38.8 2.0 %collective-permute-start.9 = (bf16[768,256]{1,0:T(8,128)(2,1)S(1)}, bf16[768,256]{1,0:T(8,128)(2,1)S(1)}, u32[]{:S(2)}, u32[]{:S(2)}) collective-permute-start(bf16[768,256]{1,0:T(8,128)(2,1)S(1)} %get-tuple-element.47), channel_id=1, source_target_pairs={{0,8},{8,0},{16,24},{24,16},{1,9},{9,1},{17,25},{25,17},{2,10},{10... | collective-permute-start | bytes 1179656 | tf_op jit(solution)/shard_map/ppermute | solution.py:602
  39.4 1.4 %collective-permute-start.10 = (bf16[256,256]{1,0:T(8,128)(2,1)S(1)}, bf16[256,256]{1,0:T(8,128)(2,1)S(1)}, u32[]{:S(2)}, u32[]{:S(2)}) collective-permute-start(bf16[256,256]{1,0:T(8,128)(2,1)S(1)} %shard_map.96), channel_id=1, source_target_pairs={{0,8},{8,0},{16,24},{24,16},{1,9},{9,1},{17,25},{25,17},{2,10},{10... | collective-permute-start | bytes 393224 | tf_op jit(solution)/shard_map/ppermute | solution.py:602

commit v6 on v5

--- a/solution.py
+++ b/solution.py
@@ -364,10 +364,18 @@
 
 
 def settle_kernel(
-    expn, dup, ddn, coupled, packed, lower, bases, sems
+    expn, dup, ddn, coupled, packed, source1, one, up, down, lower, bases, sems
 ):
     del coupled
     outer, first = roles()
+
+    @pl.when(outer)
+    def _():
+        put(first, source1, up, down, sems.at[0])
+
+    @pl.when(jnp.logical_not(outer))
+    def _():
+        put(first, one, up, down, sems.at[0])
 
     @pl.when(jnp.logical_not(outer))
     def _():
@@ -381,20 +389,14 @@
             lower, step, lambda c, rows: arrive(lower.at[:, rows, :], sems.at[2 + c])
         )
 
+    arrive(source1, sems.at[0])
+
 
 def inner_second_kernel(
-    dup, ddn, crossed, coupled, source2, lower, bases, source1, one,
-    up, down, out, trace, turned, rest, tail, added2, upper, sems,
+    dup, ddn, crossed, coupled, source2, lower, bases,
+    out, trace, turned, rest, tail, added2, upper, sems,
 ):
     outer, first = roles()
-
-    @pl.when(outer)
-    def _():
-        put(first, source1, up, down, sems.at[CHUNKS + 1])
-
-    @pl.when(jnp.logical_not(outer))
-    def _():
-        put(first, one, up, down, sems.at[CHUNKS + 1])
 
     @pl.when(jnp.logical_not(outer))
     def _():
@@ -426,8 +428,6 @@
 
         each_chunk_of(upper, step, second)
         arrive(rest, sems.at[CHUNKS])
-
-    arrive(source1, sems.at[CHUNKS + 1])
 
 
 def inner_rest_kernel(rest, trace, turned, tail, out, sems):
@@ -573,27 +573,26 @@
         **small,
     )
     reached = lax.ppermute(coupled, "layer", across)
-    lower, bases = call(
+    up, down, lower, bases = call(
         settle_kernel,
-        (kept(2, points // 2, points), kept(2 * k, points)),
+        (like(1, *field), like(1, *field), kept(2, points // 2, points), kept(2 * k, points)),
         (expansion, *diagonals),
-        (coupled, packed),
+        (coupled, packed, source1, one),
         [],
         2 + CHUNKS // 2,
         **large,
     )
     step = points // CHUNKS
-    up, down, most, two, turned, rest, tail = call(
+    most, two, turned, rest, tail = call(
         inner_second_kernel,
         (
-            *(like(1, *field), like(1, *field)),
             *(kept(points - step, width), kept(*field), kept(*field)),
             *(kept(2, step, points), kept(step, width)),
         ),
         diagonals,
-        (crossed, reached, source2, lower, bases, source1, one),
+        (crossed, reached, source2, lower, bases),
         [field, (2, points // 2 - step, points)],
-        CHUNKS + 2,
+        CHUNKS + 1,
         **large,
     )
     (last,) = call(

time: 42.1 us -> 42.3 us (level)
  no operation moved by 1% of the time
where the time goes in v6:
time: 42.3 us; the launch traced here: 41.7 us
  starting transfers between devices  20.7 us (49%)
  Pallas kernels  14.9 us (35%)
  waiting for transfers between devices  5.38 us (13%)
  between operations  0.77 us (2%)
    pallas_call x12, Pallas kernels, call(): pl.pallas_call(body, out_shape=tuple((pltpu.VMEM(*out) if keep else out f...  14.9 us
    all_to_all x1, starting transfers between devices, wave(): gathered = lax.all_to_all(payload, 'trace', 0, 0)  6.37 us
    all_to_all x1, waiting for transfers between devices, wave(): lax.all_to_all(payload, ('layer', 'trace'), 0, 0, axis_index_groups=groups)  3.55 us
    all_to_all x1, starting transfers between devices, wave(): lax.all_to_all(payload, ('layer', 'trace'), 0, 0, axis_index_groups=groups)  3.55 us
    ppermute x1, starting transfers between devices, wave(): packed = lax.ppermute(pack, ('layer', 'trace'), pairs)  2.08 us
    ppermute x1, starting transfers between devices, wave(): reached = lax.ppermute(coupled, 'layer', across)  2.01 us
    ppermute x1, starting transfers between devices, wave(): crossed = lax.ppermute(product, ('layer', 'trace'), pairs)  1.82 us
    ppermute x1, starting transfers between devices, wave(): before = lax.ppermute(before, 'layer', swap)  1.78 us
  transfers between devices with their start and end apart: 13, of which 3 were waited for; matrix products, arithmetic and copies ran while one was open for 0% of the time, Pallas kernels for 23%

profile of v6, /device:TPU:1, one launch (start us, length us, event | category | flops | bytes accessed | tf_op | source)
XLA Modules:
  0.0 41.7 jit_solution(15571339378635487151)
XLA Ops:
  0.6 1.6 %shard_map.86 = (bf16[8,2,32,256]{3,2,1,0:T(8,128)(2,1)}, bf16[96,1024]{1,0:T(8,128)(2,1)S(1)}, bf16[1024,256]{1,0:T(8,128)(2,1)S(1)}, bf16[32,1024]{1,0:T(8,128...) custom-call(bf16[1,1024,256]{2,1,0:T(8,128)(2,1)} %sup.3, bf16[1,1024,256]{2,1,0:T(8,128)(2,1)} %sdn.3, ...), custom_call_target="tpu_custom_call" | custom-call | flops 16777216 | bytes 1048576 | tf_op jit(solution)/shard_map/pallas_call | solution.py:57
  2.2 6.4 %all-to-all-start = ((bf16[8,2,32,256]{3,2,1,0:T(8,128)(2,1)}), bf16[8,2,32,256]{3,2,1,0:T(8,128)(2,1)S(1)}, u32[]{:S(2)}, u32[]{:S(2)}) async-start(bf16[8,2,32,256]{3,2,1,0:T(8,128)(2,1)} %get-tuple-element.27), calls=%async_computation | async-start | bytes 524288 | tf_op jit(solution)/shard_map/all_to_all | solution.py:506
  8.6 2.1 %collective-permute-start = (bf16[96,1024]{1,0:T(8,128)(2,1)S(1)}, bf16[96,1024]{1,0:T(8,128)(2,1)S(1)}, u32[]{:S(2)}, u32[]{:S(2)}) collective-permute-start(bf16[96,1024]{1,0:T(8,128)(2,1)S(1)} %get-tuple-element.31), channel_id=1, source_target_pairs={{8,16},{9,17},{10,18},{11,19},{12,20},{13,21},{14,22},{15,23},{16,... | collective-permute-start | bytes 589832 | tf_op jit(solution)/shard_map/ppermute | solution.py:509
  10.7 1.3 %collective-permute-start.1 = (bf16[32,1024]{1,0:T(8,128)(2,1)S(1)}, bf16[32,1024]{1,0:T(8,128)(2,1)S(1)}, u32[]{:S(2)}, u32[]{:S(2)}) collective-permute-start(bf16[32,1024]{1,0:T(8,128)(2,1)S(1)} %get-tuple-element.33.expn1), channel_id=1, source_target_pairs={{0,8},{8,0},{16,24},{24,16},{1,9},{9,1},{17,25},{25,17},{2,10},{10... | collective-permute-start | bytes 196616 | tf_op jit(solution)/shard_map/ppermute | solution.py:510
  12.0 2.2 %shard_map.87 = (bf16[256,256]{1,0:T(8,128)(2,1)S(1)}, bf16[256,256]{1,0:T(8,128)(2,1)S(1)}, bf16[256,256]{1,0:T(8,128)(2,1)S(1)}, bf16[256,256]{1,0:T(8,128)(2,1)S(1)}, bf16[2,1024,1024]{2,1,0:T(8,128)(2,1)S(1)}) custom-call(bf16[1,2,1024,1024]{3,2,1,0:T(8,128)(2,1)} %dup.7, bf16[1,2,1024,1024]{3,2,1,0:T(8,128)(2,1)} %ddn.7, ...), custom_call_target="tpu_custom_call" | custom-call | flops 1073741824 | bytes 4194304 | tf_op jit(solution)/shard_map/pallas_call | solution.py:57
  14.2 1.0 %collective-permute-start.3 = (bf16[256,256]{1,0:T(8,128)(2,1)S(1)}, bf16[256,256]{1,0:T(8,128)(2,1)S(1)}, u32[]{:S(2)}, u32[]{:S(2)}) collective-permute-start(bf16[256,256]{1,0:T(8,128)(2,1)S(1)} %get-tuple-element.35), channel_id=1, source_target_pairs={{0,8},{8,0},{16,24},{24,16},{1,9},{9,1},{17,25},{25,17},{2,10},{10... | collective-permute-start | bytes 393224 | tf_op jit(solution)/shard_map/ppermute | solution.py:520
  15.2 0.1 collective-permute-start.4
  15.3 0.4 %collective-permute-start.5 = (bf16[256,256]{1,0:T(8,128)(2,1)S(1)}, bf16[256,256]{1,0:T(8,128)(2,1)S(1)}, u32[]{:S(2)}, u32[]{:S(2)}) collective-permute-start(bf16[256,256]{1,0:T(8,128)(2,1)S(1)} %get-tuple-element.37), channel_id=1, source_target_pairs={{0,8},{8,0},{16,24},{24,16},{1,9},{9,1},{17,25},{25,17},{2,10},{10... | collective-permute-start | bytes 393224 | tf_op jit(solution)/shard_map/ppermute | solution.py:520
  15.7 0.0 collective-permute-done.1.before.refs_5_
  15.7 0.1 collective-permute-start.6
  15.8 0.0 collective-permute-done.packed
  15.8 1.1 %shard_map.88 = (bf16[96,1024]{1,0:T(8,128)(2,1)S(1)}, bf16[32,128]{1,0:T(8,128)(2,1)S(1)}) custom-call(bf16[2,1024,1024]{2,1,0:T(8,128)(2,1)S(1)} %get-tuple-element.30.block, bf16[96,1024]{1,0:T(8,128)(2,1)S(1)} %collective-permute-done.packed, bf16[32,1024]{1,0:T(8,128)(2,1)S(1)} %get-tuple-element.32.own, bf16[32,1024]{1,0:T(8,128)(2,1)S(1)} %get-tuple-element.33.expn1, ...), custom_call_target="tpu_custom_call" | custom-call | flops 1073741824 | bytes 4194304 | tf_op jit(solution)/shard_map/pallas_call | solution.py:57
  16.9 0.0 all-to-all-done.gathered
  17.0 1.8 %collective-permute-start.2 = (bf16[32,256]{1,0:T(8,128)(2,1)S(1)}, bf16[32,256]{1,0:T(8,128)(2,1)S(1)}, u32[]{:S(2)}, u32[]{:S(2)}) collective-permute-start(bf16[32,256]{1,0:T(8,128)(2,1)S(1)} %shard_map.89), channel_id=1, source_target_pairs={{0,8},{8,0},{16,24},{24,16},{1,9},{9,1},{17,25},{25,17},{2,10},{10... | collective-permute-start | bytes 49160 | tf_op jit(solution)/shard_map/ppermute | solution.py:533
  18.8 0.0 collective-permute-done.3.refs_0_
  18.8 0.0 collective-permute-done.4.refs_1_
  18.8 0.0 collective-permute-done.5.refs_2_
  18.8 0.0 collective-permute-done.6.refs_3_
  18.8 0.3 shard_map.90.sums
  19.1 0.5 %collective-permute-done.2.before.refs_4_ = bf16[32,256]{1,0:T(8,128)(2,1)S(1)} collective-permute-done((bf16[32,256]{1,0:T(8,128)(2,1)S(1)}, bf16[32,256]{1,0:T(8,128)(2,1)S(1)}, u32[]{:S(2)}, u32[]{:S(2)}) %collective-permute-start.2) | collective-permute-done | bytes 16416 | tf_op jit(solution)/shard_map/ppermute | solution.py:533
  19.6 0.9 %shard_map.91.payload = bf16[8,80,256]{2,1,0:T(8,128)(2,1)} custom-call(bf16[32,256]{1,0:T(8,128)(2,1)S(1)} %collective-permute-done.2.before.refs_4_, f32[64,256]{1,0:T(8,128)S(1)} %shard_map.90.sums, bf16[32,128]{1,0:T(8,128)(2,1)S(1)} %get-tuple-element.34.mixed, bf16[96,1024]{1,0:T(8,128)(2,1)S(1)} %collective-permute-done.packed), custom_call_target="tpu_custom_call" | custom-call | flops 16777216 | bytes 1048576 | tf_op jit(solution)/shard_map/pallas_call | solution.py:57
  20.5 3.5 %all-to-all-start.1 = ((bf16[8,80,256]{2,1,0:T(8,128)(2,1)}), bf16[8,80,256]{2,1,0:T(8,128)(2,1)S(1)}, u32[]{:S(2)}, u32[]{:S(2)}) async-start(bf16[8,80,256]{2,1,0:T(8,128)(2,1)} %shard_map.91.payload), calls=%async_computation.1 | async-start | bytes 655360 | tf_op jit(solution)/shard_map/all_to_all | solution.py:555
  24.1 3.2 %shard_map.93 = (bf16[1024,256]{1,0:T(8,128)(2,1)S(1)}, bf16[1024,256]{1,0:T(8,128)(2,1)S(1)}, bf16[1024,256]{1,0:T(8,128)(2,1)S(1)}) custom-call(bf16[1,1024,256]{2,1,0:T(8,128)(2,1)} %sup.3, bf16[1,1024,256]{2,1,0:T(8,128)(2,1)} %sdn.3, bf16[1,2,1024,1024]{3,2,1,0:T(8,128)(2,1)} %dup.7, bf16[1,2,1024,1024]{3,2,1,0:T(8,128)(2,1)} %ddn.7, ...), custom_call_target="tpu_custom_call" | custom-call | flops 1073741824 | bytes 4194304 | tf_op jit(solution)/shard_map/pallas_call | solution.py:57
  27.3 1.8 %collective-permute-start.7 = (bf16[1024,256]{1,0:T(8,128)(2,1)S(1)}, bf16[1024,256]{1,0:T(8,128)(2,1)S(1)}, u32[]{:S(2)}, u32[]{:S(2)}) collective-permute-start(bf16[1024,256]{1,0:T(8,128)(2,1)S(1)} %get-tuple-element.43), channel_id=1, source_target_pairs={{8,16},{9,17},{10,18},{11,19},{12,20},{13,21},{14,22},{15,23},{16,... | collective-permute-start | bytes 1572872 | tf_op jit(solution)/shard_map/ppermute | solution.py:565
  29.1 3.6 %all-to-all-done.1.second = bf16[8,80,256]{2,1,0:T(8,128)(2,1)S(1)} async-done(((bf16[8,80,256]{2,1,0:T(8,128)(2,1)}), bf16[8,80,256]{2,1,0:T(8,128)(2,1)S(1)}, u32[]{:S(2)}, u32[]{:S(2)}) %all-to-all-start.1) | async-done | bytes 327712 | tf_op jit(solution)/shard_map/all_to_all | solution.py:555
  32.6 0.6 %shard_map.92.coupled = bf16[64,256]{1,0:T(8,128)(2,1)S(1)} custom-call(bf16[8,2,32,256]{3,2,1,0:T(8,128)(2,1)S(1)} %all-to-all-done.gathered, bf16[8,80,256]{2,1,0:T(8,128)(2,1)S(1)} %all-to-all-done.1.second, bf16[96,1024]{1,0:T(8,128)(2,1)S(1)} %collective-permute-done.packed, bf16[2,32,256]{2,1,0:T(8,128)(2,1)S(1)} %get-tuple-element.28.couple1), custom_call_target="tpu_custom_call" | custom-call | flops 16777216 | bytes 1048576 | tf_op jit(solution)/shard_map/pallas_call | solution.py:57
  33.2 2.0 %collective-permute-start.8 = (bf16[64,256]{1,0:T(8,128)(2,1)S(1)}, bf16[64,256]{1,0:T(8,128)(2,1)S(1)}, u32[]{:S(2)}, u32[]{:S(2)}) collective-permute-start(bf16[64,256]{1,0:T(8,128)(2,1)S(1)} %shard_map.92.coupled), channel_id=1, source_target_pairs={{0,24},{8,16},{16,8},{24,0},{1,25},{9,17},{17,9},{25,1},{2,26},{10... | collective-permute-start | bytes 98312 | tf_op jit(solution)/shard_map/ppermute | solution.py:575
  35.2 1.8 %shard_map.94 = (bf16[1,1024,256]{2,1,0:T(8,128)(2,1)}, bf16[1,1024,256]{2,1,0:T(8,128)(2,1)}, bf16[2,512,1024]{2,1,0:T(8,128)(2,1)S(1)}, bf16[64,1024]{1,0:T(8,128)(2,1)S(1)}) custom-call(bf16[1,2,32,1024]{3,2,1,0:T(8,128)(2,1)} %expn.3, bf16[1,2,1024,1024]{3,2,1,0:T(8,128)(2,1)} %dup.7, bf16[1,2,1024,1024]{3,2,1,0:T(8,128)(2,1)} %ddn.7, ...), custom_call_target="tpu_custom_call" | custom-call | flops 1073741824 | bytes 4194304 | tf_op jit(solution)/shard_map/pallas_call | solution.py:57
  37.0 0.0 collective-permute-done.7.crossed
  37.1 0.0 collective-permute-done.8.coupled
  37.1 1.9 %shard_map.95 = (bf16[768,256]{1,0:T(8,128)(2,1)S(1)}, bf16[1024,256]{1,0:T(8,128)(2,1)S(1)}, bf16[1024,256]{1,0:T(8,128)(2,1)S(1)}, bf16[2,256,1024]{2,1,0:T(8,128)(2,1)S(1)}, bf16[256,256]{1,0:T(8,128)(2,1)S(1)}) custom-call(bf16[1,2,1024,1024]{3,2,1,0:T(8,128)(2,1)} %dup.7, bf16[1,2,1024,1024]{3,2,1,0:T(8,128)(2,1)} %ddn.7, ...), custom_call_target="tpu_custom_call" | custom-call | flops 1073741824 | bytes 4194304 | tf_op jit(solution)/shard_map/pallas_call | solution.py:57
  38.9 0.1 collective-permute-start.9
  39.0 0.5 %shard_map.96 = bf16[256,256]{1,0:T(8,128)(2,1)S(1)} custom-call(bf16[2,256,1024]{2,1,0:T(8,128)(2,1)S(1)} %get-tuple-element.48.rest, bf16[1024,256]{1,0:T(8,128)(2,1)S(1)} %get-tuple-element.49.trace.two, bf16[1024,256]{1,0:T(8,128)(2,1)S(1)} %get-tuple-element.50.turned, bf16[256,256]{1,0:T(8,128)(2,1)S(1)} %get-tuple-element.51.tail), custom_call_target="tpu_custom_call" | custom-call | flops 16777216 | bytes 1048576 | tf_op jit(solution)/shard_map/pallas_call | solution.py:57
  39.5 0.1 collective-permute-start.10
  39.6 1.3 %collective-permute-done.10.last = bf16[256,256]{1,0:T(8,128)(2,1)S(1)} collective-permute-done((bf16[256,256]{1,0:T(8,128)(2,1)S(1)}, bf16[256,256]{1,0:T(8,128)(2,1)S(1)}, u32[]{:S(2)}, u32[]{:S(2)}) %collective-permute-start.10) | collective-permute-done | bytes 131104 | tf_op jit(solution)/shard_map/ppermute | solution.py:601
  40.9 0.0 collective-permute-done.9.most
  40.9 0.8 %shard_map.97 = (bf16[1,1024,256]{2,1,0:T(8,128)(2,1)}, bf16[1,1024,256]{2,1,0:T(8,128)(2,1)}) custom-call(bf16[1,1024,256]{2,1,0:T(8,128)(2,1)} %get-tuple-element.41.before_up, bf16[1,1024,256]{2,1,0:T(8,128)(2,1)} %get-tuple-element.42.before_down, ...), custom_call_target="tpu_custom_call", output_to_operand_aliasing={{0}: (0, {}), {1}: (1, {})} | custom-call | flops 16777216 | bytes 1048576 | tf_op jit(solution)/shard_map/pallas_call | solution.py:57
  (1 shorter events, 0.0 us)
Async XLA Ops:
  2.2 14.7 %all-to-all-start = ((bf16[8,2,32,256]{3,2,1,0:T(8,128)(2,1)}), bf16[8,2,32,256]{3,2,1,0:T(8,128)(2,1)S(1)}, u32[]{:S(2)}, u32[]{:S(2)}) async-start(bf16[8,2,32,256]{3,2,1,0:T(8,128)(2,1)} %get-tuple-element.27), calls=%async_computation | async-start | bytes 524288 | tf_op jit(solution)/shard_map/all_to_all | solution.py:506
  8.6 7.2 %collective-permute-start = (bf16[96,1024]{1,0:T(8,128)(2,1)S(1)}, bf16[96,1024]{1,0:T(8,128)(2,1)S(1)}, u32[]{:S(2)}, u32[]{:S(2)}) collective-permute-start(bf16[96,1024]{1,0:T(8,128)(2,1)S(1)} %get-tuple-element.31), channel_id=1, source_target_pairs={{8,16},{9,17},{10,18},{11,19},{12,20},{13,21},{14,22},{15,23},{16,... | collective-permute-start | bytes 589832 | tf_op jit(solution)/shard_map/ppermute | solution.py:509
  10.7 5.0 %collective-permute-start.1 = (bf16[32,1024]{1,0:T(8,128)(2,1)S(1)}, bf16[32,1024]{1,0:T(8,128)(2,1)S(1)}, u32[]{:S(2)}, u32[]{:S(2)}) collective-permute-start(bf16[32,1024]{1,0:T(8,128)(2,1)S(1)} %get-tuple-element.33.expn1), channel_id=1, source_target_pairs={{0,8},{8,0},{16,24},{24,16},{1,9},{9,1},{17,25},{25,17},{2,10},{10... | collective-permute-start | bytes 196616 | tf_op jit(solution)/shard_map/ppermute | solution.py:510
  14.2 4.5 %collective-permute-start.3 = (bf16[256,256]{1,0:T(8,128)(2,1)S(1)}, bf16[256,256]{1,0:T(8,128)(2,1)S(1)}, u32[]{:S(2)}, u32[]{:S(2)}) collective-permute-start(bf16[256,256]{1,0:T(8,128)(2,1)S(1)} %get-tuple-element.35), channel_id=1, source_target_pairs={{0,8},{8,0},{16,24},{24,16},{1,9},{9,1},{17,25},{25,17},{2,10},{10... | collective-permute-start | bytes 393224 | tf_op jit(solution)/shard_map/ppermute | solution.py:520
  15.2 3.5 %collective-permute-start.4 = (bf16[256,256]{1,0:T(8,128)(2,1)S(1)}, bf16[256,256]{1,0:T(8,128)(2,1)S(1)}, u32[]{:S(2)}, u32[]{:S(2)}) collective-permute-start(bf16[256,256]{1,0:T(8,128)(2,1)S(1)} %get-tuple-element.36), channel_id=1, source_target_pairs={{0,8},{8,0},{16,24},{24,16},{1,9},{9,1},{17,25},{25,17},{2,10},{10... | collective-permute-start | bytes 393224 | tf_op jit(solution)/shard_map/ppermute | solution.py:520
  15.3 3.5 %collective-permute-start.5 = (bf16[256,256]{1,0:T(8,128)(2,1)S(1)}, bf16[256,256]{1,0:T(8,128)(2,1)S(1)}, u32[]{:S(2)}, u32[]{:S(2)}) collective-permute-start(bf16[256,256]{1,0:T(8,128)(2,1)S(1)} %get-tuple-element.37), channel_id=1, source_target_pairs={{0,8},{8,0},{16,24},{24,16},{1,9},{9,1},{17,25},{25,17},{2,10},{10... | collective-permute-start | bytes 393224 | tf_op jit(solution)/shard_map/ppermute | solution.py:520
  15.7 3.0 %collective-permute-start.6 = (bf16[256,256]{1,0:T(8,128)(2,1)S(1)}, bf16[256,256]{1,0:T(8,128)(2,1)S(1)}, u32[]{:S(2)}, u32[]{:S(2)}) collective-permute-start(bf16[256,256]{1,0:T(8,128)(2,1)S(1)} %get-tuple-element.38), channel_id=1, source_target_pairs={{0,8},{8,0},{16,24},{24,16},{1,9},{9,1},{17,25},{25,17},{2,10},{10... | collective-permute-start | bytes 393224 | tf_op jit(solution)/shard_map/ppermute | solution.py:520
  17.0 2.6 %collective-permute-start.2 = (bf16[32,256]{1,0:T(8,128)(2,1)S(1)}, bf16[32,256]{1,0:T(8,128)(2,1)S(1)}, u32[]{:S(2)}, u32[]{:S(2)}) collective-permute-start(bf16[32,256]{1,0:T(8,128)(2,1)S(1)} %shard_map.89), channel_id=1, source_target_pairs={{0,8},{8,0},{16,24},{24,16},{1,9},{9,1},{17,25},{25,17},{2,10},{10... | collective-permute-start | bytes 49160 | tf_op jit(solution)/shard_map/ppermute | solution.py:533
  20.5 12.1 %all-to-all-start.1 = ((bf16[8,80,256]{2,1,0:T(8,128)(2,1)}), bf16[8,80,256]{2,1,0:T(8,128)(2,1)S(1)}, u32[]{:S(2)}, u32[]{:S(2)}) async-start(bf16[8,80,256]{2,1,0:T(8,128)(2,1)} %shard_map.91.payload), calls=%async_computation.1 | async-start | bytes 655360 | tf_op jit(solution)/shard_map/all_to_all | solution.py:555
  27.3 9.8 %collective-permute-start.7 = (bf16[1024,256]{1,0:T(8,128)(2,1)S(1)}, bf16[1024,256]{1,0:T(8,128)(2,1)S(1)}, u32[]{:S(2)}, u32[]{:S(2)}) collective-permute-start(bf16[1024,256]{1,0:T(8,128)(2,1)S(1)} %get-tuple-element.43), channel_id=1, source_target_pairs={{8,16},{9,17},{10,18},{11,19},{12,20},{13,21},{14,22},{15,23},{16,... | collective-permute-start | bytes 1572872 | tf_op jit(solution)/shard_map/ppermute | solution.py:565
  33.2 3.8 %collective-permute-start.8 = (bf16[64,256]{1,0:T(8,128)(2,1)S(1)}, bf16[64,256]{1,0:T(8,128)(2,1)S(1)}, u32[]{:S(2)}, u32[]{:S(2)}) collective-permute-start(bf16[64,256]{1,0:T(8,128)(2,1)S(1)} %shard_map.92.coupled), channel_id=1, source_target_pairs={{0,24},{8,16},{16,8},{24,0},{1,25},{9,17},{17,9},{25,1},{2,26},{10... | collective-permute-start | bytes 98312 | tf_op jit(solution)/shard_map/ppermute | solution.py:575
  38.9 2.0 %collective-permute-start.9 = (bf16[768,256]{1,0:T(8,128)(2,1)S(1)}, bf16[768,256]{1,0:T(8,128)(2,1)S(1)}, u32[]{:S(2)}, u32[]{:S(2)}) collective-permute-start(bf16[768,256]{1,0:T(8,128)(2,1)S(1)} %get-tuple-element.47), channel_id=1, source_target_pairs={{0,8},{8,0},{16,24},{24,16},{1,9},{9,1},{17,25},{25,17},{2,10},{10... | collective-permute-start | bytes 1179656 | tf_op jit(solution)/shard_map/ppermute | solution.py:601
  39.5 1.4 %collective-permute-start.10 = (bf16[256,256]{1,0:T(8,128)(2,1)S(1)}, bf16[256,256]{1,0:T(8,128)(2,1)S(1)}, u32[]{:S(2)}, u32[]{:S(2)}) collective-permute-start(bf16[256,256]{1,0:T(8,128)(2,1)S(1)} %shard_map.96), channel_id=1, source_target_pairs={{0,8},{8,0},{16,24},{24,16},{1,9},{9,1},{17,25},{25,17},{2,10},{10... | collective-permute-start | bytes 393224 | tf_op jit(solution)/shard_map/ppermute | solution.py:601

commit v7 on v5

--- a/solution.py
+++ b/solution.py
@@ -258,7 +258,7 @@
         out[...] = (dot(couple1[0], coeffs) + dot(couple1[1], rotate(coeffs))).astype(BF16)
 
 
-def inner_gather_kernel(before, sums, mixed, packed, payload, small, sems):
+def inner_gather_kernel(before, sums, mixed, packed, payload, small, copies, sems):
     outer, _ = roles()
 
     @pl.when(jnp.logical_not(outer))
@@ -274,8 +274,8 @@
         small[2 * k :, :k] = mixed[:half, :k]
         small[2 * k :, k : 2 * k] = mixed[half:, :k]
         for o in range(payload.shape[0]):
-            start(small, payload.at[o], sems.at[0])
-        arrive(payload, sems.at[0])
+            copies[o] = small[...]
+        start(copies, payload, sems.at[0]).wait()
 
 
 def inner_apply_kernel(sup, sdn, dup, ddn, payload, *refs):
@@ -545,7 +545,7 @@
         (like(owners, 2 * k + k // 2, width),),
         (),
         (before, sums, mixed, packed),
-        [(2 * k + k // 2, width)],
+        [(2 * k + k // 2, width), (owners, 2 * k + k // 2, width)],
         1,
         **small,
     )

time: 42.1 us -> 42.2 us (level)
  no operation moved by 1% of the time
where the time goes in v7:
time: 42.2 us; the launch traced here: 41.6 us
  starting transfers between devices  20.7 us (49%)
  Pallas kernels  14.8 us (35%)
  waiting for transfers between devices  5.36 us (13%)
  between operations  0.77 us (2%)
    pallas_call x12, Pallas kernels, call(): pl.pallas_call(body, out_shape=tuple((pltpu.VMEM(*out) if keep else out f...  14.8 us
    all_to_all x1, starting transfers between devices, wave(): gathered = lax.all_to_all(payload, 'trace', 0, 0)  6.37 us
    all_to_all x1, starting transfers between devices, wave(): lax.all_to_all(payload, ('layer', 'trace'), 0, 0, axis_index_groups=groups)  3.55 us
    all_to_all x1, waiting for transfers between devices, wave(): lax.all_to_all(payload, ('layer', 'trace'), 0, 0, axis_index_groups=groups)  3.53 us
    ppermute x1, starting transfers between devices, wave(): packed = lax.ppermute(pack, ('layer', 'trace'), pairs)  2.08 us
    ppermute x1, starting transfers between devices, wave(): reached = lax.ppermute(coupled, 'layer', across)  2.03 us
    ppermute x1, starting transfers between devices, wave(): crossed = lax.ppermute(product, ('layer', 'trace'), pairs)  1.82 us
    ppermute x1, starting transfers between devices, wave(): before = lax.ppermute(before, 'layer', swap)  1.78 us
  transfers between devices with their start and end apart: 13, of which 3 were waited for; matrix products, arithmetic and copies ran while one was open for 0% of the time, Pallas kernels for 23%

profile of v7, /device:TPU:1, one launch (start us, length us, event | category | flops | bytes accessed | tf_op | source)
XLA Modules:
  0.0 41.6 jit_solution(9739938895384951027)
XLA Ops:
  0.6 1.6 %shard_map.86 = (bf16[8,2,32,256]{3,2,1,0:T(8,128)(2,1)}, bf16[96,1024]{1,0:T(8,128)(2,1)S(1)}, bf16[1024,256]{1,0:T(8,128)(2,1)S(1)}, bf16[32,1024]{1,0:T(8,128...) custom-call(bf16[1,1024,256]{2,1,0:T(8,128)(2,1)} %sup.3, bf16[1,1024,256]{2,1,0:T(8,128)(2,1)} %sdn.3, ...), custom_call_target="tpu_custom_call" | custom-call | flops 16777216 | bytes 1048576 | tf_op jit(solution)/shard_map/pallas_call | solution.py:57
  2.2 6.4 %all-to-all-start = ((bf16[8,2,32,256]{3,2,1,0:T(8,128)(2,1)}), bf16[8,2,32,256]{3,2,1,0:T(8,128)(2,1)S(1)}, u32[]{:S(2)}, u32[]{:S(2)}) async-start(bf16[8,2,32,256]{3,2,1,0:T(8,128)(2,1)} %get-tuple-element.27), calls=%async_computation | async-start | bytes 524288 | tf_op jit(solution)/shard_map/all_to_all | solution.py:506
  8.6 2.1 %collective-permute-start = (bf16[96,1024]{1,0:T(8,128)(2,1)S(1)}, bf16[96,1024]{1,0:T(8,128)(2,1)S(1)}, u32[]{:S(2)}, u32[]{:S(2)}) collective-permute-start(bf16[96,1024]{1,0:T(8,128)(2,1)S(1)} %get-tuple-element.31), channel_id=1, source_target_pairs={{8,16},{9,17},{10,18},{11,19},{12,20},{13,21},{14,22},{15,23},{16,... | collective-permute-start | bytes 589832 | tf_op jit(solution)/shard_map/ppermute | solution.py:509
  10.7 1.3 %collective-permute-start.1 = (bf16[32,1024]{1,0:T(8,128)(2,1)S(1)}, bf16[32,1024]{1,0:T(8,128)(2,1)S(1)}, u32[]{:S(2)}, u32[]{:S(2)}) collective-permute-start(bf16[32,1024]{1,0:T(8,128)(2,1)S(1)} %get-tuple-element.33.expn1), channel_id=1, source_target_pairs={{0,8},{8,0},{16,24},{24,16},{1,9},{9,1},{17,25},{25,17},{2,10},{10... | collective-permute-start | bytes 196616 | tf_op jit(solution)/shard_map/ppermute | solution.py:510
  12.0 2.2 %shard_map.87 = (bf16[256,256]{1,0:T(8,128)(2,1)S(1)}, bf16[256,256]{1,0:T(8,128)(2,1)S(1)}, bf16[256,256]{1,0:T(8,128)(2,1)S(1)}, bf16[256,256]{1,0:T(8,128)(2,1)S(1)}, bf16[2,1024,1024]{2,1,0:T(8,128)(2,1)S(1)}) custom-call(bf16[1,2,1024,1024]{3,2,1,0:T(8,128)(2,1)} %dup.7, bf16[1,2,1024,1024]{3,2,1,0:T(8,128)(2,1)} %ddn.7, ...), custom_call_target="tpu_custom_call" | custom-call | flops 1073741824 | bytes 4194304 | tf_op jit(solution)/shard_map/pallas_call | solution.py:57
  14.2 1.0 %collective-permute-start.3 = (bf16[256,256]{1,0:T(8,128)(2,1)S(1)}, bf16[256,256]{1,0:T(8,128)(2,1)S(1)}, u32[]{:S(2)}, u32[]{:S(2)}) collective-permute-start(bf16[256,256]{1,0:T(8,128)(2,1)S(1)} %get-tuple-element.35), channel_id=1, source_target_pairs={{0,8},{8,0},{16,24},{24,16},{1,9},{9,1},{17,25},{25,17},{2,10},{10... | collective-permute-start | bytes 393224 | tf_op jit(solution)/shard_map/ppermute | solution.py:520
  15.2 0.1 collective-permute-start.4
  15.3 0.4 %collective-permute-start.5 = (bf16[256,256]{1,0:T(8,128)(2,1)S(1)}, bf16[256,256]{1,0:T(8,128)(2,1)S(1)}, u32[]{:S(2)}, u32[]{:S(2)}) collective-permute-start(bf16[256,256]{1,0:T(8,128)(2,1)S(1)} %get-tuple-element.37), channel_id=1, source_target_pairs={{0,8},{8,0},{16,24},{24,16},{1,9},{9,1},{17,25},{25,17},{2,10},{10... | collective-permute-start | bytes 393224 | tf_op jit(solution)/shard_map/ppermute | solution.py:520
  15.7 0.0 collective-permute-done.1.before.refs_5_
  15.7 0.1 collective-permute-start.6
  15.8 0.0 collective-permute-done.packed
  15.8 1.1 %shard_map.88 = (bf16[96,1024]{1,0:T(8,128)(2,1)S(1)}, bf16[32,128]{1,0:T(8,128)(2,1)S(1)}) custom-call(bf16[2,1024,1024]{2,1,0:T(8,128)(2,1)S(1)} %get-tuple-element.30.block, bf16[96,1024]{1,0:T(8,128)(2,1)S(1)} %collective-permute-done.packed, bf16[32,1024]{1,0:T(8,128)(2,1)S(1)} %get-tuple-element.32.own, bf16[32,1024]{1,0:T(8,128)(2,1)S(1)} %get-tuple-element.33.expn1, ...), custom_call_target="tpu_custom_call" | custom-call | flops 1073741824 | bytes 4194304 | tf_op jit(solution)/shard_map/pallas_call | solution.py:57
  16.9 0.0 all-to-all-done.gathered
  17.0 1.8 %collective-permute-start.2 = (bf16[32,256]{1,0:T(8,128)(2,1)S(1)}, bf16[32,256]{1,0:T(8,128)(2,1)S(1)}, u32[]{:S(2)}, u32[]{:S(2)}) collective-permute-start(bf16[32,256]{1,0:T(8,128)(2,1)S(1)} %shard_map.89), channel_id=1, source_target_pairs={{0,8},{8,0},{16,24},{24,16},{1,9},{9,1},{17,25},{25,17},{2,10},{10... | collective-permute-start | bytes 49160 | tf_op jit(solution)/shard_map/ppermute | solution.py:533
  18.8 0.0 collective-permute-done.3.refs_0_
  18.8 0.0 collective-permute-done.4.refs_1_
  18.8 0.0 collective-permute-done.5.refs_2_
  18.8 0.0 collective-permute-done.6.refs_3_
  18.8 0.3 shard_map.90.sums
  19.1 0.5 %collective-permute-done.2.before.refs_4_ = bf16[32,256]{1,0:T(8,128)(2,1)S(1)} collective-permute-done((bf16[32,256]{1,0:T(8,128)(2,1)S(1)}, bf16[32,256]{1,0:T(8,128)(2,1)S(1)}, u32[]{:S(2)}, u32[]{:S(2)}) %collective-permute-start.2) | collective-permute-done | bytes 16416 | tf_op jit(solution)/shard_map/ppermute | solution.py:533
  19.6 0.9 %shard_map.91.payload = bf16[8,80,256]{2,1,0:T(8,128)(2,1)} custom-call(bf16[32,256]{1,0:T(8,128)(2,1)S(1)} %collective-permute-done.2.before.refs_4_, f32[64,256]{1,0:T(8,128)S(1)} %shard_map.90.sums, bf16[32,128]{1,0:T(8,128)(2,1)S(1)} %get-tuple-element.34.mixed, bf16[96,1024]{1,0:T(8,128)(2,1)S(1)} %collective-permute-done.packed), custom_call_target="tpu_custom_call" | custom-call | flops 16777216 | bytes 1048576 | tf_op jit(solution)/shard_map/pallas_call | solution.py:57
  20.5 3.5 %all-to-all-start.1 = ((bf16[8,80,256]{2,1,0:T(8,128)(2,1)}), bf16[8,80,256]{2,1,0:T(8,128)(2,1)S(1)}, u32[]{:S(2)}, u32[]{:S(2)}) async-start(bf16[8,80,256]{2,1,0:T(8,128)(2,1)} %shard_map.91.payload), calls=%async_computation.1 | async-start | bytes 655360 | tf_op jit(solution)/shard_map/all_to_all | solution.py:555
  24.1 3.2 %shard_map.92 = (bf16[1024,256]{1,0:T(8,128)(2,1)S(1)}, bf16[1024,256]{1,0:T(8,128)(2,1)S(1)}, bf16[1024,256]{1,0:T(8,128)(2,1)S(1)}) custom-call(bf16[1,1024,256]{2,1,0:T(8,128)(2,1)} %sup.3, bf16[1,1024,256]{2,1,0:T(8,128)(2,1)} %sdn.3, bf16[1,2,1024,1024]{3,2,1,0:T(8,128)(2,1)} %dup.7, bf16[1,2,1024,1024]{3,2,1,0:T(8,128)(2,1)} %ddn.7, ...), custom_call_target="tpu_custom_call" | custom-call | flops 1073741824 | bytes 4194304 | tf_op jit(solution)/shard_map/pallas_call | solution.py:57
  27.3 1.8 %collective-permute-start.7 = (bf16[1024,256]{1,0:T(8,128)(2,1)S(1)}, bf16[1024,256]{1,0:T(8,128)(2,1)S(1)}, u32[]{:S(2)}, u32[]{:S(2)}) collective-permute-start(bf16[1024,256]{1,0:T(8,128)(2,1)S(1)} %get-tuple-element.40), channel_id=1, source_target_pairs={{8,16},{9,17},{10,18},{11,19},{12,20},{13,21},{14,22},{15,23},{16,... | collective-permute-start | bytes 1572872 | tf_op jit(solution)/shard_map/ppermute | solution.py:565
  29.1 3.5 %all-to-all-done.1.second = bf16[8,80,256]{2,1,0:T(8,128)(2,1)S(1)} async-done(((bf16[8,80,256]{2,1,0:T(8,128)(2,1)}), bf16[8,80,256]{2,1,0:T(8,128)(2,1)S(1)}, u32[]{:S(2)}, u32[]{:S(2)}) %all-to-all-start.1) | async-done | bytes 327712 | tf_op jit(solution)/shard_map/all_to_all | solution.py:555
  32.6 0.6 %shard_map.93.coupled = bf16[64,256]{1,0:T(8,128)(2,1)S(1)} custom-call(bf16[8,2,32,256]{3,2,1,0:T(8,128)(2,1)S(1)} %all-to-all-done.gathered, bf16[8,80,256]{2,1,0:T(8,128)(2,1)S(1)} %all-to-all-done.1.second, bf16[96,1024]{1,0:T(8,128)(2,1)S(1)} %collective-permute-done.packed, bf16[2,32,256]{2,1,0:T(8,128)(2,1)S(1)} %get-tuple-element.28.couple1), custom_call_target="tpu_custom_call" | custom-call | flops 16777216 | bytes 1048576 | tf_op jit(solution)/shard_map/pallas_call | solution.py:57
  33.2 2.0 %collective-permute-start.8 = (bf16[64,256]{1,0:T(8,128)(2,1)S(1)}, bf16[64,256]{1,0:T(8,128)(2,1)S(1)}, u32[]{:S(2)}, u32[]{:S(2)}) collective-permute-start(bf16[64,256]{1,0:T(8,128)(2,1)S(1)} %shard_map.93.coupled), channel_id=1, source_target_pairs={{0,24},{8,16},{16,8},{24,0},{1,25},{9,17},{17,9},{25,1},{2,26},{10... | collective-permute-start | bytes 98312 | tf_op jit(solution)/shard_map/ppermute | solution.py:575
  35.2 1.6 %shard_map.94 = (bf16[2,512,1024]{2,1,0:T(8,128)(2,1)S(1)}, bf16[64,1024]{1,0:T(8,128)(2,1)S(1)}) custom-call(bf16[1,2,32,1024]{3,2,1,0:T(8,128)(2,1)} %expn.3, bf16[1,2,1024,1024]{3,2,1,0:T(8,128)(2,1)} %dup.7, bf16[1,2,1024,1024]{3,2,1,0:T(8,128)(2,1)} %ddn.7, bf16[64,256]{1,0:T(8,128)(2,1)S(1)} %shard_map.93.coupled, ...), custom_call_target="tpu_custom_call" | custom-call | flops 1073741824 | bytes 4194304 | tf_op jit(solution)/shard_map/pallas_call | solution.py:57
  36.9 0.0 collective-permute-done.7.crossed
  36.9 0.0 collective-permute-done.8.coupled
  36.9 1.9 %shard_map.95 = (bf16[1,1024,256]{2,1,0:T(8,128)(2,1)}, bf16[1,1024,256]{2,1,0:T(8,128)(2,1)}, bf16[768,256]{1,0:T(8,128)(2,1)S(1)}, bf16[1024,256]{1,0:T(8,128)...) custom-call(bf16[1,2,1024,1024]{3,2,1,0:T(8,128)(2,1)} %dup.7, ...), custom_call_target="tpu_custom_call" | custom-call | flops 1073741824 | bytes 4194304 | tf_op jit(solution)/shard_map/pallas_call | solution.py:57
  38.8 0.1 collective-permute-start.9
  38.9 0.5 %shard_map.96 = bf16[256,256]{1,0:T(8,128)(2,1)S(1)} custom-call(bf16[2,256,1024]{2,1,0:T(8,128)(2,1)S(1)} %get-tuple-element.48.rest, bf16[1024,256]{1,0:T(8,128)(2,1)S(1)} %get-tuple-element.49.trace.two, bf16[1024,256]{1,0:T(8,128)(2,1)S(1)} %get-tuple-element.50.turned, bf16[256,256]{1,0:T(8,128)(2,1)S(1)} %get-tuple-element.51.tail), custom_call_target="tpu_custom_call" | custom-call | flops 16777216 | bytes 1048576 | tf_op jit(solution)/shard_map/pallas_call | solution.py:57
  39.4 0.1 collective-permute-start.10
  39.5 1.3 %collective-permute-done.10.last = bf16[256,256]{1,0:T(8,128)(2,1)S(1)} collective-permute-done((bf16[256,256]{1,0:T(8,128)(2,1)S(1)}, bf16[256,256]{1,0:T(8,128)(2,1)S(1)}, u32[]{:S(2)}, u32[]{:S(2)}) %collective-permute-start.10) | collective-permute-done | bytes 131104 | tf_op jit(solution)/shard_map/ppermute | solution.py:602
  40.8 0.0 collective-permute-done.9.most
  40.8 0.8 %shard_map.97 = (bf16[1,1024,256]{2,1,0:T(8,128)(2,1)}, bf16[1,1024,256]{2,1,0:T(8,128)(2,1)}) custom-call(bf16[1,1024,256]{2,1,0:T(8,128)(2,1)} %get-tuple-element.45.before_up, bf16[1,1024,256]{2,1,0:T(8,128)(2,1)} %get-tuple-element.46.before_down, ...), custom_call_target="tpu_custom_call", output_to_operand_aliasing={{0}: (0, {}), {1}: (1, {})} | custom-call | flops 16777216 | bytes 1048576 | tf_op jit(solution)/shard_map/pallas_call | solution.py:57
  (1 shorter events, 0.0 us)
Async XLA Ops:
  2.2 14.7 %all-to-all-start = ((bf16[8,2,32,256]{3,2,1,0:T(8,128)(2,1)}), bf16[8,2,32,256]{3,2,1,0:T(8,128)(2,1)S(1)}, u32[]{:S(2)}, u32[]{:S(2)}) async-start(bf16[8,2,32,256]{3,2,1,0:T(8,128)(2,1)} %get-tuple-element.27), calls=%async_computation | async-start | bytes 524288 | tf_op jit(solution)/shard_map/all_to_all | solution.py:506
  8.6 7.2 %collective-permute-start = (bf16[96,1024]{1,0:T(8,128)(2,1)S(1)}, bf16[96,1024]{1,0:T(8,128)(2,1)S(1)}, u32[]{:S(2)}, u32[]{:S(2)}) collective-permute-start(bf16[96,1024]{1,0:T(8,128)(2,1)S(1)} %get-tuple-element.31), channel_id=1, source_target_pairs={{8,16},{9,17},{10,18},{11,19},{12,20},{13,21},{14,22},{15,23},{16,... | collective-permute-start | bytes 589832 | tf_op jit(solution)/shard_map/ppermute | solution.py:509
  10.7 5.0 %collective-permute-start.1 = (bf16[32,1024]{1,0:T(8,128)(2,1)S(1)}, bf16[32,1024]{1,0:T(8,128)(2,1)S(1)}, u32[]{:S(2)}, u32[]{:S(2)}) collective-permute-start(bf16[32,1024]{1,0:T(8,128)(2,1)S(1)} %get-tuple-element.33.expn1), channel_id=1, source_target_pairs={{0,8},{8,0},{16,24},{24,16},{1,9},{9,1},{17,25},{25,17},{2,10},{10... | collective-permute-start | bytes 196616 | tf_op jit(solution)/shard_map/ppermute | solution.py:510
  14.2 4.5 %collective-permute-start.3 = (bf16[256,256]{1,0:T(8,128)(2,1)S(1)}, bf16[256,256]{1,0:T(8,128)(2,1)S(1)}, u32[]{:S(2)}, u32[]{:S(2)}) collective-permute-start(bf16[256,256]{1,0:T(8,128)(2,1)S(1)} %get-tuple-element.35), channel_id=1, source_target_pairs={{0,8},{8,0},{16,24},{24,16},{1,9},{9,1},{17,25},{25,17},{2,10},{10... | collective-permute-start | bytes 393224 | tf_op jit(solution)/shard_map/ppermute | solution.py:520
  15.2 3.5 %collective-permute-start.4 = (bf16[256,256]{1,0:T(8,128)(2,1)S(1)}, bf16[256,256]{1,0:T(8,128)(2,1)S(1)}, u32[]{:S(2)}, u32[]{:S(2)}) collective-permute-start(bf16[256,256]{1,0:T(8,128)(2,1)S(1)} %get-tuple-element.36), channel_id=1, source_target_pairs={{0,8},{8,0},{16,24},{24,16},{1,9},{9,1},{17,25},{25,17},{2,10},{10... | collective-permute-start | bytes 393224 | tf_op jit(solution)/shard_map/ppermute | solution.py:520
  15.3 3.5 %collective-permute-start.5 = (bf16[256,256]{1,0:T(8,128)(2,1)S(1)}, bf16[256,256]{1,0:T(8,128)(2,1)S(1)}, u32[]{:S(2)}, u32[]{:S(2)}) collective-permute-start(bf16[256,256]{1,0:T(8,128)(2,1)S(1)} %get-tuple-element.37), channel_id=1, source_target_pairs={{0,8},{8,0},{16,24},{24,16},{1,9},{9,1},{17,25},{25,17},{2,10},{10... | collective-permute-start | bytes 393224 | tf_op jit(solution)/shard_map/ppermute | solution.py:520
  15.7 3.0 %collective-permute-start.6 = (bf16[256,256]{1,0:T(8,128)(2,1)S(1)}, bf16[256,256]{1,0:T(8,128)(2,1)S(1)}, u32[]{:S(2)}, u32[]{:S(2)}) collective-permute-start(bf16[256,256]{1,0:T(8,128)(2,1)S(1)} %get-tuple-element.38), channel_id=1, source_target_pairs={{0,8},{8,0},{16,24},{24,16},{1,9},{9,1},{17,25},{25,17},{2,10},{10... | collective-permute-start | bytes 393224 | tf_op jit(solution)/shard_map/ppermute | solution.py:520
  17.0 2.6 %collective-permute-start.2 = (bf16[32,256]{1,0:T(8,128)(2,1)S(1)}, bf16[32,256]{1,0:T(8,128)(2,1)S(1)}, u32[]{:S(2)}, u32[]{:S(2)}) collective-permute-start(bf16[32,256]{1,0:T(8,128)(2,1)S(1)} %shard_map.89), channel_id=1, source_target_pairs={{0,8},{8,0},{16,24},{24,16},{1,9},{9,1},{17,25},{25,17},{2,10},{10... | collective-permute-start | bytes 49160 | tf_op jit(solution)/shard_map/ppermute | solution.py:533
  20.5 12.1 %all-to-all-start.1 = ((bf16[8,80,256]{2,1,0:T(8,128)(2,1)}), bf16[8,80,256]{2,1,0:T(8,128)(2,1)S(1)}, u32[]{:S(2)}, u32[]{:S(2)}) async-start(bf16[8,80,256]{2,1,0:T(8,128)(2,1)} %shard_map.91.payload), calls=%async_computation.1 | async-start | bytes 655360 | tf_op jit(solution)/shard_map/all_to_all | solution.py:555
  27.3 9.6 %collective-permute-start.7 = (bf16[1024,256]{1,0:T(8,128)(2,1)S(1)}, bf16[1024,256]{1,0:T(8,128)(2,1)S(1)}, u32[]{:S(2)}, u32[]{:S(2)}) collective-permute-start(bf16[1024,256]{1,0:T(8,128)(2,1)S(1)} %get-tuple-element.40), channel_id=1, source_target_pairs={{8,16},{9,17},{10,18},{11,19},{12,20},{13,21},{14,22},{15,23},{16,... | collective-permute-start | bytes 1572872 | tf_op jit(solution)/shard_map/ppermute | solution.py:565
  33.2 3.7 %collective-permute-start.8 = (bf16[64,256]{1,0:T(8,128)(2,1)S(1)}, bf16[64,256]{1,0:T(8,128)(2,1)S(1)}, u32[]{:S(2)}, u32[]{:S(2)}) collective-permute-start(bf16[64,256]{1,0:T(8,128)(2,1)S(1)} %shard_map.93.coupled), channel_id=1, source_target_pairs={{0,24},{8,16},{16,8},{24,0},{1,25},{9,17},{17,9},{25,1},{2,26},{10... | collective-permute-start | bytes 98312 | tf_op jit(solution)/shard_map/ppermute | solution.py:575
  38.8 2.0 %collective-permute-start.9 = (bf16[768,256]{1,0:T(8,128)(2,1)S(1)}, bf16[768,256]{1,0:T(8,128)(2,1)S(1)}, u32[]{:S(2)}, u32[]{:S(2)}) collective-permute-start(bf16[768,256]{1,0:T(8,128)(2,1)S(1)} %get-tuple-element.47), channel_id=1, source_target_pairs={{0,8},{8,0},{16,24},{24,16},{1,9},{9,1},{17,25},{25,17},{2,10},{10... | collective-permute-start | bytes 1179656 | tf_op jit(solution)/shard_map/ppermute | solution.py:602
  39.4 1.4 %collective-permute-start.10 = (bf16[256,256]{1,0:T(8,128)(2,1)S(1)}, bf16[256,256]{1,0:T(8,128)(2,1)S(1)}, u32[]{:S(2)}, u32[]{:S(2)}) collective-permute-start(bf16[256,256]{1,0:T(8,128)(2,1)S(1)} %shard_map.96), channel_id=1, source_target_pairs={{0,8},{8,0},{16,24},{24,16},{1,9},{9,1},{17,25},{25,17},{2,10},{10... | collective-permute-start | bytes 393224 | tf_op jit(solution)/shard_map/ppermute | solution.py:602
